TPU v7x, 128 devices: a whole 4x4x4 slice. The times are simulated.
128 devices in a mesh: src: 32 (over y, z, core), tgt: 4 (over x).
Axes of the slice: x: 4, y: 4, z: 4, core: 2. Of those that a mesh axis runs over, the one named last changes fastest.
Arguments:
- src_points: float32 [32, 16384], P(None, 'src'), may hold values from -10 to 10
- tgt_points: float32 [32, 65536], P(None, 'tgt'), may hold values from -10 to 10
Outputs:
- source_dual: float32 [16384], P('src')
- target_dual: float32 [65536], P('tgt')
- mapped_targets: float32 [32, 65536], P(None, 'tgt')
All inputs are finite; a program needn't handle non-finite values.
Results may differ from a plain program's by a relative error of at most 0.0003.
Values sent between devices are 32-bit elements; how exact they have to be, the bound alone decides.
No kernel may reach another device: no remote copies, remote signals or barrier semaphores. Data moves between devices by JAX's collectives and lax.ppermute only.
A program may use at most 192 MiB of HBM per device.

v0:
```python
import math

import jax
import jax.numpy as jnp
from jax import lax
from jax.sharding import PartitionSpec as P

EPSILON = 0.5


def body(src_points, tgt_points):
    dims = src_points.shape[0]
    rows = src_points.shape[1]
    columns = tgt_points.shape[1]
    width_block = min(2048, columns)
    block_count = columns // width_block
    log_src = -math.log(rows * lax.axis_size("src"))
    log_tgt = -math.log(columns * lax.axis_size("tgt"))
    src_sq = jnp.sum(src_points * src_points, axis=0)
    tgt_blocks = tgt_points.reshape(dims, block_count, width_block).transpose(1, 0, 2)
    tgt_sq = jnp.sum(tgt_blocks * tgt_blocks, axis=1)

    def cost_tile(tgt_block, block_sq):
        cross = lax.dot_general(
            src_points,
            tgt_block,
            (((0,), (0,)), ((), ())),
            precision=lax.Precision.HIGHEST,
            preferred_element_type=jnp.float32,
        )
        return src_sq[:, None] + block_sq[None, :] - 2.0 * cross

    def row_dual(dual_tgt):

        def row_visit(carry, items):
            tgt_block, block_sq, dual_block = items
            scores = (dual_block[None, :] - cost_tile(tgt_block, block_sq)) / EPSILON + log_tgt
            peak = jnp.max(scores, axis=1)
            newest = jnp.maximum(carry[0], peak)
            total = carry[1] * jnp.exp(carry[0] - newest) + jnp.sum(
                jnp.exp(scores - newest[:, None]), axis=1
            )
            return ((newest, total), None)

        start = (jnp.full((rows,), -jnp.inf, jnp.float32), jnp.zeros((rows,), jnp.float32))
        (peak, total), _ = lax.scan(row_visit, start, (tgt_blocks, tgt_sq, dual_tgt))
        summit = lax.pmax(peak, "tgt")
        whole = lax.psum(total * jnp.exp(peak - summit), "tgt")
        return -EPSILON * (summit + jnp.log(whole))

    def col_partials(dual_src):

        def col_visit(items):
            tgt_block, block_sq = items
            scores = (dual_src[:, None] - cost_tile(tgt_block, block_sq)) / EPSILON + log_src
            peak = jnp.max(scores, axis=0)
            weights = jnp.exp(scores - peak[None, :])
            total = jnp.sum(weights, axis=0)
            return (peak, total)

        return lax.map(col_visit, (tgt_blocks, tgt_sq))

    def col_dual(dual_src):
        peaks, totals = col_partials(dual_src)
        summit = lax.pmax(peaks, "src")
        whole = lax.psum(totals * jnp.exp(peaks - summit), "src")
        return -EPSILON * (summit + jnp.log(whole))

    dual_tgt = jnp.zeros((block_count, width_block), jnp.float32)
    dual_src = row_dual(dual_tgt)
    dual_tgt = col_dual(dual_src)
    dual_src = row_dual(dual_tgt)
    dual_tgt = col_dual(dual_src)

    def weigh(items):
        tgt_block, block_sq, dual_block = items
        weights = jnp.exp(
            (dual_src[:, None] + dual_block[None, :] - cost_tile(tgt_block, block_sq)) / EPSILON
            + log_src
        )
        return jnp.dot(
            src_points, weights, precision=lax.Precision.HIGHEST, preferred_element_type=jnp.float32
        )

    moments = lax.map(weigh, (tgt_blocks, tgt_sq, dual_tgt))
    moments = lax.psum(moments, "src")
    mapped = moments.transpose(1, 0, 2).reshape(dims, columns)
    return (dual_src, dual_tgt.reshape(columns), mapped)


def solution(mesh):
    placed = (P(None, "src"), P(None, "tgt"))
    return jax.shard_map(
        body,
        mesh=mesh,
        in_specs=placed,
        out_specs=(P("src"), P("tgt"), P(None, "tgt")),
        check_vma=False,
    )
```

profile of v0, /device:TPU:1, one launch (start us, length us, event | category | flops | bytes accessed | tf_op | source)
XLA Modules:
  0.0 847.7 jit_solution(729219108184565988)
XLA Ops:
  11.5 69.6 %while.63 = (s32[]{:T(128)}, f32[512]{0:T(512)S(1)}, f32[512]{0:T(512)S(1)}, f32[512]{0:T(512)S(1)}, f32[8,2048]{1,0:T(8,128)S(1)}, /*index=5*/f32[8,32,2048]{2,...) while((s32[]{:T(128)}, f32[512]{0:T(512)S(1)}, f32[512]{0:T(512)S(1)}, f32[512]{0:T(512)S(1)}, ...), condition=%wide.region_5.6_spmd.clone, body=%wide.region_2.5_spmd.clone.sunk | while | flops 412092928 | bytes 8769648 | solution.py:46
  11.5 5.8 fusion.91
  20.2 5.8 fusion.91
  28.9 5.8 fusion.91
  37.6 5.8 fusion.91
  46.3 5.8 fusion.91
  55.0 5.8 fusion.91
  63.7 5.8 fusion.91
  72.4 5.8 fusion.91
  81.0 9.3 %pmax.28 = f32[512]{0:T(512)S(1)} all-reduce(f32[512]{0:T(512)S(1)} %get-tuple-element.212), channel_id=1, replica_groups=mesh['src'=32,'tgt'=4] {'tgt'}, use_global_device_ids=true, to_apply=%region_6.7 | all-reduce | flops 512 | bytes 4096 | tf_op jit(solution)/shard_map/pmax | solution.py:47
  90.4 6.0 psum.35
  96.4 43.3 %while.60 = (s32[]{:T(128)}, f32[8,2048]{1,0:T(8,128)S(1)}, f32[8,2048]{1,0:T(8,128)S(1)}, f32[512]{0:T(512)S(1)}, f32[512]{0:T(512)S(1)}, /*index=5*/f32[8,2048...) while((s32[]{:T(128)}, f32[8,2048]{1,0:T(8,128)S(1)}, ...), condition=%wide.region_11.12_spmd, body=%wide.region_8.11_spmd.sunk | while | flops 412086272 | bytes 8802421 | solution.py:61
  96.4 4.3 fusion.81
  101.8 4.3 fusion.81
  107.3 4.3 fusion.81
  112.7 4.3 fusion.81
  118.1 4.3 fusion.81
  128.9 4.3 fusion.81
  140.4 101.0 %all-reduce.6.cloned.1.call-done = f32[8,2048]{1,0:T(8,128)} async-done(((f32[8,2048]{1,0:T(8,128)}), f32[8,2048]{1,0:T(8,128)}) %all-reduce.6.cloned.1.call-update) | async-done | bytes 65552 | tf_op jit(solution)/shard_map/pmax | solution.py:65
  243.2 96.2 %all-reduce.8.cloned.1.call-done = f32[8,2048]{1,0:T(8,128)} async-done(((f32[8,2048]{1,0:T(8,128)}), f32[8,2048]{1,0:T(8,128)}) %all-reduce.8.cloned.1.call-update) | async-done | bytes 65552 | tf_op jit(solution)/shard_map/psum | solution.py:66
  340.3 69.7 %while.64 = (s32[]{:T(128)}, f32[512]{0:T(512)S(1)}, f32[512]{0:T(512)S(1)}, f32[8,2048]{1,0:T(8,128)S(1)}, f32[512]{0:T(512)S(1)}, /*index=5*/f32[8,2048]{1,0:T...) while((s32[]{:T(128)}, f32[512]{0:T(512)S(1)}, ...), condition=%wide.region_17.18_spmd.clone, body=%wide.region_14.17_spmd.clone.sunk | while | flops 412092928 | bytes 8794232 | solution.py:46
  340.3 5.8 fusion.94
  349.1 5.8 fusion.94
  357.8 5.8 fusion.94
  366.5 5.8 fusion.94
  375.2 5.8 fusion.94
  383.9 5.8 fusion.94
  392.6 5.8 fusion.94
  401.4 5.8 fusion.94
  410.0 8.5 pmax.30
  418.5 6.0 psum.37
  424.5 43.3 %while.61 = (s32[]{:T(128)}, f32[8,2048]{1,0:T(8,128)S(1)}, f32[8,2048]{1,0:T(8,128)S(1)}, f32[512]{0:T(512)S(1)}, f32[512]{0:T(512)S(1)}, /*index=5*/f32[8,2048...) while((s32[]{:T(128)}, f32[8,2048]{1,0:T(8,128)S(1)}, ...), condition=%wide.region_23.24_spmd, body=%wide.region_20.23_spmd.sunk | while | flops 412086272 | bytes 8802421 | solution.py:61
  424.6 4.3 fusion.83
  435.4 4.3 fusion.83
  446.2 4.3 fusion.83
  457.0 4.3 fusion.83
  468.6 97.1 %all-reduce.10.cloned.1.call-done = f32[8,2048]{1,0:T(8,128)} async-done(((f32[8,2048]{1,0:T(8,128)}), f32[8,2048]{1,0:T(8,128)}) %all-reduce.10.cloned.1.call-update) | async-done | bytes 65552 | tf_op jit(solution)/shard_map/pmax | solution.py:65
  567.5 96.4 %all-reduce.12.cloned.1.call-done = f32[8,2048]{1,0:T(8,128)} async-done(((f32[8,2048]{1,0:T(8,128)}), f32[8,2048]{1,0:T(8,128)}) %all-reduce.12.cloned.1.call-update) | async-done | bytes 65552 | tf_op jit(solution)/shard_map/psum | solution.py:66
  664.7 64.1 %while.62 = (s32[]{:T(128)}, f32[8,32,2048]{2,1,0:T(8,128)}, f32[512]{0:T(512)S(1)}, f32[8,2048]{1,0:T(8,128)S(1)}, f32[512]{0:T(512)S(1)}, /*index=5*/f32[8,204...) while((s32[]{:T(128)}, f32[8,32,2048]{2,1,0:T(8,128)}, f32[512]{0:T(512)S(1)}, ...), condition=%wide.region_27.28_spmd, body=%wide.region_26.27_spmd.sunk | while | flops 812646400 | bytes 9097829 | solution.py:85
  668.2 4.5 fusion.89
  676.2 4.5 fusion.89
  684.2 4.5 fusion.89
  692.3 4.5 fusion.89
  700.3 4.5 fusion.89
  708.3 4.5 fusion.89
  716.3 4.5 fusion.89
  724.3 4.5 fusion.89
  732.6 105.6 %all-reduce.14.cloned.1.call-done = f32[32,16384]{1,0:T(8,128)} async-done(((f32[32,16384]{1,0:T(8,128)}), f32[32,16384]{1,0:T(8,128)}) %all-reduce.14.cloned.1.call-update) | async-done | bytes 2097168 | tf_op jit(solution)/shard_map/psum | solution.py:86
  (208 shorter events, 134.4 us)
Async XLA Ops:
  7.2 234.3 %all-reduce.6.cloned.1.call-start = ((), (), s32[]{:S(2)}) async-start(), calls=%async_computation | async-start | bytes 131072 | tf_op jit(solution)/shard_map/pmax | solution.py:65
  10.0 1.4 copy-start
  139.7 0.6 copy-start.2
  140.4 199.0 %all-reduce.8.cloned.1.call-start = ((), (), s32[]{:S(2)}) async-start(), calls=%async_computation.1 | async-start | bytes 131072 | tf_op jit(solution)/shard_map/psum | solution.py:66
  243.0 322.6 %all-reduce.10.cloned.1.call-start = ((), (), s32[]{:S(2)}) async-start(), calls=%async_computation.2 | async-start | bytes 131072 | tf_op jit(solution)/shard_map/pmax | solution.py:65
  467.8 0.6 copy-start.1
  468.5 195.3 %all-reduce.12.cloned.1.call-start = ((), (), s32[]{:S(2)}) async-start(), calls=%async_computation.3 | async-start | bytes 131072 | tf_op jit(solution)/shard_map/psum | solution.py:66
  567.2 270.9 %all-reduce.14.cloned.1.call-start = ((), (), s32[]{:S(2)}) async-start(), calls=%async_computation.4 | async-start | bytes 4194304 | tf_op jit(solution)/shard_map/psum | solution.py:86
  728.8 112.4 %copy-start.3 = (f32[512]{0:T(512)}, f32[512]{0:T(512)S(1)}, u32[]{:S(2)}) copy-start(f32[512]{0:T(512)S(1)} %get-tuple-element.849) | copy-start | bytes 6148
Sparse Core Ops, SparseCore 0:
  140.5 100.9 all-reduce.5
  245.3 94.0 all-reduce.7
  468.6 96.9 all-reduce.9
  569.7 94.0 all-reduce.11
  732.0 106.0 all-reduce.13
where the time goes:
time: 849 us; the launch traced here: 848 us
  waiting for transfers between devices  496 us (58%)
  matrix products  226 us (27%)
  other arithmetic  60.8 us (7%)
  blocking collectives  29.7 us (3%)
  local copies, waits for them, and re-layouts  19.1 us (2%)
  between operations  13.9 us (2%)
    pmax x2, waiting for transfers between devices, col_dual(): summit = lax.pmax(peaks, 'src')  198 us
    psum x2, waiting for transfers between devices, col_dual(): whole = lax.psum(totals * jnp.exp(peaks - summit), 'src')  193 us
    dot_general x40, matrix products, cost_tile(): lax.dot_general(src_points, tgt_block, (((0,), (0,)), ((), ())), precisio...  190 us
    psum x1, waiting for transfers between devices, body(): moments = lax.psum(moments, 'src')  106 us
    reduce_sum x16, other arithmetic, row_visit(): jnp.sum(jnp.exp(scores - newest[:, None]), axis=1)  45.1 us
    dot_general x8, matrix products, weigh(): jnp.dot(src_points, weights, precision=lax.Precision.HIGHEST, preferred_e...  35.8 us
    pmax x2, blocking collectives, row_dual(): summit = lax.pmax(peak, 'tgt')  17.8 us
  transfers between devices with their start and end apart: 5, of which 5 were waited for; matrix products, arithmetic and copies ran while one was open for 0% of the time, Pallas kernels for 0%

commit v1 on v0

v1 whole, which is shorter than its diff:
```python
import functools
import math

import jax
import jax.numpy as jnp
from jax import lax
from jax.experimental import pallas as pl
from jax.experimental.pallas import tpu as pltpu
from jax.sharding import PartitionSpec as P

EPSILON = 0.5
LOG2E = 1.4426950408889634
UNIT = LOG2E / EPSILON
BF = jnp.bfloat16
F32 = jnp.float32
DEPTH = 256
VMEM_LIMIT = 56 * 2**20


def params():
    return pltpu.CompilerParams(vmem_limit_bytes=VMEM_LIMIT)


def log2(a):
    return jnp.log(a) * LOG2E


def split3(a):
    a1 = a.astype(BF)
    rest = a - a1.astype(F32)
    a2 = rest.astype(BF)
    rest = rest - a2.astype(F32)
    return a1, a2, rest.astype(BF)


def square_norm(points):
    return jnp.sum(points * points, axis=0, keepdims=True)


def build_still(points, term, out):
    n = points.shape[1]
    p1, p2, p3 = (p.astype(F32) for p in split3(points * (2 * UNIT)))
    t1, t2, t3 = (t.astype(F32) for t in split3(term))
    ones = jnp.ones((3, n), F32)
    zeros = jnp.zeros((DEPTH - 198, n), F32)
    whole = jnp.concatenate([p1, p1, p1, p2, p2, p3, t1, t2, t3, ones, zeros], axis=0)
    out[...] = whole.T.astype(BF)


def build_moving(points, term, out):
    n = points.shape[1]
    p1, p2, p3 = split3(points)
    t1, t2, t3 = (t.astype(F32) for t in split3(term))
    for row, part in enumerate((p1, p2, p3, p1, p2, p1)):
        out[32 * row : 32 * row + 32, :] = part
    ones, zeros = jnp.ones((3, n), F32), jnp.zeros((10, n), F32)
    out[192:208, :] = jnp.concatenate([ones, t1, t2, t3, zeros], axis=0).astype(BF)


def tree(op, items):
    items = list(items)
    while len(items) > 1:
        items = [op(a, b) for a, b in zip(items[::2], items[1::2])] + items[len(items) & ~1 :]
    return items[0]


def lanes(block):
    return jnp.concatenate([block[k : k + 1, :] for k in range(block.shape[0])], axis=1)


def rows(line):
    return jnp.concatenate([line[:, k : k + 128] for k in range(0, line.shape[1], 128)], axis=0)


def sweep(steps, make, multiply, process):
    make(0, 0)
    multiply(0)
    make(1, 1)

    def pair(t, carry):
        multiply(1)
        make(lax.rem(2 * t + 2, steps), 0)
        process(2 * t, 0)
        multiply(0)
        make(lax.rem(2 * t + 3, steps), 1)
        process(2 * t + 1, 1)
        return carry

    lax.fori_loop(0, steps // 2, pair, 0)


def row_first_kernel(tile, x_ref, y_ref, out, still, moving, scores, peak, total):
    count = x_ref.shape[1]
    x = x_ref[...]
    build_still(x, -UNIT * square_norm(x), still)
    moving[:, 208:DEPTH, :] = jnp.zeros((2, DEPTH - 208, tile), BF)
    peak[...] = jnp.full(peak.shape, -1e30, F32)
    total[...] = jnp.zeros(total.shape, F32)

    def make(t, slot):
        y = y_ref[:, pl.ds(pl.multiple_of(t * tile, tile), tile)]
        build_moving(y, -UNIT * square_norm(y), moving.at[slot])

    def multiply(slot):
        scores[slot] = jnp.dot(still[...], moving[slot], preferred_element_type=F32)

    def process(t, slot):
        for r in range(0, count, 8):
            s = [scores[slot, r : r + 8, k : k + 128] for k in range(0, tile, 128)]
            old = peak[r : r + 8, :]
            new = jnp.maximum(old, tree(jnp.maximum, s))
            part = tree(jnp.add, [jnp.exp2(a - new) for a in s])
            total[r : r + 8, :] = total[r : r + 8, :] * jnp.exp2(old - new) + part
            peak[r : r + 8, :] = new

    sweep(y_ref.shape[1] // tile, make, multiply, process)
    peaks = peak[...].T
    top = jnp.max(peaks, axis=0, keepdims=True)
    whole = jnp.sum(total[...].T * jnp.exp2(peaks - top), axis=0, keepdims=True)
    out[...] = jnp.concatenate([rows(top), rows(whole)], axis=0)


def row_first(x, y):
    tile, count = 1024, x.shape[1]
    return pl.pallas_call(
        functools.partial(row_first_kernel, tile),
        out_shape=jax.ShapeDtypeStruct((8, 128), F32),
        scratch_shapes=[
            pltpu.VMEM((count, DEPTH), BF),
            pltpu.VMEM((2, DEPTH, tile), BF),
            pltpu.VMEM((2, count, tile), F32),
            pltpu.VMEM((count, 128), F32),
            pltpu.VMEM((count, 128), F32),
        ],
        compiler_params=params(),
        name="row_first",
    )(x, y)


def col_first_kernel(tile, log_b, x_ref, y_ref, a0, a1, a2, a3, out, dual_out, still, moving, scores):
    count = x_ref.shape[1]
    parts = [a[...] for a in (a0, a1, a2, a3)]
    top = tree(jnp.maximum, [p[0:4] for p in parts])
    whole = tree(jnp.add, [p[4:8] * jnp.exp2(p[0:4] - top) for p in parts])
    dual = -(top + log2(whole) + log_b)
    dual_out[...] = dual
    x = x_ref[...]
    build_still(x, lanes(dual) - UNIT * square_norm(x), still)
    moving[:, 208:DEPTH, :] = jnp.zeros((2, DEPTH - 208, tile), BF)

    def make(t, slot):
        y = y_ref[:, pl.ds(pl.multiple_of(t * tile, tile), tile)]
        build_moving(y, -UNIT * square_norm(y), moving.at[slot])

    def multiply(slot):
        scores[slot] = jnp.dot(still[...], moving[slot], preferred_element_type=F32)

    def process(t, slot):
        tops, sums = [], []
        for k in range(0, tile, 128):
            peak = total = None
            for c in range(0, count, 128):
                s = [scores[slot, r : r + 8, k : k + 128] for r in range(c, c + 128, 8)]
                new = tree(jnp.maximum, s)
                if c:
                    new = jnp.maximum(peak, new)
                part = tree(jnp.add, [jnp.exp2(a - new) for a in s])
                total = total * jnp.exp2(peak - new) + part if c else part
                peak = new
            best = jnp.max(peak, axis=0, keepdims=True)
            tops.append(best)
            sums.append(jnp.sum(total * jnp.exp2(peak - best), axis=0, keepdims=True))
        out[t] = jnp.concatenate(tops + sums, axis=0)

    sweep(y_ref.shape[1] // tile, make, multiply, process)


def col_first(x, y, parts, log_b):
    tile, count = 512, x.shape[1]
    steps = y.shape[1] // tile
    return pl.pallas_call(
        functools.partial(col_first_kernel, tile, log_b),
        out_shape=(
            jax.ShapeDtypeStruct((steps, 8, 128), F32),
            jax.ShapeDtypeStruct((4, 128), F32),
        ),
        scratch_shapes=[
            pltpu.VMEM((count, DEPTH), BF),
            pltpu.VMEM((2, DEPTH, tile), BF),
            pltpu.VMEM((2, count, tile), F32),
        ],
        compiler_params=params(),
        name="col_first",
    )(x, y, *parts)


def join_targets_kernel(log_a, in_ref, own, out):
    top = in_ref[0, 0:4]
    for s in range(1, in_ref.shape[0]):
        top = jnp.maximum(top, in_ref[s, 0:4])
    whole = jnp.zeros((4, 128), F32)
    for s in range(in_ref.shape[0]):
        whole = whole + in_ref[s, 4:8] * jnp.exp2(in_ref[s, 0:4] - top)
    dual = -(top + log2(whole) + log_a)
    own[...] = dual
    for s in range(out.shape[0]):
        out[s] = dual


def join_targets(parts, log_a):
    return pl.pallas_call(
        functools.partial(join_targets_kernel, log_a),
        out_shape=(
            jax.ShapeDtypeStruct((4, 128), F32),
            jax.ShapeDtypeStruct((parts.shape[0], 4, 128), F32),
        ),
        compiler_params=params(),
        name="join_targets",
    )(parts)


def row_second_kernel(tile, log_b, x_ref, y_ref, f_ref, g_ref, out, still, moving, scores, total):
    count = x_ref.shape[1]
    x = x_ref[...]
    build_still(x, lanes(f_ref[...]) - UNIT * square_norm(x), still)
    moving[:, 208:DEPTH, :] = jnp.zeros((2, DEPTH - 208, tile), BF)
    total[...] = jnp.zeros(total.shape, F32)
    group = tile // 128

    def make(t, slot):
        y = y_ref[:, pl.ds(pl.multiple_of(t * tile, tile), tile)]
        g = lanes(g_ref[pl.ds(pl.multiple_of(t * group, group), group), :])
        build_moving(y, g + log_b - UNIT * square_norm(y), moving.at[slot])

    def multiply(slot):
        scores[slot] = jnp.dot(still[...], moving[slot], preferred_element_type=F32)

    def process(t, slot):
        for r in range(0, count, 8):
            e = [jnp.exp2(scores[slot, r : r + 8, k : k + 128]) for k in range(0, tile, 128)]
            total[r : r + 8, :] += tree(jnp.add, e)

    sweep(y_ref.shape[1] // tile, make, multiply, process)
    out[...] = rows(jnp.sum(total[...].T, axis=0, keepdims=True))


def row_second(x, y, f, g, log_b):
    tile, count = 1024, x.shape[1]
    return pl.pallas_call(
        functools.partial(row_second_kernel, tile, log_b),
        out_shape=jax.ShapeDtypeStruct((4, 128), F32),
        scratch_shapes=[
            pltpu.VMEM((count, DEPTH), BF),
            pltpu.VMEM((2, DEPTH, tile), BF),
            pltpu.VMEM((2, count, tile), F32),
            pltpu.VMEM((count, 128), F32),
        ],
        compiler_params=params(),
        name="row_second",
    )(x, y, f, g)


def join_sources_kernel(f_ref, a0, a1, a2, a3, own, out):
    whole = (a0[...] + a1[...]) + (a2[...] + a3[...])
    dual = f_ref[...] - log2(whole)
    own[...] = dual * (1.0 / UNIT)
    for s in range(out.shape[0]):
        out[s] = dual


def join_sources(f, parts, copies):
    return pl.pallas_call(
        join_sources_kernel,
        out_shape=(
            jax.ShapeDtypeStruct((4, 128), F32),
            jax.ShapeDtypeStruct((copies, 4, 128), F32),
        ),
        compiler_params=params(),
        name="join_sources",
    )(f, *parts)


def col_second_kernel(log_a, x_ref, f_ref, y_ref, g_ref, out, still, moving, scores, weights, values, total):
    tile = x_ref.shape[2]
    count = y_ref.shape[1]
    y = y_ref[...]
    g = g_ref[...]
    build_still(y, lanes(g) + log_a - UNIT * square_norm(y), still)
    moving[:, 208:DEPTH, :] = jnp.zeros((2, DEPTH - 208, tile), BF)
    values[:, 96:128, :] = jnp.ones((2, 32, 2 * tile), BF)
    total[...] = jnp.zeros(total.shape, F32)

    def make(t, slot):
        x = x_ref[t]
        f = lanes(f_ref[t])
        build_moving(x, f - UNIT * square_norm(x), moving.at[slot])

    def multiply(slot):
        scores[slot] = jnp.dot(still[...], moving[slot], preferred_element_type=F32)

    def process(t, slot):
        for part in range(3):
            piece = moving[slot, 32 * part : 32 * part + 32, :]
            values[slot, 32 * part : 32 * part + 32, 0:tile] = piece
            values[slot, 32 * part : 32 * part + 32, tile : 2 * tile] = piece
        for r in range(0, count, 16):
            for k in range(0, tile, 128):
                e = jnp.exp2(scores[slot, r : r + 16, k : k + 128])
                high = e.astype(BF)
                weights[slot, r : r + 16, k : k + 128] = high
                weights[slot, r : r + 16, tile + k : tile + k + 128] = (e - high.astype(F32)).astype(BF)
        total[...] += lax.dot_general(
            weights[slot], values[slot], (((1,), (1,)), ((), ())), preferred_element_type=F32
        )

    steps = x_ref.shape[0]
    make(0, 0)
    multiply(0)

    def pair(t, carry):
        make(2 * t + 1, 1)
        multiply(1)
        process(2 * t, 0)
        make(lax.rem(2 * t + 2, steps), 0)
        multiply(0)
        process(2 * t + 1, 1)
        return carry

    lax.fori_loop(0, steps // 2, pair, 0)
    sums = total[...].T
    weight = sums[96:97, :]
    mapped = (sums[0:32] + sums[32:64] + sums[64:96]) / weight
    for k in range(4):
        out[32 * k : 32 * k + 32, :] = mapped[:, 128 * k : 128 * k + 128]
    out[128:132, :] = (g - rows(log2(weight))) * (1.0 / UNIT)
    out[132:136, :] = jnp.zeros((4, 128), F32)


def col_second(x, f, y, g, log_a):
    steps, dims, tile = x.shape
    count = y.shape[1]
    return pl.pallas_call(
        functools.partial(col_second_kernel, log_a),
        out_shape=jax.ShapeDtypeStruct((136, 128), F32),
        scratch_shapes=[
            pltpu.VMEM((count, DEPTH), BF),
            pltpu.VMEM((2, DEPTH, tile), BF),
            pltpu.VMEM((2, count, tile), F32),
            pltpu.VMEM((2, count, 2 * tile), BF),
            pltpu.VMEM((2, 128, 2 * tile), BF),
            pltpu.VMEM((count, 128), F32),
        ],
        compiler_params=params(),
        name="col_second",
    )(x, f, y, g)


def unpack_kernel(in_ref, mapped, dual):
    for b in range(in_ref.shape[0]):
        for k in range(4):
            column = 512 * b + 128 * k
            mapped[:, column : column + 128] = in_ref[b, 32 * k : 32 * k + 32, :]
        dual[4 * b : 4 * b + 4, :] = in_ref[b, 128:132, :]


def unpack(parts):
    blocks, group = parts.shape[0], 8
    return pl.pallas_call(
        unpack_kernel,
        grid=(blocks // group,),
        in_specs=[pl.BlockSpec((group, 136, 128), lambda b: (b, 0, 0))],
        out_specs=(
            pl.BlockSpec((32, 512 * group), lambda b: (0, b)),
            pl.BlockSpec((4 * group, 128), lambda b: (b, 0)),
        ),
        out_shape=(
            jax.ShapeDtypeStruct((32, 512 * blocks), F32),
            jax.ShapeDtypeStruct((4 * blocks, 128), F32),
        ),
        compiler_params=params(),
        name="unpack",
    )(parts)


def over_tgt(part):
    n = lax.axis_size("tgt")
    turns = [[(i, (i + k) % n) for i in range(n)] for k in (1, 3, 2)]
    return [part] + [lax.ppermute(part, "tgt", turn) for turn in turns]


def body(x, y):
    sources, columns = lax.axis_size("src"), y.shape[1]
    log_a = -math.log2(x.shape[1] * sources)
    log_b = -math.log2(columns * lax.axis_size("tgt"))
    me = lax.axis_index("src")
    every_x = lax.all_gather(x, "src")
    own_y = lax.dynamic_slice_in_dim(y, me * (columns // sources), columns // sources, axis=1)

    first = over_tgt(row_first(x, y))
    partial, f1 = col_first(x, y, first, log_b)
    partial = lax.all_to_all(partial, "src", 0, 0)
    own_g, copies = join_targets(partial, log_a)
    g1 = lax.all_to_all(copies, "src", 0, 0)
    second = over_tgt(row_second(x, y, f1, g1.reshape(4 * sources, 128), log_b))
    source_dual, copies = join_sources(f1, second, sources)
    f2 = lax.all_to_all(copies, "src", 0, 0)
    block = col_second(every_x, f2, own_y, own_g, log_a)
    blocks = lax.all_to_all(jnp.broadcast_to(block[None], (sources, 136, 128)), "src", 0, 0)
    mapped, target_dual = unpack(blocks)
    return source_dual.reshape(-1), target_dual.reshape(-1), mapped


def solution(mesh):
    return jax.shard_map(
        body,
        mesh=mesh,
        in_specs=(P(None, "src"), P(None, "tgt")),
        out_specs=(P("src"), P("tgt"), P(None, "tgt")),
        check_vma=False,
    )
```

time: 849 us -> 168 us (0.20)
  waiting for transfers between devices: 496 us -> 14.2 us
  matrix products: 226 us -> 0 us
  other arithmetic: 60.8 us -> 0 us
  Pallas kernels: 0 us -> 57.8 us
  blocking collectives: 29.7 us -> 64.3 us
  local copies, waits for them, and re-layouts: 19.1 us -> 4.29 us
  starting transfers between devices: 0.61 us -> 12.6 us
    psum x3 -> x0, waiting for transfers between devices: 298 us -> none  [the longest x2 193 us: col_dual(): whole = lax.psum(totals * jnp.exp(peaks - summit), 'src')]
    dot_general x48 -> x0, matrix products: 226 us -> none  [the longest x40 190 us: cost_tile(): lax.dot_general(src_points, tgt_block, (((0,), (0,)), ((), ())), precisio...]
    pmax x2 -> x0, waiting for transfers between devices: 198 us -> none  [col_dual(): summit = lax.pmax(peaks, 'src')]
    all_to_all x0 -> x3, blocking collectives: none -> 64.3 us  [the longest x1 34 us: body(): lax.all_to_all(jnp.broadcast_to(block[None], (sources, 136, 128)), 'src',...]
    pallas_call x0 -> x7, Pallas kernels: none -> 57.8 us  [the longest x1 18.9 us: col_second(): pl.pallas_call(functools.partial(col_second_kernel, log_a), out_shape=jax...]
    reduce_sum x34 -> x0, other arithmetic: 55.6 us -> none  [the longest x16 45.1 us: row_visit(): jnp.sum(jnp.exp(scores - newest[:, None]), axis=1)]
    pmax x2 -> x0, blocking collectives: 17.8 us -> none  [row_dual(): summit = lax.pmax(peak, 'tgt')]
    psum x2 -> x0, blocking collectives: 12 us -> none  [row_dual(): whole = lax.psum(total * jnp.exp(peak - summit), 'tgt')]
  transfers between devices with their start and end apart: 5 -> 8, of which waited for: 5 -> 5; matrix products, arithmetic and copies ran while one was open for 0% -> 1% of each run, Pallas kernels for 0% -> 21%
where the time goes in v1:
time: 168 us; the launch traced here: 167 us
  blocking collectives  64.3 us (38%)
  Pallas kernels  57.8 us (34%)
  waiting for transfers between devices  14.2 us (8%)
  between operations  14.1 us (8%)
  starting transfers between devices  12.6 us (8%)
  local copies, waits for them, and re-layouts  4.29 us (3%)
    all_to_all x1, blocking collectives, body(): lax.all_to_all(jnp.broadcast_to(block[None], (sources, 136, 128)), 'src',...  34 us
    pallas_call x1, Pallas kernels, col_second(): pl.pallas_call(functools.partial(col_second_kernel, log_a), out_shape=jax...  18.9 us
    all_to_all x1, blocking collectives, body(): partial = lax.all_to_all(partial, 'src', 0, 0)  18 us
    all_to_all x1, blocking collectives, body(): g1 = lax.all_to_all(copies, 'src', 0, 0)  12.2 us
    pallas_call x1, Pallas kernels, col_first(): pl.pallas_call(functools.partial(col_first_kernel, tile, log_b), out_shap...  11.7 us
    pallas_call x1, Pallas kernels, row_first(): pl.pallas_call(functools.partial(row_first_kernel, tile), out_shape=jax.S...  11.6 us
    pallas_call x1, Pallas kernels, row_second(): pl.pallas_call(functools.partial(row_second_kernel, tile, log_b), out_sha...  8.82 us
    ppermute x6, waiting for transfers between devices, over_tgt(): return [part] + [lax.ppermute(part, 'tgt', turn) for turn in turns]  7.52 us
  transfers between devices with their start and end apart: 8, of which 5 were waited for; matrix products, arithmetic and copies ran while one was open for 1% of the time, Pallas kernels for 21%

profile of v1, /device:TPU:1, one launch (start us, length us, event | category | flops | bytes accessed | tf_op | source)
XLA Modules:
  0.0 167.3 jit_solution(3677597600616454285)
XLA Ops:
  7.2 0.0 all-gather.3.cloned.1.call-start
  7.2 0.7 all-gather.3.cloned.1.call-update
  7.9 11.6 %row_first.1.a0 = f32[8,128]{1,0:T(8,128)} custom-call(f32[32,512]{1,0:T(8,128)} %x_ref.5, f32[32,16384]{1,0:T(8,128)} %y_ref.5), custom_call_target="tpu_custom_call" | custom-call | tf_op jit(solution)/shard_map/row_first/pallas_call | solution.py:125
  19.5 3.6 %collective-permute-start.2 = (f32[8,128]{1,0:T(8,128)}, f32[8,128]{1,0:T(8,128)S(1)}, u32[]{:S(2)}, u32[]{:S(2)}) collective-permute-start(f32[8,128]{1,0:T(8,128)} %row_first.1.a0), channel_id=1, source_target_pairs={{0,2},{1,3},{2,0},{3,1},{4,6},{5,7},{6,4},{7,5},{8,10},{9,11},{10,... | collective-permute-start | bytes 12296 | tf_op jit(solution)/shard_map/ppermute | solution.py:388
  23.1 0.9 collective-permute-start.1
  23.9 0.6 collective-permute-start
  24.5 0.0 collective-permute-done.2.a3
  24.5 0.0 copy-start.1
  24.5 1.3 collective-permute-done.1.a2
  25.9 0.0 copy-start.2
  25.9 2.4 %collective-permute-done.a1 = f32[8,128]{1,0:T(8,128)S(1)} collective-permute-done((f32[8,128]{1,0:T(8,128)}, f32[8,128]{1,0:T(8,128)S(1)}, u32[]{:S(2)}, u32[]{:S(2)}) %collective-permute-start) | collective-permute-done | bytes 4128 | tf_op jit(solution)/shard_map/ppermute | solution.py:388
  28.2 0.0 copy-done.1
  28.2 0.0 copy-done.2
  28.2 0.0 copy-start.3
  28.2 0.6 copy-done.3
  28.8 11.7 %col_first.1 = (f32[32,8,128]{2,1,0:T(8,128)}, f32[4,128]{1,0:T(4,128)}) custom-call(f32[32,512]{1,0:T(8,128)} %x_ref.5, f32[32,16384]{1,0:T(8,128)} %y_ref.5, f32[8,128]{1,0:T(8,128)} %row_first.1.a0, f32[8,128]{1,0:T(8,128)} %copy-done.3, f32[8,128]{1,0:T(8,128)} %copy-done.2, f32[8,128]{1,0:T(8,128)} %copy-done.1), custom_call_target="tpu_custom_call" | custom-call | tf_op jit(solution)/shard_map/col_first/pallas_call | solution.py:181
  40.5 18.0 %all_to_all.20.in_ref = f32[32,8,128]{2,1,0:T(8,128)} all-to-all(f32[32,8,128]{2,1,0:T(8,128)} %get-tuple-element.12), channel_id=1, replica_groups=mesh['src'=32,'tgt'=4] {'src'}, dimensions={0} | all-to-all | bytes 262144 | tf_op jit(solution)/shard_map/all_to_all | solution.py:401
  58.5 1.6 join_targets.1
  60.2 12.2 %all_to_all.21 = f32[32,4,128]{2,1,0:T(4,128)} all-to-all(f32[32,4,128]{2,1,0:T(4,128)} %get-tuple-element.13), channel_id=1, replica_groups=mesh['src'=32,'tgt'=4] {'src'}, dimensions={0} | all-to-all | bytes 131072 | tf_op jit(solution)/shard_map/all_to_all | solution.py:403
  72.4 8.8 %row_second.1.a0 = f32[4,128]{1,0:T(4,128)} custom-call(f32[32,512]{1,0:T(8,128)} %x_ref.5, f32[32,16384]{1,0:T(8,128)} %y_ref.5, f32[4,128]{1,0:T(4,128)} %get-tuple-element.11.f_ref, f32[128,128]{1,0:T(8,128)} %bitcast.5), custom_call_target="tpu_custom_call" | custom-call | tf_op jit(solution)/shard_map/row_second/pallas_call | solution.py:249
  81.2 0.2 collective-permute-start.5
  81.4 1.7 %collective-permute-start.4 = (f32[4,128]{1,0:T(4,128)}, f32[4,128]{1,0:T(4,128)S(1)}, u32[]{:S(2)}, u32[]{:S(2)}) collective-permute-start(f32[4,128]{1,0:T(4,128)} %row_second.1.a0), channel_id=1, source_target_pairs={{0,3},{1,0},{2,1},{3,2},{4,7},{5,4},{6,5},{7,6},{8,11},{9,8},{10,9... | collective-permute-start | bytes 6152 | tf_op jit(solution)/shard_map/ppermute | solution.py:388
  83.1 0.0 collective-permute-start.3
  83.1 2.2 %collective-permute-done.5.a3 = f32[4,128]{1,0:T(4,128)S(1)} collective-permute-done((f32[4,128]{1,0:T(4,128)}, f32[4,128]{1,0:T(4,128)S(1)}, u32[]{:S(2)}, u32[]{:S(2)}) %collective-permute-start.5) | collective-permute-done | bytes 2080 | tf_op jit(solution)/shard_map/ppermute | solution.py:388
  85.4 0.0 copy-start.4
  85.4 0.0 collective-permute-done.4.a2
  85.4 0.0 copy-start.5
  85.4 1.6 collective-permute-done.3.a1
  87.0 0.0 copy-done.4
  87.0 0.0 copy-done.5
  87.0 0.0 copy-start.6
  87.0 0.6 copy-done.6
  87.6 1.4 join_sources.1
  88.9 5.6 %all-to-all-start.2 = ((f32[32,4,128]{2,1,0:T(4,128)}), f32[32,4,128]{2,1,0:T(4,128)S(1)}, u32[]{:S(2)}, u32[]{:S(2)}) async-start(f32[32,4,128]{2,1,0:T(4,128)} %get-tuple-element.15), calls=%async_computation.2 | async-start | bytes 131072 | tf_op jit(solution)/shard_map/all_to_all | solution.py:406
  94.5 1.5 constant_dynamic-slice_fusion.y_ref
  96.0 6.0 %all-to-all-done.2.f_ref = f32[32,4,128]{2,1,0:T(4,128)S(1)} async-done(((f32[32,4,128]{2,1,0:T(4,128)}), f32[32,4,128]{2,1,0:T(4,128)S(1)}, u32[]{:S(2)}, u32[]{:S(2)}) %all-to-all-start.2) | async-done | bytes 65568 | tf_op jit(solution)/shard_map/all_to_all | solution.py:406
  102.0 0.0 copy-start
  102.0 0.0 all-gather.3.cloned.1.call-done
  102.0 0.6 copy-done
  102.6 18.9 %col_second.1 = f32[136,128]{1,0:T(8,128)} custom-call(f32[32,32,512]{2,1,0:T(8,128)} %bitcast.4, f32[32,4,128]{2,1,0:T(4,128)} %copy-done, f32[32,512]{1,0:T(8,128)} %constant_dynamic-slice_fusion.y_ref, f32[4,128]{1,0:T(4,128)} %get-tuple-element.16.g_ref), custom_call_target="tpu_custom_call" | custom-call | tf_op jit(solution)/shard_map/col_second/pallas_call | solution.py:342
  121.6 1.0 broadcast_in_dim.2
  122.6 34.0 %all_to_all.22.in_ref = f32[32,136,128]{2,1,0:T(8,128)} all-to-all(f32[32,136,128]{2,1,0:T(8,128)S(1)} %broadcast_in_dim.2), channel_id=1, replica_groups=mesh['src'=32,'tgt'=4] {'src'}, dimensions={0} | all-to-all | bytes 4456448 | tf_op jit(solution)/shard_map/all_to_all | solution.py:408
  156.6 3.8 %unpack.1 = (f32[32,16384]{1,0:T(8,128)}, f32[128,128]{1,0:T(8,128)}) custom-call(f32[32,136,128]{2,1,0:T(8,128)} %all_to_all.22.in_ref), custom_call_target="tpu_custom_call" | custom-call | tf_op jit(solution)/shard_map/unpack/pallas_call | solution.py:368
Async XLA Ops:
  7.2 94.9 %all-gather.3.cloned.1.call-start = ((), (), s32[]{:S(2)}) async-start(), calls=%async_computation.4 | async-start | bytes 2162688 | tf_op jit(solution)/shard_map/all_gather | solution.py:396
  19.5 5.0 %collective-permute-start.2 = (f32[8,128]{1,0:T(8,128)}, f32[8,128]{1,0:T(8,128)S(1)}, u32[]{:S(2)}, u32[]{:S(2)}) collective-permute-start(f32[8,128]{1,0:T(8,128)} %row_first.1.a0), channel_id=1, source_target_pairs={{0,2},{1,3},{2,0},{3,1},{4,6},{5,7},{6,4},{7,5},{8,10},{9,11},{10,... | collective-permute-start | bytes 12296 | tf_op jit(solution)/shard_map/ppermute | solution.py:388
  23.1 2.8 %collective-permute-start.1 = (f32[8,128]{1,0:T(8,128)}, f32[8,128]{1,0:T(8,128)S(1)}, u32[]{:S(2)}, u32[]{:S(2)}) collective-permute-start(f32[8,128]{1,0:T(8,128)} %row_first.1.a0), channel_id=1, source_target_pairs={{0,3},{1,0},{2,1},{3,2},{4,7},{5,4},{6,5},{7,6},{8,11},{9,8},{10,9... | collective-permute-start | bytes 12296 | tf_op jit(solution)/shard_map/ppermute | solution.py:388
  23.9 4.3 %collective-permute-start = (f32[8,128]{1,0:T(8,128)}, f32[8,128]{1,0:T(8,128)S(1)}, u32[]{:S(2)}, u32[]{:S(2)}) collective-permute-start(f32[8,128]{1,0:T(8,128)} %row_first.1.a0), channel_id=1, source_target_pairs={{0,1},{1,2},{2,3},{3,0},{4,5},{5,6},{6,7},{7,4},{8,9},{9,10},{10,1... | collective-permute-start | bytes 12296 | tf_op jit(solution)/shard_map/ppermute | solution.py:388
  24.5 3.7 %copy-start.1 = (f32[8,128]{1,0:T(8,128)}, f32[8,128]{1,0:T(8,128)S(1)}, u32[]{:S(2)}) copy-start(f32[8,128]{1,0:T(8,128)S(1)} %collective-permute-done.2.a3) | copy-start | bytes 12292
  25.9 2.4 %copy-start.2 = (f32[8,128]{1,0:T(8,128)}, f32[8,128]{1,0:T(8,128)S(1)}, u32[]{:S(2)}) copy-start(f32[8,128]{1,0:T(8,128)S(1)} %collective-permute-done.1.a2) | copy-start | bytes 12292
  28.2 0.6 copy-start.3
  81.2 4.2 %collective-permute-start.5 = (f32[4,128]{1,0:T(4,128)}, f32[4,128]{1,0:T(4,128)S(1)}, u32[]{:S(2)}, u32[]{:S(2)}) collective-permute-start(f32[4,128]{1,0:T(4,128)} %row_second.1.a0), channel_id=1, source_target_pairs={{0,2},{1,3},{2,0},{3,1},{4,6},{5,7},{6,4},{7,5},{8,10},{9,11},{10,... | collective-permute-start | bytes 6152 | tf_op jit(solution)/shard_map/ppermute | solution.py:388
  81.4 4.0 %collective-permute-start.4 = (f32[4,128]{1,0:T(4,128)}, f32[4,128]{1,0:T(4,128)S(1)}, u32[]{:S(2)}, u32[]{:S(2)}) collective-permute-start(f32[4,128]{1,0:T(4,128)} %row_second.1.a0), channel_id=1, source_target_pairs={{0,3},{1,0},{2,1},{3,2},{4,7},{5,4},{6,5},{7,6},{8,11},{9,8},{10,9... | collective-permute-start | bytes 6152 | tf_op jit(solution)/shard_map/ppermute | solution.py:388
  83.1 3.9 %collective-permute-start.3 = (f32[4,128]{1,0:T(4,128)}, f32[4,128]{1,0:T(4,128)S(1)}, u32[]{:S(2)}, u32[]{:S(2)}) collective-permute-start(f32[4,128]{1,0:T(4,128)} %row_second.1.a0), channel_id=1, source_target_pairs={{0,1},{1,2},{2,3},{3,0},{4,5},{5,6},{6,7},{7,4},{8,9},{9,10},{10,1... | collective-permute-start | bytes 6152 | tf_op jit(solution)/shard_map/ppermute | solution.py:388
  85.4 1.6 copy-start.4
  85.4 1.6 copy-start.5
  87.0 0.6 copy-start.6
  88.9 13.1 %all-to-all-start.2 = ((f32[32,4,128]{2,1,0:T(4,128)}), f32[32,4,128]{2,1,0:T(4,128)S(1)}, u32[]{:S(2)}, u32[]{:S(2)}) async-start(f32[32,4,128]{2,1,0:T(4,128)} %get-tuple-element.15), calls=%async_computation.2 | async-start | bytes 131072 | tf_op jit(solution)/shard_map/all_to_all | solution.py:406
  102.0 0.6 copy-start
Sparse Core Ops, SparseCore 0:
  10.3 48.1 all-gather.2

commit v2 on v0

v2 whole, which is shorter than its diff:
```python
import functools
import math

import jax
import jax.numpy as jnp
from jax import lax
from jax.experimental import pallas as pl
from jax.experimental.pallas import tpu as pltpu
from jax.sharding import Mesh
from jax.sharding import PartitionSpec as P

EPSILON = 0.5
LOG2E = 1.4426950408889634
UNIT = LOG2E / EPSILON
BF = jnp.bfloat16
F32 = jnp.float32
DEPTH = 256
VMEM_LIMIT = 56 * 2**20


def params():
    return pltpu.CompilerParams(vmem_limit_bytes=VMEM_LIMIT)


def log2(a):
    return jnp.log(a) * LOG2E


def split3(a):
    a1 = a.astype(BF)
    rest = a - a1.astype(F32)
    a2 = rest.astype(BF)
    rest = rest - a2.astype(F32)
    return a1, a2, rest.astype(BF)


def square_norm(points):
    return jnp.sum(points * points, axis=0, keepdims=True)


def build_still(points, term, out, shift=None):
    n = points.shape[1]
    p1, p2, p3 = (p.astype(F32) for p in split3(points * (2 * UNIT)))
    out[:, 0:128] = jnp.concatenate([p1, p1, p1, p2], axis=0).T.astype(BF)
    out[:, 128:256] = jnp.concatenate([p2, p3, still_terms(term, shift)], axis=0).T.astype(BF)


def still_terms(term, shift):
    n = term.shape[1]
    parts = [t.astype(F32) for t in split3(term)] + [jnp.ones((3, n), F32)]
    if shift is not None:
        parts += [t.astype(F32) for t in split3(shift)]
    return jnp.concatenate(parts + [jnp.zeros((64 - sum(p.shape[0] for p in parts), n), F32)], axis=0)


def build_moving(points, term, out):
    n = points.shape[1]
    p1, p2, p3 = split3(points)
    t1, t2, t3 = (t.astype(F32) for t in split3(term))
    for row, part in enumerate((p1, p2, p3, p1, p2, p1)):
        out[32 * row : 32 * row + 32, :] = part
    ones, zeros = jnp.ones((3, n), F32), jnp.zeros((7, n), F32)
    out[192:208, :] = jnp.concatenate([ones, t1, t2, t3, ones, zeros], axis=0).astype(BF)


def tree(op, items):
    items = list(items)
    while len(items) > 1:
        items = [op(a, b) for a, b in zip(items[::2], items[1::2])] + items[len(items) & ~1 :]
    return items[0]


def lanes(block):
    return jnp.concatenate([block[k : k + 1, :] for k in range(block.shape[0])], axis=1)


def rows(line):
    return jnp.concatenate([line[:, k : k + 128] for k in range(0, line.shape[1], 128)], axis=0)


def sweep(steps, make, multiply, process):
    make(0, 0)
    multiply(0)
    make(1, 1)

    def pair(t, carry):
        multiply(1)
        make(lax.rem(2 * t + 2, steps), 0)
        process(2 * t, 0)
        multiply(0)
        make(lax.rem(2 * t + 3, steps), 1)
        process(2 * t + 1, 1)
        return carry

    lax.fori_loop(0, steps // 2, pair, 0)


def row_first_kernel(tile, x_ref, y_ref, out, still, moving, scores, peak, total):
    count = x_ref.shape[1]
    steps = y_ref.shape[1] // tile
    x = x_ref[...]
    norm = -UNIT * square_norm(x)
    build_still(x, norm, still)
    moving[:, 208:DEPTH, :] = jnp.zeros((2, DEPTH - 208, tile), BF)
    peak[...] = jnp.zeros(peak.shape, F32)
    total[...] = jnp.zeros(total.shape, F32)

    def make(t, slot):
        y = y_ref[:, pl.ds(pl.multiple_of(t * tile, tile), tile)]
        build_moving(y, -UNIT * square_norm(y), moving.at[slot])

    def multiply(slot):
        scores[slot] = jnp.dot(still[...], moving[slot], preferred_element_type=F32)

    make(0, 0)
    sample = jnp.dot(still[...], moving[0, :, 0:256], preferred_element_type=F32)
    base = jnp.max(jnp.maximum(sample[:, 0:128], sample[:, 128:256]).T, axis=0, keepdims=True)
    _, p2, p3 = split3(x * (2 * UNIT))
    terms = still_terms(norm, -base)
    still[:, 128:256] = jnp.concatenate([p2.astype(F32), p3.astype(F32), terms], axis=0).T.astype(BF)

    def process(t, slot):
        for r in range(0, count, 8):
            e = [jnp.exp2(scores[slot, r : r + 8, k : k + 128]) for k in range(0, tile, 128)]
            total[r : r + 8, :] += tree(jnp.add, e)

    sweep(steps, make, multiply, process)

    @pl.when(jnp.max(total[...]) > 1e34)
    def _():
        peak[...] = jnp.full(peak.shape, -1e30, F32)
        total[...] = jnp.zeros(total.shape, F32)

        def step(t, carry):
            make(t, 0)
            multiply(0)
            for r in range(0, count, 8):
                s = [scores[0, r : r + 8, k : k + 128] for k in range(0, tile, 128)]
                old = peak[r : r + 8, :]
                new = jnp.maximum(old, tree(jnp.maximum, s))
                part = tree(jnp.add, [jnp.exp2(a - new) for a in s])
                total[r : r + 8, :] = total[r : r + 8, :] * jnp.exp2(old - new) + part
                peak[r : r + 8, :] = new
            return carry

        lax.fori_loop(0, steps, step, 0)

    peaks = peak[...].T
    top = jnp.max(peaks, axis=0, keepdims=True)
    whole = jnp.sum(total[...].T * jnp.exp2(peaks - top), axis=0, keepdims=True)
    pair = jnp.concatenate([rows(top + base), rows(whole)], axis=0)
    for s in range(out.shape[0]):
        out[s] = pair


def row_first(x, y, copies):
    tile, count = 1024, x.shape[1]
    return pl.pallas_call(
        functools.partial(row_first_kernel, tile),
        out_shape=jax.ShapeDtypeStruct((copies, 8, 128), F32),
        scratch_shapes=[
            pltpu.VMEM((count, DEPTH), BF),
            pltpu.VMEM((2, DEPTH, tile), BF),
            pltpu.VMEM((2, count, tile), F32),
            pltpu.VMEM((count, 128), F32),
            pltpu.VMEM((count, 128), F32),
        ],
        compiler_params=params(),
        name="row_first",
    )(x, y)


def col_first_kernel(tile, log_b, at, x0, x1, x2, x3, parts, y_ref, out, dual_out, still, moving, scores, found):
    count = x0.shape[1]
    half = found.shape[0] // 2
    for k, x_ref in enumerate((x0, x1, x2, x3)):
        row = (at[0] + 4 - k) % 4
        pieces = [parts[4 * s + row] for s in range(4)]
        top = tree(jnp.maximum, [p[0:4] for p in pieces])
        whole = tree(jnp.add, [p[4:8] * jnp.exp2(p[0:4] - top) for p in pieces])
        dual = -(top + log2(whole) + log_b)
        dual_out[4 * k : 4 * k + 4, :] = dual
        x = x_ref[...]
        build_still(x, lanes(dual) - UNIT * square_norm(x), still.at[pl.ds(count * k, count)])
    moving[:, 208:DEPTH, :] = jnp.zeros((2, DEPTH - 208, tile), BF)

    def make(t, slot):
        y = y_ref[:, pl.ds(pl.multiple_of(t * tile, tile), tile)]
        build_moving(y, -UNIT * square_norm(y), moving.at[slot])

    def multiply(slot):
        scores[slot] = jnp.dot(still[...], moving[slot], preferred_element_type=F32)

    def process(t, slot):
        for k in range(0, tile, 128):
            column = slice(k, k + 128)
            total = [jnp.exp2(scores[slot, 8 * q : 8 * q + 8, column]) for q in range(8)]
            for r in range(64, 4 * count, 64):
                total = [a + jnp.exp2(scores[slot, r + 8 * q : r + 8 * q + 8, column]) for q, a in enumerate(total)]
            found[pl.ds(half + 2 * t + k // 128, 1), :] = jnp.sum(tree(jnp.add, total), axis=0, keepdims=True)

    found[0:half, :] = jnp.zeros((half, 128), F32)
    steps = y_ref.shape[1] // tile
    sweep(steps, make, multiply, process)

    @pl.when(jnp.min(found[half:, :]) < 1e-25)
    def _():
        def step(t, carry):
            make(t, 0)
            multiply(0)
            for k in range(0, tile, 128):
                peak = jnp.full((8, 128), -1e30, F32)
                total = jnp.zeros((8, 128), F32)
                for r in range(0, 4 * count, 128):
                    s = [scores[0, r + q : r + q + 8, k : k + 128] for q in range(0, 128, 8)]
                    new = jnp.maximum(peak, tree(jnp.maximum, s))
                    total = total * jnp.exp2(peak - new) + tree(jnp.add, [jnp.exp2(a - new) for a in s])
                    peak = new
                best = jnp.max(peak, axis=0, keepdims=True)
                found[pl.ds(2 * t + k // 128, 1), :] = best
                whole = jnp.sum(total * jnp.exp2(peak - best), axis=0, keepdims=True)
                found[pl.ds(half + 2 * t + k // 128, 1), :] = whole
            return carry

        lax.fori_loop(0, steps, step, 0)

    for s in range(out.shape[0]):
        out[s] = found[...]


def at_start(shape):
    return pl.BlockSpec(shape, lambda i, at: (0,) * len(shape))


def col_first(at, blocks, parts, y, log_b, copies):
    tile, count = 256, blocks[0].shape[1]
    width = y.shape[1] // 4
    lines = width // 64
    return pl.pallas_call(
        functools.partial(col_first_kernel, tile, log_b),
        out_shape=(
            jax.ShapeDtypeStruct((copies, lines, 128), F32),
            jax.ShapeDtypeStruct((16, 128), F32),
        ),
        grid_spec=pltpu.PrefetchScalarGridSpec(
            num_scalar_prefetch=1,
            grid=(1,),
            in_specs=[at_start(b.shape) for b in blocks]
            + [at_start(parts.shape), pl.BlockSpec((32, width), lambda i, at: (0, at[0]))],
            out_specs=(at_start((copies, lines, 128)), at_start((16, 128))),
            scratch_shapes=[
                pltpu.VMEM((4 * count, DEPTH), BF),
                pltpu.VMEM((2, DEPTH, tile), BF),
                pltpu.VMEM((2, 4 * count, tile), F32),
                pltpu.VMEM((lines, 128), F32),
            ],
        ),
        compiler_params=params(),
        name="col_first",
    )(at, *blocks, parts, y)


def row_second_kernel(
    tile, log_a, log_b, at, x0, x1, x2, x3, f_ref, parts, y_ref, out, own, every, still, moving, scores, total, dual
):
    count = x0.shape[1]
    half = parts.shape[1] // 2
    top = tree(jnp.maximum, [parts[s, 0:half] for s in range(parts.shape[0])])
    whole = tree(jnp.add, [parts[s, half:] * jnp.exp2(parts[s, 0:half] - top) for s in range(parts.shape[0])])
    g = -(top + log2(whole) + log_a)
    every[...] = g
    for t in range(half // 2):
        dual[t] = g[2 * t : 2 * t + 2]
    own[...] = jnp.concatenate([dual[2 * at[1]], dual[2 * at[1] + 1]], axis=0)
    for k, x_ref in enumerate((x0, x1, x2, x3)):
        x = x_ref[...]
        f = lanes(f_ref[4 * k : 4 * k + 4])
        build_still(x, f - UNIT * square_norm(x), still.at[pl.ds(count * k, count)])
    moving[:, 208:DEPTH, :] = jnp.zeros((2, DEPTH - 208, tile), BF)
    total[...] = jnp.zeros(total.shape, F32)

    def make(t, slot):
        y = y_ref[:, pl.ds(pl.multiple_of(t * tile, tile), tile)]
        build_moving(y, lanes(dual[t]) + log_b - UNIT * square_norm(y), moving.at[slot])

    def multiply(slot):
        scores[slot] = jnp.dot(still[...], moving[slot], preferred_element_type=F32)

    def process(t, slot):
        for r in range(0, 4 * count, 8):
            e = [jnp.exp2(scores[slot, r : r + 8, k : k + 128]) for k in range(0, tile, 128)]
            total[r : r + 8, :] += tree(jnp.add, e)

    sweep(y_ref.shape[1] // tile, make, multiply, process)
    for k in range(4):
        line = jnp.sum(total[count * k : count * k + count, :].T, axis=0, keepdims=True)
        row = (at[0] + 4 - k) % 4
        for s in range(out.shape[0]):
            out[s, row] = rows(line)


def row_second(at, blocks, f, parts, y, log_a, log_b, copies):
    tile, count = 256, blocks[0].shape[1]
    width = y.shape[1] // 4
    return pl.pallas_call(
        functools.partial(row_second_kernel, tile, log_a, log_b),
        out_shape=(
            jax.ShapeDtypeStruct((copies, 4, 4, 128), F32),
            jax.ShapeDtypeStruct((4, 128), F32),
            jax.ShapeDtypeStruct((width // 128, 128), F32),
        ),
        grid_spec=pltpu.PrefetchScalarGridSpec(
            num_scalar_prefetch=1,
            grid=(1,),
            in_specs=[at_start(b.shape) for b in blocks]
            + [at_start(f.shape), at_start(parts.shape), pl.BlockSpec((32, width), lambda i, at: (0, at[0]))],
            out_specs=(at_start((copies, 4, 4, 128)), at_start((4, 128)), at_start((width // 128, 128))),
            scratch_shapes=[
                pltpu.VMEM((4 * count, DEPTH), BF),
                pltpu.VMEM((2, DEPTH, tile), BF),
                pltpu.VMEM((2, 4 * count, tile), F32),
                pltpu.VMEM((4 * count, 128), F32),
                pltpu.VMEM((width // tile, 2, 128), F32),
            ],
        ),
        compiler_params=params(),
        name="row_second",
    )(at, *blocks, f, parts, y)


def col_second_kernel(
    tile, log_a, at, x0, x1, x2, x3, f_ref, parts, y_ref, g_ref, out, own, still, moving, scores, weights, values, dual
):
    count = x0.shape[1]
    half = 4 * count
    for k, x_ref in enumerate((x0, x1, x2, x3)):
        row = (at[0] + 4 - k) % 4
        whole = tree(jnp.add, [parts[s, row] for s in range(parts.shape[0])])
        f = f_ref[4 * k : 4 * k + 4, :] - log2(whole)
        if k == 0:
            own[...] = f * (1.0 / UNIT)
        x = x_ref[...]
        build_still(x, lanes(f) - UNIT * square_norm(x), still.at[pl.ds(count * k, count)])
        for part, piece in enumerate(split3(x)):
            values[32 * part : 32 * part + 32, count * k : count * k + count] = piece
            values[32 * part : 32 * part + 32, half + count * k : half + count * k + count] = piece
    values[96:112, :] = jnp.ones((16, 2 * half), BF)
    moving[:, 208:DEPTH, :] = jnp.zeros((2, DEPTH - 208, tile), BF)
    weights[1] = jnp.zeros((2 * half, tile), BF)
    out[:, 128:136, :] = jnp.zeros((out.shape[0], 8, 128), F32)
    for t in range(dual.shape[0]):
        dual[t] = g_ref[2 * t : 2 * t + 2, :]

    def make(t, slot):
        y = y_ref[:, pl.ds(pl.multiple_of(t * tile, tile), tile)]
        build_moving(y, lanes(dual[t]) + log_a - UNIT * square_norm(y), moving.at[slot])

    def multiply(slot):
        scores[slot] = jnp.dot(still[...], moving[slot], preferred_element_type=F32)

    def weigh(slot):
        for r in range(0, half, 16):
            for k in range(0, tile, 128):
                e = jnp.exp2(scores[slot, r : r + 16, k : k + 128])
                high = e.astype(BF)
                weights[slot, r : r + 16, k : k + 128] = high
                weights[slot, half + r : half + r + 16, k : k + 128] = (e - high.astype(F32)).astype(BF)

    def gather(block, slot):
        sums = jnp.dot(values[...], weights[slot], preferred_element_type=F32)
        moment = sums[0:32] + sums[32:64] + sums[64:96]
        for h in range(2):
            k = 2 * slot + h
            out[block, 32 * k : 32 * k + 32, :] = moment[:, 128 * h : 128 * h + 128]
            out[block, 128 + k : 129 + k, :] = sums[96:97, 128 * h : 128 * h + 128]

    steps = y_ref.shape[1] // tile
    make(0, 0)
    multiply(0)
    make(1, 1)

    def pair(t, carry):
        multiply(1)
        make(lax.rem(2 * t + 2, steps), 0)
        gather(lax.rem(t + steps // 2 - 1, steps // 2), 1)
        weigh(0)
        multiply(0)
        make(lax.rem(2 * t + 3, steps), 1)
        gather(t, 0)
        weigh(1)
        return carry

    lax.fori_loop(0, steps // 2, pair, 0)
    gather(steps // 2 - 1, 1)


def col_second(at, blocks, f, parts, y, g, log_a):
    tile, count = 256, blocks[0].shape[1]
    width = y.shape[1] // 4
    return pl.pallas_call(
        functools.partial(col_second_kernel, tile, log_a),
        out_shape=(
            jax.ShapeDtypeStruct((width // 512, 136, 128), F32),
            jax.ShapeDtypeStruct((4, 128), F32),
        ),
        grid_spec=pltpu.PrefetchScalarGridSpec(
            num_scalar_prefetch=1,
            grid=(1,),
            in_specs=[at_start(b.shape) for b in blocks]
            + [at_start(f.shape), at_start(parts.shape), pl.BlockSpec((32, width), lambda i, at: (0, at[0]))]
            + [at_start(g.shape)],
            out_specs=(at_start((width // 512, 136, 128)), at_start((4, 128))),
            scratch_shapes=[
                pltpu.VMEM((4 * count, DEPTH), BF),
                pltpu.VMEM((2, DEPTH, tile), BF),
                pltpu.VMEM((2, 4 * count, tile), F32),
                pltpu.VMEM((2, 8 * count, tile), BF),
                pltpu.VMEM((112, 8 * count), BF),
                pltpu.VMEM((width // tile, 2, 128), F32),
            ],
        ),
        compiler_params=params(),
        name="col_second",
    )(at, *blocks, f, parts, y, g)


def finish_kernel(parts, g_ref, out):
    sums = tree(jnp.add, [parts[s] for s in range(parts.shape[0])])
    for k in range(4):
        out[32 * k : 32 * k + 32, :] = sums[32 * k : 32 * k + 32] / sums[128 + k : 129 + k]
    dual = (g_ref[...] - log2(sums[128:132])) * (1.0 / UNIT)
    out[128:136, :] = jnp.concatenate([dual, dual], axis=0)


def finish(parts, g):
    return pl.pallas_call(
        finish_kernel,
        out_shape=jax.ShapeDtypeStruct((136, 128), F32),
        compiler_params=params(),
        name="finish",
    )(parts, g)


TURNS = (0, 1, 3, 2)


def place_kernel(turns, at, *refs):
    mapped, dual = refs[-2:]
    y, z, core = at[0], at[1] // 2, at[1] % 2
    for n, ref in enumerate(refs[:-2]):
        turn, owner = turns[n // 2], core if n % 2 == 0 else 1 - core
        for b in range(4):
            row = jnp.where(owner == 0, y - TURNS[b], y - turn) & 3
            column = jnp.where(owner == 0, z - turn, z - TURNS[b]) & 3
            spot = row * 8 + column * 2 + owner
            for k in range(4):
                where = pl.ds(pl.multiple_of(512 * spot + 128 * k, 128), 128)
                mapped[:, where] = ref[b, 32 * k : 32 * k + 32, :]
            dual[spot] = ref[b, 128:132, :]


def place(at, pieces, turns):
    return pl.pallas_call(
        functools.partial(place_kernel, turns),
        out_shape=(jax.ShapeDtypeStruct((32, 16384), F32), jax.ShapeDtypeStruct((32, 4, 128), F32)),
        grid_spec=pltpu.PrefetchScalarGridSpec(
            num_scalar_prefetch=1,
            grid=(1,),
            in_specs=[at_start(piece.shape) for piece in pieces],
            out_specs=(at_start((32, 16384)), at_start((32, 4, 128))),
        ),
        compiler_params=params(),
        name="place",
    )(at, *pieces)


def turned(block, turn, first):
    pairs = []
    for y in range(4):
        for z in range(4):
            for core in range(2):
                along_y = (core == 0) == first
                to = ((y + turn) % 4, z) if along_y else (y, (z + turn) % 4)
                pairs.append((8 * y + 2 * z + core, 8 * to[0] + 2 * to[1] + core))
    return lax.ppermute(block, ("y", "z", "core"), pairs)


def publish(at, block):
    line = jnp.stack([block] + [turned(block, turn, True) for turn in TURNS[1:]])
    turns = (0, 2, 1, 3)
    pieces = [line] + [turned(line, turn, False) for turn in turns[1:]]
    others = [lax.ppermute(piece, "core", [(0, 1), (1, 0)]) for piece in pieces]
    return place(at, [p for pair in zip(pieces, others) for p in pair], turns)


def spread(copies, axes):
    return lax.all_to_all(copies, axes, 0, 0)


def body(x, y):
    log_a = -math.log2(x.shape[1] * 32)
    log_b = -math.log2(y.shape[1] * 4)
    place = lax.axis_index("y"), lax.axis_index(("z", "core"))
    at = jnp.stack(place).astype(jnp.int32)
    blocks = [x] + [lax.ppermute(x, "y", [(i, (i + k) % 4) for i in range(4)]) for k in (1, 2, 3)]

    first = spread(row_first(x, y, 16), ("tgt", "y"))
    partial, f1 = col_first(at, blocks, first, y, log_b, 8)
    partial = spread(partial, ("z", "core"))
    second, own_g, g1 = row_second(at, blocks, f1, partial, y, log_a, log_b, 16)
    sums, source_dual = col_second(at, blocks, f1, spread(second, ("tgt", "y")), y, g1, log_a)
    mapped, target_dual = publish(at, finish(spread(sums, ("z", "core")), own_g))
    return source_dual.reshape(-1), target_dual.reshape(-1), mapped


def solution(mesh):
    fine = Mesh(mesh.devices.reshape(4, 4, 2, 4), ("y", "z", "core", "tgt"))
    sources = ("y", "z", "core")
    return jax.shard_map(
        body,
        mesh=fine,
        in_specs=(P(None, sources), P(None, "tgt")),
        out_specs=(P(sources), P("tgt"), P(None, "tgt")),
        check_vma=False,
    )
```

time: 849 us -> 157 us (0.18)
  waiting for transfers between devices: 496 us -> 14.7 us
  matrix products: 226 us -> 0 us
  Pallas kernels: 0 us -> 59.7 us
  other arithmetic: 60.8 us -> 1.57 us
  starting transfers between devices: 0.61 us -> 24.6 us
  blocking collectives: 29.7 us -> 53.2 us
  local copies, waits for them, and re-layouts: 19.1 us -> 2.31 us
  between operations: 13.9 us -> 0.73 us
    psum x3 -> x0, waiting for transfers between devices: 298 us -> none  [the longest x2 193 us: col_dual(): whole = lax.psum(totals * jnp.exp(peaks - summit), 'src')]
    dot_general x48 -> x0, matrix products: 226 us -> none  [the longest x40 190 us: cost_tile(): lax.dot_general(src_points, tgt_block, (((0,), (0,)), ((), ())), precisio...]
    pmax x2 -> x0, waiting for transfers between devices: 198 us -> none  [col_dual(): summit = lax.pmax(peaks, 'src')]
    pallas_call x0 -> x6, Pallas kernels: none -> 59.7 us  [the longest x1 19.3 us: col_first(): pl.pallas_call(functools.partial(col_first_kernel, tile, log_b), out_shap...]
    reduce_sum x34 -> x0, other arithmetic: 55.6 us -> none  [the longest x16 45.1 us: row_visit(): jnp.sum(jnp.exp(scores - newest[:, None]), axis=1)]
    all_to_all x0 -> x3, blocking collectives: none -> 53.2 us  [spread(): return lax.all_to_all(copies, axes, 0, 0)]
    ppermute x0 -> x13, starting transfers between devices: none -> 18.8 us  [the longest x4 8.68 us: publish(): others = [lax.ppermute(piece, 'core', [(0, 1), (1, 0)]) for piece in pieces]]
    pmax x2 -> x0, blocking collectives: 17.8 us -> none  [row_dual(): summit = lax.pmax(peak, 'tgt')]
  transfers between devices with their start and end apart: 5 -> 14, of which waited for: 5 -> 7; matrix products, arithmetic and copies ran while one was open for 0% -> 0% of each run, Pallas kernels for 0% -> 6%
where the time goes in v2:
time: 157 us
  Pallas kernels  59.7 us (38%)
  blocking collectives  53.2 us (34%)
  starting transfers between devices  24.6 us (16%)
  waiting for transfers between devices  14.7 us (9%)
  local copies, waits for them, and re-layouts  2.31 us (1%)
  other arithmetic  1.57 us (1%)
    all_to_all x3, blocking collectives, spread(): return lax.all_to_all(copies, axes, 0, 0)  53.2 us
    pallas_call x1, Pallas kernels, col_first(): pl.pallas_call(functools.partial(col_first_kernel, tile, log_b), out_shap...  19.3 us
    pallas_call x1, Pallas kernels, col_second(): pl.pallas_call(functools.partial(col_second_kernel, tile, log_a), out_sha...  16.1 us
    pallas_call x1, Pallas kernels, row_first(): pl.pallas_call(functools.partial(row_first_kernel, tile), out_shape=jax.S...  9.47 us
    pallas_call x1, Pallas kernels, row_second(): pl.pallas_call(functools.partial(row_second_kernel, tile, log_a, log_b),...  9.39 us
    ppermute x4, starting transfers between devices, publish(): others = [lax.ppermute(piece, 'core', [(0, 1), (1, 0)]) for piece in pieces]  8.68 us
    ppermute x6, waiting for transfers between devices, turned(): return lax.ppermute(block, ('y', 'z', 'core'), pairs)  7.38 us
    all_to_all x1, waiting for transfers between devices, spread(): return lax.all_to_all(copies, axes, 0, 0)  5.85 us
  transfers between devices with their start and end apart: 14, of which 7 were waited for; matrix products, arithmetic and copies ran while one was open for 0% of the time, Pallas kernels for 6%

profile of v2, /device:TPU:1, one launch (start us, length us, event | category | flops | bytes accessed | tf_op | source)
XLA Modules:
  0.0 156.8 jit_solution(5818653182803918244)
XLA Ops:
  0.6 3.6 %collective-permute-start.2 = (f32[32,512]{1,0:T(8,128)}, f32[32,512]{1,0:T(8,128)S(1)}, u32[]{:S(2)}, u32[]{:S(2)}) collective-permute-start(f32[32,512]{1,0:T(8,128)} %x0.5), channel_id=1, source_target_pairs={{0,96},{32,0},{64,32},{96,64},{1,97},{33,1},{65,33},{97,65},{2,98}... | collective-permute-start | bytes 196616 | tf_op jit(solution)/shard_map/ppermute | solution.py:505
  4.3 0.3 collective-permute-start.1
  4.6 0.7 collective-permute-start
  5.3 9.5 %row_first.1 = f32[16,8,128]{2,1,0:T(8,128)} custom-call(f32[32,512]{1,0:T(8,128)} %x0.5, f32[32,16384]{1,0:T(8,128)} %y_ref.7), custom_call_target="tpu_custom_call" | custom-call | tf_op jit(solution)/shard_map/row_first/pallas_call | solution.py:158
  14.8 5.8 %all-to-all-start = ((f32[16,8,128]{2,1,0:T(8,128)}), f32[16,8,128]{2,1,0:T(8,128)S(1)}, u32[]{:S(2)}, u32[]{:S(2)}) async-start(f32[16,8,128]{2,1,0:T(8,128)} %row_first.1), calls=%async_computation | async-start | bytes 131072 | tf_op jit(solution)/shard_map/all_to_all | solution.py:497
  20.6 0.7 pad_add_fusion.at
  21.3 5.8 %all-to-all-done.parts = f32[16,8,128]{2,1,0:T(8,128)S(1)} async-done(((f32[16,8,128]{2,1,0:T(8,128)}), f32[16,8,128]{2,1,0:T(8,128)S(1)}, u32[]{:S(2)}, u32[]{:S(2)}) %all-to-all-start) | async-done | bytes 65568 | tf_op jit(solution)/shard_map/all_to_all | solution.py:497
  27.1 0.0 collective-permute-done.2.x3
  27.1 0.0 collective-permute-done.1.x2
  27.1 0.0 copy-start.2
  27.1 0.0 collective-permute-done.x1
  27.2 0.6 copy-done.11
  27.7 0.1 copy-done.1
  27.8 0.0 copy-done.2
  27.8 0.6 copy-done.3
  28.5 19.3 %col_first.1 = (f32[8,64,128]{2,1,0:T(8,128)}, f32[16,128]{1,0:T(8,128)}) custom-call(s32[2]{0:T(128)} %pad_add_fusion.at, f32[32,512]{1,0:T(8,128)} %x0.5, f32[32,512]{1,0:T(8,128)} %copy-done.3, f32[32,512]{1,0:T(8,128)} %copy-done.2, f32[32,512]{1,0:T(8,128)} %copy-done.1, f32[16,8,128]{2,1,0:T(8,128)} %copy-done.11, f32[32,16384]{1,0:T(8,128)} %y_ref.7), custom_call_target="tpu_custom_call" | custom-call | tf_op jit(solution)/shard_map/col_first/pallas_call | solution.py:239
  47.7 25.8 %all_to_all.20.parts = f32[8,64,128]{2,1,0:T(8,128)} all-to-all(f32[8,64,128]{2,1,0:T(8,128)} %get-tuple-element.13), channel_id=1, replica_groups=mesh['y'=4,'z'=4,'core'=2,'tgt'=4] {'z','core'}, dimensions={0} | all-to-all | bytes 524288 | tf_op jit(solution)/shard_map/all_to_all | solution.py:497
  73.5 9.4 %row_second.1 = (f32[16,4,4,128]{3,2,1,0:T(4,128)}, f32[4,128]{1,0:T(4,128)}, f32[32,128]{1,0:T(8,128)}) custom-call(s32[2]{0:T(128)} %pad_add_fusion.at, f32[32,512]{1,0:T(8,128)} %x0.5, f32[32,512]{1,0:T(8,128)} %copy-done.3, f32[32,512]{1,0:T(8,128)} %copy-done.2, f32[32,512]{1,0:T(8,128)} %copy-done.1, f32[16,128]{1,0:T(8,128)} %get-tuple-element.12.f_ref, ...), custom_call_target="tpu_custom_call" | custom-call | tf_op jit(solution)/shard_map/row_second/pallas_call | solution.py:305
  82.9 10.9 %all_to_all.21.parts = f32[16,4,4,128]{3,2,1,0:T(4,128)} all-to-all(f32[16,4,4,128]{3,2,1,0:T(4,128)} %get-tuple-element.14), channel_id=1, replica_groups=mesh['y'=4,'z'=4,'core'=2,'tgt'=4] {'tgt','y'}, dimensions={0} | all-to-all | bytes 262144 | tf_op jit(solution)/shard_map/all_to_all | solution.py:497
  93.8 16.1 %col_second.1 = (f32[8,136,128]{2,1,0:T(8,128)}, f32[4,128]{1,0:T(4,128)}) custom-call(s32[2]{0:T(128)} %pad_add_fusion.at, f32[32,512]{1,0:T(8,128)} %x0.5, f32[32,512]{1,0:T(8,128)} %copy-done.3, f32[32,512]{1,0:T(8,128)} %copy-done.2, f32[32,512]{1,0:T(8,128)} %copy-done.1, f32[16,128]{1,0:T(8,128)} %get-tuple-element.12.f_ref, ...), custom_call_target="tpu_custom_call" | custom-call | tf_op jit(solution)/shard_map/col_second/pallas_call | solution.py:400
  109.9 16.4 %all_to_all.22.parts = f32[8,136,128]{2,1,0:T(8,128)} all-to-all(f32[8,136,128]{2,1,0:T(8,128)} %get-tuple-element.17), channel_id=1, replica_groups=mesh['y'=4,'z'=4,'core'=2,'tgt'=4] {'z','core'}, dimensions={0} | all-to-all | bytes 1114112 | tf_op jit(solution)/shard_map/all_to_all | solution.py:497
  126.3 1.7 %finish.1 = f32[136,128]{1,0:T(8,128)} custom-call(f32[8,136,128]{2,1,0:T(8,128)} %all_to_all.22.parts, f32[4,128]{1,0:T(4,128)} %get-tuple-element.18.g_ref), custom_call_target="tpu_custom_call" | custom-call | tf_op jit(solution)/shard_map/finish/pallas_call | solution.py:436
  128.0 0.6 collective-permute-start.5
  128.7 2.0 %collective-permute-start.4 = (f32[136,128]{1,0:T(8,128)}, f32[136,128]{1,0:T(8,128)S(1)}, u32[]{:S(2)}, u32[]{:S(2)}) collective-permute-start(f32[136,128]{1,0:T(8,128)} %finish.1), channel_id=1, source_target_pairs={{0,96},{4,28},{8,104},{12,4},{16,112},{20,12},{24,120},{28,20},{32... | collective-permute-start | bytes 208904 | tf_op jit(solution)/shard_map/ppermute | solution.py:485
  130.7 0.0 collective-permute-start.3
  130.7 2.2 %collective-permute-done.5 = f32[136,128]{1,0:T(8,128)S(1)} collective-permute-done((f32[136,128]{1,0:T(8,128)}, f32[136,128]{1,0:T(8,128)S(1)}, u32[]{:S(2)}, u32[]{:S(2)}) %collective-permute-start.5) | collective-permute-done | bytes 69664 | tf_op jit(solution)/shard_map/ppermute | solution.py:485
  132.9 0.0 collective-permute-done.4
  132.9 2.4 %collective-permute-done.3 = f32[136,128]{1,0:T(8,128)S(1)} collective-permute-done((f32[136,128]{1,0:T(8,128)}, f32[136,128]{1,0:T(8,128)S(1)}, u32[]{:S(2)}, u32[]{:S(2)}) %collective-permute-start.3) | collective-permute-done | bytes 69664 | tf_op jit(solution)/shard_map/ppermute | solution.py:485
  135.3 0.9 pad_maximum_fusion.refs_0_
  136.2 0.0 copy-start
  136.2 1.3 collective-permute-start.11
  137.6 0.2 collective-permute-start.9
  137.8 1.2 collective-permute-start.7
  139.0 2.6 %collective-permute-start.6 = (f32[4,136,128]{2,1,0:T(8,128)S(1)}, f32[4,136,128]{2,1,0:T(8,128)S(1)}, u32[]{:S(2)}, u32[]{:S(2)}) collective-permute-start(f32[4,136,128]{2,1,0:T(8,128)S(1)} %pad_maximum_fusion.refs_0_), channel_id=1, source_target_pairs={{0,4},{4,0},{1,5},{5,1},{2,6},{6,2},{3,7},{7,3},{8,12},{12,8},{9,1... | collective-permute-start | bytes 835592 | tf_op jit(solution)/shard_map/ppermute | solution.py:492
  141.6 0.4 collective-permute-done.11.refs_6_
  142.0 3.0 %collective-permute-start.12 = (f32[4,136,128]{2,1,0:T(8,128)S(1)}, f32[4,136,128]{2,1,0:T(8,128)S(1)}, u32[]{:S(2)}, u32[]{:S(2)}) collective-permute-start(f32[4,136,128]{2,1,0:T(8,128)S(1)} %collective-permute-done.11.refs_6_), channel_id=1, source_target_pairs={{0,4},{4,0},{1,5},{5,1},{2,6},{6,2},{3,7},{7,3},{8,12},{12,8},{9,1... | collective-permute-start | bytes 835592 | tf_op jit(solution)/shard_map/ppermute | solution.py:492
  145.0 2.4 %collective-permute-done.9.refs_4_ = f32[4,136,128]{2,1,0:T(8,128)S(1)} collective-permute-done((f32[4,136,128]{2,1,0:T(8,128)S(1)}, f32[4,136,128]{2,1,0:T(8,128)S(1)}, u32[]{:S(2)}, u32[]{:S(2)}) %collective-permute-start.9) | collective-permute-done | bytes 278560 | tf_op jit(solution)/shard_map/ppermute | solution.py:485
  147.4 2.9 %collective-permute-start.10 = (f32[4,136,128]{2,1,0:T(8,128)S(1)}, f32[4,136,128]{2,1,0:T(8,128)S(1)}, u32[]{:S(2)}, u32[]{:S(2)}) collective-permute-start(f32[4,136,128]{2,1,0:T(8,128)S(1)} %collective-permute-done.9.refs_4_), channel_id=1, source_target_pairs={{0,4},{4,0},{1,5},{5,1},{2,6},{6,2},{3,7},{7,3},{8,12},{12,8},{9,1... | collective-permute-start | bytes 835592 | tf_op jit(solution)/shard_map/ppermute | solution.py:492
  150.4 0.0 collective-permute-done.7.refs_2_
  150.4 0.1 collective-permute-start.8
  150.5 0.0 collective-permute-done.6.refs_1_
  150.5 0.0 collective-permute-done.12.refs_7_
  150.5 1.1 collective-permute-done.10.refs_5_
  151.6 0.4 collective-permute-done.8.refs_3_
  152.0 0.0 copy-done.6
  152.0 0.3 copy-done.9
  152.3 0.7 copy-done.10
  153.0 3.8 %place.1 = (f32[32,16384]{1,0:T(8,128)}, f32[32,4,128]{2,1,0:T(4,128)}) custom-call(s32[2]{0:T(128)} %pad_add_fusion.at, f32[4,136,128]{2,1,0:T(8,128)} %copy-done, f32[4,136,128]{2,1,0:T(8,128)} %copy-done.7, f32[4,136,128]{2,1,0:T(8,128)} %copy-done.6, f32[4,136,128]{2,1,0:T(8,128)} %copy-done.10, f32[4,136,128]{2,1,0:T(8,128)} %copy-done.5, ...), custom_call_target="tpu_custom_call" | custom-call | tf_op jit(solution)/shard_map/place/pallas_call | solution.py:463
  (15 shorter events, 0.0 us)
Async XLA Ops:
  0.6 26.5 %collective-permute-start.2 = (f32[32,512]{1,0:T(8,128)}, f32[32,512]{1,0:T(8,128)S(1)}, u32[]{:S(2)}, u32[]{:S(2)}) collective-permute-start(f32[32,512]{1,0:T(8,128)} %x0.5), channel_id=1, source_target_pairs={{0,96},{32,0},{64,32},{96,64},{1,97},{33,1},{65,33},{97,65},{2,98}... | collective-permute-start | bytes 196616 | tf_op jit(solution)/shard_map/ppermute | solution.py:505
  4.3 22.9 %collective-permute-start.1 = (f32[32,512]{1,0:T(8,128)}, f32[32,512]{1,0:T(8,128)S(1)}, u32[]{:S(2)}, u32[]{:S(2)}) collective-permute-start(f32[32,512]{1,0:T(8,128)} %x0.5), channel_id=1, source_target_pairs={{0,64},{32,96},{64,0},{96,32},{1,65},{33,97},{65,1},{97,33},{2,66}... | collective-permute-start | bytes 196616 | tf_op jit(solution)/shard_map/ppermute | solution.py:505
  4.6 22.5 %collective-permute-start = (f32[32,512]{1,0:T(8,128)}, f32[32,512]{1,0:T(8,128)S(1)}, u32[]{:S(2)}, u32[]{:S(2)}) collective-permute-start(f32[32,512]{1,0:T(8,128)} %x0.5), channel_id=1, source_target_pairs={{0,32},{32,64},{64,96},{96,0},{1,33},{33,65},{65,97},{97,1},{2,34}... | collective-permute-start | bytes 196616 | tf_op jit(solution)/shard_map/ppermute | solution.py:505
  14.8 12.3 %all-to-all-start = ((f32[16,8,128]{2,1,0:T(8,128)}), f32[16,8,128]{2,1,0:T(8,128)S(1)}, u32[]{:S(2)}, u32[]{:S(2)}) async-start(f32[16,8,128]{2,1,0:T(8,128)} %row_first.1), calls=%async_computation | async-start | bytes 131072 | tf_op jit(solution)/shard_map/all_to_all | solution.py:497
  27.1 0.6 copy-start.11
  27.1 0.7 copy-start.1
  27.1 0.7 copy-start.2
  27.8 0.6 copy-start.3
  128.0 4.9 %collective-permute-start.5 = (f32[136,128]{1,0:T(8,128)}, f32[136,128]{1,0:T(8,128)S(1)}, u32[]{:S(2)}, u32[]{:S(2)}) collective-permute-start(f32[136,128]{1,0:T(8,128)} %finish.1), channel_id=1, source_target_pairs={{0,64},{4,20},{8,72},{12,28},{16,80},{20,4},{24,88},{28,12},{32,96... | collective-permute-start | bytes 208904 | tf_op jit(solution)/shard_map/ppermute | solution.py:485
  128.7 4.2 %collective-permute-start.4 = (f32[136,128]{1,0:T(8,128)}, f32[136,128]{1,0:T(8,128)S(1)}, u32[]{:S(2)}, u32[]{:S(2)}) collective-permute-start(f32[136,128]{1,0:T(8,128)} %finish.1), channel_id=1, source_target_pairs={{0,96},{4,28},{8,104},{12,4},{16,112},{20,12},{24,120},{28,20},{32... | collective-permute-start | bytes 208904 | tf_op jit(solution)/shard_map/ppermute | solution.py:485
  130.7 4.6 %collective-permute-start.3 = (f32[136,128]{1,0:T(8,128)}, f32[136,128]{1,0:T(8,128)S(1)}, u32[]{:S(2)}, u32[]{:S(2)}) collective-permute-start(f32[136,128]{1,0:T(8,128)} %finish.1), channel_id=1, source_target_pairs={{0,32},{4,12},{8,40},{12,20},{16,48},{20,28},{24,56},{28,4},{32,64... | collective-permute-start | bytes 208904 | tf_op jit(solution)/shard_map/ppermute | solution.py:485
  136.2 15.8 %copy-start = (f32[4,136,128]{2,1,0:T(8,128)}, f32[4,136,128]{2,1,0:T(8,128)S(1)}, u32[]{:S(2)}) copy-start(f32[4,136,128]{2,1,0:T(8,128)S(1)} %pad_maximum_fusion.refs_0_) | copy-start | bytes 835588
  136.2 5.8 %collective-permute-start.11 = (f32[4,136,128]{2,1,0:T(8,128)S(1)}, f32[4,136,128]{2,1,0:T(8,128)S(1)}, u32[]{:S(2)}, u32[]{:S(2)}) collective-permute-start(f32[4,136,128]{2,1,0:T(8,128)S(1)} %pad_maximum_fusion.refs_0_), channel_id=1, source_target_pairs={{0,24},{4,100},{8,0},{12,108},{16,8},{20,116},{24,16},{28,124},{32... | collective-permute-start | bytes 835592 | tf_op jit(solution)/shard_map/ppermute | solution.py:485
  137.6 9.9 %collective-permute-start.9 = (f32[4,136,128]{2,1,0:T(8,128)S(1)}, f32[4,136,128]{2,1,0:T(8,128)S(1)}, u32[]{:S(2)}, u32[]{:S(2)}) collective-permute-start(f32[4,136,128]{2,1,0:T(8,128)S(1)} %pad_maximum_fusion.refs_0_), channel_id=1, source_target_pairs={{0,8},{4,36},{8,16},{12,44},{16,24},{20,52},{24,0},{28,60},{32,40}... | collective-permute-start | bytes 835592 | tf_op jit(solution)/shard_map/ppermute | solution.py:485
  137.8 12.6 %collective-permute-start.7 = (f32[4,136,128]{2,1,0:T(8,128)S(1)}, f32[4,136,128]{2,1,0:T(8,128)S(1)}, u32[]{:S(2)}, u32[]{:S(2)}) collective-permute-start(f32[4,136,128]{2,1,0:T(8,128)S(1)} %pad_maximum_fusion.refs_0_), channel_id=1, source_target_pairs={{0,16},{4,68},{8,24},{12,76},{16,0},{20,84},{24,8},{28,92},{32,48}... | collective-permute-start | bytes 835592 | tf_op jit(solution)/shard_map/ppermute | solution.py:485
  139.0 11.5 %collective-permute-start.6 = (f32[4,136,128]{2,1,0:T(8,128)S(1)}, f32[4,136,128]{2,1,0:T(8,128)S(1)}, u32[]{:S(2)}, u32[]{:S(2)}) collective-permute-start(f32[4,136,128]{2,1,0:T(8,128)S(1)} %pad_maximum_fusion.refs_0_), channel_id=1, source_target_pairs={{0,4},{4,0},{1,5},{5,1},{2,6},{6,2},{3,7},{7,3},{8,12},{12,8},{9,1... | collective-permute-start | bytes 835592 | tf_op jit(solution)/shard_map/ppermute | solution.py:492
  142.0 10.0 %copy-start.4 = (f32[4,136,128]{2,1,0:T(8,128)}, f32[4,136,128]{2,1,0:T(8,128)S(1)}, u32[]{:S(2)}) copy-start(f32[4,136,128]{2,1,0:T(8,128)S(1)} %collective-permute-done.11.refs_6_) | copy-start | bytes 835588
  142.0 8.5 %collective-permute-start.12 = (f32[4,136,128]{2,1,0:T(8,128)S(1)}, f32[4,136,128]{2,1,0:T(8,128)S(1)}, u32[]{:S(2)}, u32[]{:S(2)}) collective-permute-start(f32[4,136,128]{2,1,0:T(8,128)S(1)} %collective-permute-done.11.refs_6_), channel_id=1, source_target_pairs={{0,4},{4,0},{1,5},{5,1},{2,6},{6,2},{3,7},{7,3},{8,12},{12,8},{9,1... | collective-permute-start | bytes 835592 | tf_op jit(solution)/shard_map/ppermute | solution.py:492
  147.4 4.5 %copy-start.5 = (f32[4,136,128]{2,1,0:T(8,128)}, f32[4,136,128]{2,1,0:T(8,128)S(1)}, u32[]{:S(2)}) copy-start(f32[4,136,128]{2,1,0:T(8,128)S(1)} %collective-permute-done.9.refs_4_) | copy-start | bytes 835588
  147.4 4.1 %collective-permute-start.10 = (f32[4,136,128]{2,1,0:T(8,128)S(1)}, f32[4,136,128]{2,1,0:T(8,128)S(1)}, u32[]{:S(2)}, u32[]{:S(2)}) collective-permute-start(f32[4,136,128]{2,1,0:T(8,128)S(1)} %collective-permute-done.9.refs_4_), channel_id=1, source_target_pairs={{0,4},{4,0},{1,5},{5,1},{2,6},{6,2},{3,7},{7,3},{8,12},{12,8},{9,1... | collective-permute-start | bytes 835592 | tf_op jit(solution)/shard_map/ppermute | solution.py:492
  150.4 1.6 %copy-start.6 = (f32[4,136,128]{2,1,0:T(8,128)}, f32[4,136,128]{2,1,0:T(8,128)S(1)}, u32[]{:S(2)}) copy-start(f32[4,136,128]{2,1,0:T(8,128)S(1)} %collective-permute-done.7.refs_2_) | copy-start | bytes 835588
  150.4 1.6 %collective-permute-start.8 = (f32[4,136,128]{2,1,0:T(8,128)S(1)}, f32[4,136,128]{2,1,0:T(8,128)S(1)}, u32[]{:S(2)}, u32[]{:S(2)}) collective-permute-start(f32[4,136,128]{2,1,0:T(8,128)S(1)} %collective-permute-done.7.refs_2_), channel_id=1, source_target_pairs={{0,4},{4,0},{1,5},{5,1},{2,6},{6,2},{3,7},{7,3},{8,12},{12,8},{9,1... | collective-permute-start | bytes 835592 | tf_op jit(solution)/shard_map/ppermute | solution.py:492
  150.5 1.5 copy-start.7
  150.5 1.5 copy-start.8
  151.6 0.7 copy-start.9
  152.3 0.7 copy-start.10

commit v3 on v2

--- a/solution.py
+++ b/solution.py
@@ -63,6 +63,11 @@
     out[192:208, :] = jnp.concatenate([ones, t1, t2, t3, ones, zeros], axis=0).astype(BF)
 
 
+def quarter(y_ref, at, t, tile):
+    start = at[0] * (y_ref.shape[1] // 4) + t * tile
+    return y_ref[:, pl.ds(pl.multiple_of(start, tile), tile)]
+
+
 def tree(op, items):
     items = list(items)
     while len(items) > 1:
@@ -93,6 +98,18 @@
         return carry
 
     lax.fori_loop(0, steps // 2, pair, 0)
+
+
+def near(arrays):
+    return [pltpu.with_memory_space_constraint(a, pltpu.VMEM) for a in arrays]
+
+
+def whole(count):
+    return [pl.BlockSpec(memory_space=pltpu.VMEM)] * count
+
+
+def kept(*shapes):
+    return tuple(pltpu.VMEM(shape, F32) for shape in shapes)
 
 
 def row_first_kernel(tile, x_ref, y_ref, out, still, moving, scores, peak, total):
@@ -157,7 +174,9 @@
     tile, count = 1024, x.shape[1]
     return pl.pallas_call(
         functools.partial(row_first_kernel, tile),
-        out_shape=jax.ShapeDtypeStruct((copies, 8, 128), F32),
+        in_specs=whole(2),
+        out_specs=whole(1)[0],
+        out_shape=kept((copies, 8, 128))[0],
         scratch_shapes=[
             pltpu.VMEM((count, DEPTH), BF),
             pltpu.VMEM((2, DEPTH, tile), BF),
@@ -167,7 +186,7 @@
         ],
         compiler_params=params(),
         name="row_first",
-    )(x, y)
+    )(*near([x, y]))
 
 
 def col_first_kernel(tile, log_b, at, x0, x1, x2, x3, parts, y_ref, out, dual_out, still, moving, scores, found):
@@ -185,7 +204,7 @@
     moving[:, 208:DEPTH, :] = jnp.zeros((2, DEPTH - 208, tile), BF)
 
     def make(t, slot):
-        y = y_ref[:, pl.ds(pl.multiple_of(t * tile, tile), tile)]
+        y = quarter(y_ref, at, t, tile)
         build_moving(y, -UNIT * square_norm(y), moving.at[slot])
 
     def multiply(slot):
@@ -200,7 +219,7 @@
             found[pl.ds(half + 2 * t + k // 128, 1), :] = jnp.sum(tree(jnp.add, total), axis=0, keepdims=True)
 
     found[0:half, :] = jnp.zeros((half, 128), F32)
-    steps = y_ref.shape[1] // tile
+    steps = y_ref.shape[1] // 4 // tile
     sweep(steps, make, multiply, process)
 
     @pl.when(jnp.min(found[half:, :]) < 1e-25)
@@ -224,30 +243,25 @@
 
         lax.fori_loop(0, steps, step, 0)
 
-    for s in range(out.shape[0]):
-        out[s] = found[...]
+    out[...] = found[...]
 
 
 def at_start(shape):
     return pl.BlockSpec(shape, lambda i, at: (0,) * len(shape))
 
 
-def col_first(at, blocks, parts, y, log_b, copies):
+def col_first(at, blocks, parts, y, log_b):
     tile, count = 256, blocks[0].shape[1]
     width = y.shape[1] // 4
     lines = width // 64
     return pl.pallas_call(
         functools.partial(col_first_kernel, tile, log_b),
-        out_shape=(
-            jax.ShapeDtypeStruct((copies, lines, 128), F32),
-            jax.ShapeDtypeStruct((16, 128), F32),
-        ),
+        out_shape=kept((lines, 128), (16, 128)),
         grid_spec=pltpu.PrefetchScalarGridSpec(
             num_scalar_prefetch=1,
             grid=(1,),
-            in_specs=[at_start(b.shape) for b in blocks]
-            + [at_start(parts.shape), pl.BlockSpec((32, width), lambda i, at: (0, at[0]))],
-            out_specs=(at_start((copies, lines, 128)), at_start((16, 128))),
+            in_specs=whole(6),
+            out_specs=whole(2),
             scratch_shapes=[
                 pltpu.VMEM((4 * count, DEPTH), BF),
                 pltpu.VMEM((2, DEPTH, tile), BF),
@@ -257,16 +271,18 @@
         ),
         compiler_params=params(),
         name="col_first",
-    )(at, *blocks, parts, y)
+    )(at, *near([*blocks, parts, y]))
 
 
 def row_second_kernel(
-    tile, log_a, log_b, at, x0, x1, x2, x3, f_ref, parts, y_ref, out, own, every, still, moving, scores, total, dual
+    tile, log_a, log_b, at, x0, x1, x2, x3, f_ref, y_ref, p0, p1, p2, p3, p4, p5, p6, p7, *rest
 ):
     count = x0.shape[1]
-    half = parts.shape[1] // 2
-    top = tree(jnp.maximum, [parts[s, 0:half] for s in range(parts.shape[0])])
-    whole = tree(jnp.add, [parts[s, half:] * jnp.exp2(parts[s, 0:half] - top) for s in range(parts.shape[0])])
+    out, own, every, still, moving, scores, total, dual = rest
+    parts = (p0, p1, p2, p3, p4, p5, p6, p7)
+    half = p0.shape[0] // 2
+    top = tree(jnp.maximum, [p[0:half] for p in parts])
+    whole = tree(jnp.add, [p[half:] * jnp.exp2(p[0:half] - top) for p in parts])
     g = -(top + log2(whole) + log_a)
     every[...] = g
     for t in range(half // 2):
@@ -280,7 +296,7 @@
     total[...] = jnp.zeros(total.shape, F32)
 
     def make(t, slot):
-        y = y_ref[:, pl.ds(pl.multiple_of(t * tile, tile), tile)]
+        y = quarter(y_ref, at, t, tile)
         build_moving(y, lanes(dual[t]) + log_b - UNIT * square_norm(y), moving.at[slot])
 
     def multiply(slot):
@@ -291,7 +307,7 @@
             e = [jnp.exp2(scores[slot, r : r + 8, k : k + 128]) for k in range(0, tile, 128)]
             total[r : r + 8, :] += tree(jnp.add, e)
 
-    sweep(y_ref.shape[1] // tile, make, multiply, process)
+    sweep(y_ref.shape[1] // 4 // tile, make, multiply, process)
     for k in range(4):
         line = jnp.sum(total[count * k : count * k + count, :].T, axis=0, keepdims=True)
         row = (at[0] + 4 - k) % 4
@@ -304,17 +320,12 @@
     width = y.shape[1] // 4
     return pl.pallas_call(
         functools.partial(row_second_kernel, tile, log_a, log_b),
-        out_shape=(
-            jax.ShapeDtypeStruct((copies, 4, 4, 128), F32),
-            jax.ShapeDtypeStruct((4, 128), F32),
-            jax.ShapeDtypeStruct((width // 128, 128), F32),
-        ),
+        out_shape=kept((copies, 4, 4, 128), (4, 128), (width // 128, 128)),
         grid_spec=pltpu.PrefetchScalarGridSpec(
             num_scalar_prefetch=1,
             grid=(1,),
-            in_specs=[at_start(b.shape) for b in blocks]
-            + [at_start(f.shape), at_start(parts.shape), pl.BlockSpec((32, width), lambda i, at: (0, at[0]))],
-            out_specs=(at_start((copies, 4, 4, 128)), at_start((4, 128)), at_start((width // 128, 128))),
+            in_specs=whole(6 + len(parts)),
+            out_specs=whole(3),
             scratch_shapes=[
                 pltpu.VMEM((4 * count, DEPTH), BF),
                 pltpu.VMEM((2, DEPTH, tile), BF),
@@ -325,11 +336,11 @@
         ),
         compiler_params=params(),
         name="row_second",
-    )(at, *blocks, f, parts, y)
+    )(at, *near([*blocks, f, y, *parts]))
 
 
 def col_second_kernel(
-    tile, log_a, at, x0, x1, x2, x3, f_ref, parts, y_ref, g_ref, out, own, still, moving, scores, weights, values, dual
+    tile, log_a, at, x0, x1, x2, x3, f_ref, parts, y_ref, g_ref, mine, other, own, still, moving, scores, weights, values, dual, out
 ):
     count = x0.shape[1]
     half = 4 * count
@@ -352,7 +363,7 @@
         dual[t] = g_ref[2 * t : 2 * t + 2, :]
 
     def make(t, slot):
-        y = y_ref[:, pl.ds(pl.multiple_of(t * tile, tile), tile)]
+        y = quarter(y_ref, at, t, tile)
         build_moving(y, lanes(dual[t]) + log_a - UNIT * square_norm(y), moving.at[slot])
 
     def multiply(slot):
@@ -374,7 +385,7 @@
             out[block, 32 * k : 32 * k + 32, :] = moment[:, 128 * h : 128 * h + 128]
             out[block, 128 + k : 129 + k, :] = sums[96:97, 128 * h : 128 * h + 128]
 
-    steps = y_ref.shape[1] // tile
+    steps = y_ref.shape[1] // 4 // tile
     make(0, 0)
     multiply(0)
     make(1, 1)
@@ -392,6 +403,10 @@
 
     lax.fori_loop(0, steps // 2, pair, 0)
     gather(steps // 2 - 1, 1)
+    core = at[1] % 2
+    for z in range(mine.shape[0]):
+        mine[z] = out[2 * z + core]
+        other[z] = out[2 * z + 1 - core]
 
 
 def col_second(at, blocks, f, parts, y, g, log_a):
@@ -399,17 +414,12 @@
     width = y.shape[1] // 4
     return pl.pallas_call(
         functools.partial(col_second_kernel, tile, log_a),
-        out_shape=(
-            jax.ShapeDtypeStruct((width // 512, 136, 128), F32),
-            jax.ShapeDtypeStruct((4, 128), F32),
-        ),
+        out_shape=kept(*((width // 1024, 136, 128),) * 2) + (jax.ShapeDtypeStruct((4, 128), F32),),
         grid_spec=pltpu.PrefetchScalarGridSpec(
             num_scalar_prefetch=1,
             grid=(1,),
-            in_specs=[at_start(b.shape) for b in blocks]
-            + [at_start(f.shape), at_start(parts.shape), pl.BlockSpec((32, width), lambda i, at: (0, at[0]))]
-            + [at_start(g.shape)],
-            out_specs=(at_start((width // 512, 136, 128)), at_start((4, 128))),
+            in_specs=whole(8),
+            out_specs=whole(2) + [at_start((4, 128))],
             scratch_shapes=[
                 pltpu.VMEM((4 * count, DEPTH), BF),
                 pltpu.VMEM((2, DEPTH, tile), BF),
@@ -417,28 +427,52 @@
                 pltpu.VMEM((2, 8 * count, tile), BF),
                 pltpu.VMEM((112, 8 * count), BF),
                 pltpu.VMEM((width // tile, 2, 128), F32),
+                pltpu.VMEM((width // 512, 136, 128), F32),
             ],
         ),
         compiler_params=params(),
         name="col_second",
-    )(at, *blocks, f, parts, y, g)
-
-
-def finish_kernel(parts, g_ref, out):
-    sums = tree(jnp.add, [parts[s] for s in range(parts.shape[0])])
+    )(at, *near([*blocks, f, parts, y, g]))
+
+
+def merge_kernel(at, mine, other, *outs):
+    for k, out in enumerate(outs):
+        z = (at[1] // 2 + k) % 4
+        out[...] = mine[z] + other[z]
+
+
+def merge(at, mine, other):
+    return pl.pallas_call(
+        merge_kernel,
+        out_shape=kept(*((136, 128),) * 4),
+        grid_spec=pltpu.PrefetchScalarGridSpec(
+            num_scalar_prefetch=1,
+            grid=(1,),
+            in_specs=whole(2),
+            out_specs=whole(4),
+        ),
+        compiler_params=params(),
+        name="merge",
+    )(at, *near([mine, other]))
+
+
+def finish_kernel(g_ref, p0, p1, p2, p3, out):
+    sums = (p0[...] + p1[...]) + (p2[...] + p3[...])
     for k in range(4):
         out[32 * k : 32 * k + 32, :] = sums[32 * k : 32 * k + 32] / sums[128 + k : 129 + k]
     dual = (g_ref[...] - log2(sums[128:132])) * (1.0 / UNIT)
     out[128:136, :] = jnp.concatenate([dual, dual], axis=0)
 
 
-def finish(parts, g):
+def finish(g, parts):
     return pl.pallas_call(
         finish_kernel,
-        out_shape=jax.ShapeDtypeStruct((136, 128), F32),
+        in_specs=whole(5),
+        out_specs=whole(1)[0],
+        out_shape=kept((136, 128))[0],
         compiler_params=params(),
         name="finish",
-    )(parts, g)
+    )(*near([g, *parts]))
 
 
 TURNS = (0, 1, 3, 2)
@@ -466,12 +500,12 @@
         grid_spec=pltpu.PrefetchScalarGridSpec(
             num_scalar_prefetch=1,
             grid=(1,),
-            in_specs=[at_start(piece.shape) for piece in pieces],
+            in_specs=whole(len(pieces)),
             out_specs=(at_start((32, 16384)), at_start((32, 4, 128))),
         ),
         compiler_params=params(),
         name="place",
-    )(at, *pieces)
+    )(at, *near(pieces))
 
 
 def turned(block, turn, first):
@@ -497,19 +531,28 @@
     return lax.all_to_all(copies, axes, 0, 0)
 
 
+def along(block, axis, turn):
+    n = lax.axis_size(axis)
+    return lax.ppermute(block, axis, [(i, (i + turn) % n) for i in range(n)])
+
+
 def body(x, y):
     log_a = -math.log2(x.shape[1] * 32)
     log_b = -math.log2(y.shape[1] * 4)
     place = lax.axis_index("y"), lax.axis_index(("z", "core"))
     at = jnp.stack(place).astype(jnp.int32)
-    blocks = [x] + [lax.ppermute(x, "y", [(i, (i + k) % 4) for i in range(4)]) for k in (1, 2, 3)]
-
-    first = spread(row_first(x, y, 16), ("tgt", "y"))
-    partial, f1 = col_first(at, blocks, first, y, log_b, 8)
-    partial = spread(partial, ("z", "core"))
+    first = row_first(x, y, 16)
+    early, _ = lax.optimization_barrier((x, first))
+    blocks = [x] + [along(early, "y", turn) for turn in (1, 2, 3)]
+
+    partial, f1 = col_first(at, blocks, spread(first, ("tgt", "y")), y, log_b)
+    partial = [partial] + [along(partial, "z", turn) for turn in (2, 1, 3)]
+    partial = partial + [along(p, "core", 1) for p in partial]
     second, own_g, g1 = row_second(at, blocks, f1, partial, y, log_a, log_b, 16)
-    sums, source_dual = col_second(at, blocks, f1, spread(second, ("tgt", "y")), y, g1, log_a)
-    mapped, target_dual = publish(at, finish(spread(sums, ("z", "core")), own_g))
+    mine, other, source_dual = col_second(at, blocks, f1, spread(second, ("tgt", "y")), y, g1, log_a)
+    sums = merge(at, mine, along(other, "core", 1))
+    sums = [sums[0]] + [along(sums[turn], "z", turn) for turn in (1, 2, 3)]
+    mapped, target_dual = publish(at, finish(own_g, sums))
     return source_dual.reshape(-1), target_dual.reshape(-1), mapped
 
 

time: 157 us -> 138 us (0.88)
  blocking collectives: 53.2 us -> 11.3 us
  starting transfers between devices: 24.6 us -> 54.9 us
  Pallas kernels: 59.7 us -> 49.8 us
  waiting for transfers between devices: 14.7 us -> 16.9 us
    all_to_all x3 -> x1, blocking collectives: 53.2 us -> 11.3 us  [spread(): return lax.all_to_all(copies, axes, 0, 0)]
    ppermute x3 -> x14, starting transfers between devices: 4.67 us -> 20.1 us  [along(): return lax.ppermute(block, axis, [(i, (i + turn) % n) for i in range(n)])]
    all_to_all x1, starting transfers between devices: 5.82 us -> 18.1 us  [spread(): return lax.all_to_all(copies, axes, 0, 0)]
    ppermute x3 -> x14, waiting for transfers between devices: 0.01 us -> 6.41 us  [along(): return lax.ppermute(block, axis, [(i, (i + turn) % n) for i in range(n)])]
    all_to_all x1, waiting for transfers between devices: 5.85 us -> 2.09 us  [spread(): return lax.all_to_all(copies, axes, 0, 0)]
    pallas_call x2 -> x3, Pallas kernels: 11.2 us -> 8.58 us  [the longest x1 7.85 us: row_first(): pl.pallas_call(functools.partial(row_first_kernel, tile), in_specs=whole(...]
    pallas_call x1, Pallas kernels: 16.1 us -> 14 us  [col_second(): pl.pallas_call(functools.partial(col_second_kernel, tile, log_a), out_sha...]
    pallas_call x1, Pallas kernels: 9.39 us -> 7.45 us  [row_second(): pl.pallas_call(functools.partial(row_second_kernel, tile, log_a, log_b),...]
  transfers between devices with their start and end apart: 14 -> 25, of which waited for: 7 -> 14; matrix products, arithmetic and copies ran while one was open for 0% -> 0% of each run, Pallas kernels for 6% -> 0%
where the time goes in v3:
time: 138 us; the launch traced here: 137 us
  starting transfers between devices  54.9 us (40%)
  Pallas kernels  49.8 us (36%)
  waiting for transfers between devices  16.9 us (12%)
  blocking collectives  11.3 us (8%)
  local copies, waits for them, and re-layouts  2.43 us (2%)
    ppermute x14, starting transfers between devices, along(): return lax.ppermute(block, axis, [(i, (i + turn) % n) for i in range(n)])  20.1 us
    all_to_all x1, starting transfers between devices, spread(): return lax.all_to_all(copies, axes, 0, 0)  18.1 us
    pallas_call x1, Pallas kernels, col_first(): pl.pallas_call(functools.partial(col_first_kernel, tile, log_b), out_shap...  17.4 us
    pallas_call x1, Pallas kernels, col_second(): pl.pallas_call(functools.partial(col_second_kernel, tile, log_a), out_sha...  14 us
    all_to_all x1, blocking collectives, spread(): return lax.all_to_all(copies, axes, 0, 0)  11.3 us
    ppermute x4, starting transfers between devices, publish(): others = [lax.ppermute(piece, 'core', [(0, 1), (1, 0)]) for piece in pieces]  9.91 us
    pallas_call x1, Pallas kernels, row_first(): pl.pallas_call(functools.partial(row_first_kernel, tile), in_specs=whole(...  7.85 us
    pallas_call x1, Pallas kernels, row_second(): pl.pallas_call(functools.partial(row_second_kernel, tile, log_a, log_b),...  7.45 us
  transfers between devices with their start and end apart: 25, of which 14 were waited for; matrix products, arithmetic and copies ran while one was open for 0% of the time, Pallas kernels for 0%

profile of v3, /device:TPU:1, one launch (start us, length us, event | category | flops | bytes accessed | tf_op | source)
XLA Modules:
  0.0 136.7 jit_solution(5204127881063546878)
XLA Ops:
  0.6 1.6 %copy-done = f32[32,16384]{1,0:T(8,128)S(1)} copy-done((f32[32,16384]{1,0:T(8,128)S(1)}, f32[32,16384]{1,0:T(8,128)}, u32[]{:S(2)}) %copy-start) | copy-done | bytes 2097176
  2.2 0.8 copy-done.2
  3.1 7.9 %row_first.1 = f32[16,8,128]{2,1,0:T(8,128)} custom-call(f32[32,512]{1,0:T(8,128)S(1)} %copy-done.2, f32[32,16384]{1,0:T(8,128)S(1)} %copy-done), custom_call_target="tpu_custom_call" | custom-call | tf_op jit(solution)/shard_map/row_first/pallas_call | solution.py:175
  10.9 18.1 %all-to-all-start = ((f32[16,8,128]{2,1,0:T(8,128)}), f32[16,8,128]{2,1,0:T(8,128)S(1)}, u32[]{:S(2)}, u32[]{:S(2)}) async-start(f32[16,8,128]{2,1,0:T(8,128)} %row_first.1), calls=%async_computation | async-start | bytes 131072 | tf_op jit(solution)/shard_map/all_to_all | solution.py:531
  29.0 2.6 %collective-permute-start.2 = (f32[32,512]{1,0:T(8,128)S(1)}, f32[32,512]{1,0:T(8,128)S(1)}, u32[]{:S(2)}, u32[]{:S(2)}) collective-permute-start(f32[32,512]{1,0:T(8,128)S(1)} %copy-done.3), channel_id=1, source_target_pairs={{0,96},{32,0},{64,32},{96,64},{1,97},{33,1},{65,33},{97,65},{2,98}... | collective-permute-start | bytes 196616 | tf_op jit(solution)/shard_map/ppermute | solution.py:536
  31.7 0.6 collective-permute-start.1
  32.2 0.6 collective-permute-start
  32.8 0.6 pad_add_fusion.at
  33.4 2.1 %all-to-all-done.parts = f32[16,8,128]{2,1,0:T(8,128)S(1)} async-done(((f32[16,8,128]{2,1,0:T(8,128)}), f32[16,8,128]{2,1,0:T(8,128)S(1)}, u32[]{:S(2)}, u32[]{:S(2)}) %all-to-all-start) | async-done | bytes 65568 | tf_op jit(solution)/shard_map/all_to_all | solution.py:531
  35.5 0.8 collective-permute-done.1.x2
  36.4 0.7 collective-permute-done.x1
  37.0 17.4 %col_first.1 = (f32[64,128]{1,0:T(8,128)S(1)}, f32[16,128]{1,0:T(8,128)S(1)}) custom-call(s32[2]{0:T(128)} %pad_add_fusion.at, f32[32,512]{1,0:T(8,128)S(1)} %copy-done.3, f32[32,512]{1,0:T(8,128)S(1)} %collective-permute-done.x1, f32[32,512]{1,0:T(8,128)S(1)} %collective-permute-done.1.x2, f32[32,512]{1,0:T(8,128)S(1)} %collective-permute-done.2.x3, ...), custom_call_target="tpu_custom_call" | custom-call | tf_op jit(solution)/shard_map/col_first/pallas_call | solution.py:257
  54.5 0.1 collective-permute-start.5
  54.6 1.5 %collective-permute-start.4 = (f32[64,128]{1,0:T(8,128)S(1)}, f32[64,128]{1,0:T(8,128)S(1)}, u32[]{:S(2)}, u32[]{:S(2)}) collective-permute-start(f32[64,128]{1,0:T(8,128)S(1)} %get-tuple-element.20.p0), channel_id=1, source_target_pairs={{0,8},{8,16},{16,24},{24,0},{1,9},{9,17},{17,25},{25,1},{2,10},{10... | collective-permute-start | bytes 98312 | tf_op jit(solution)/shard_map/ppermute | solution.py:536
  56.0 5.3 %collective-permute-start.6 = (f32[64,128]{1,0:T(8,128)S(1)}, f32[64,128]{1,0:T(8,128)S(1)}, u32[]{:S(2)}, u32[]{:S(2)}) collective-permute-start(f32[64,128]{1,0:T(8,128)S(1)} %get-tuple-element.20.p0), channel_id=1, source_target_pairs={{0,4},{4,0},{1,5},{5,1},{2,6},{6,2},{3,7},{7,3},{8,12},{12,8},{9,1... | collective-permute-start | bytes 98312 | tf_op jit(solution)/shard_map/ppermute | solution.py:536
  61.3 0.0 collective-permute-done.5.p3
  61.3 0.0 collective-permute-start.9
  61.4 1.8 %collective-permute-start.8 = (f32[64,128]{1,0:T(8,128)S(1)}, f32[64,128]{1,0:T(8,128)S(1)}, u32[]{:S(2)}, u32[]{:S(2)}) collective-permute-start(f32[64,128]{1,0:T(8,128)S(1)} %collective-permute-done.4.p2), channel_id=1, source_target_pairs={{0,4},{4,0},{1,5},{5,1},{2,6},{6,2},{3,7},{7,3},{8,12},{12,8},{9,1... | collective-permute-start | bytes 98312 | tf_op jit(solution)/shard_map/ppermute | solution.py:536
  63.1 1.6 %collective-permute-start.7 = (f32[64,128]{1,0:T(8,128)S(1)}, f32[64,128]{1,0:T(8,128)S(1)}, u32[]{:S(2)}, u32[]{:S(2)}) collective-permute-start(f32[64,128]{1,0:T(8,128)S(1)} %collective-permute-done.3.p1), channel_id=1, source_target_pairs={{0,4},{4,0},{1,5},{5,1},{2,6},{6,2},{3,7},{7,3},{8,12},{12,8},{9,1... | collective-permute-start | bytes 98312 | tf_op jit(solution)/shard_map/ppermute | solution.py:536
  64.8 0.8 collective-permute-done.7.p5
  65.6 7.4 %row_second.1 = (f32[16,4,4,128]{3,2,1,0:T(4,128)S(1)}, f32[4,128]{1,0:T(4,128)S(1)}, f32[32,128]{1,0:T(8,128)S(1)}) custom-call(s32[2]{0:T(128)} %pad_add_fusion.at, f32[32,512]{1,0:T(8,128)S(1)} %copy-done.3, f32[32,512]{1,0:T(8,128)S(1)} %collective-permute-done.x1, f32[32,512]{1,0:T(8,128)S(1)} %collective-permute-done.1.x2, ...), custom_call_target="tpu_custom_call" | custom-call | tf_op jit(solution)/shard_map/row_second/pallas_call | solution.py:321
  73.1 11.3 %all_to_all.10.parts = f32[16,4,4,128]{3,2,1,0:T(4,128)S(1)} all-to-all(f32[16,4,4,128]{3,2,1,0:T(4,128)S(1)} %get-tuple-element.21), channel_id=1, replica_groups=mesh['y'=4,'z'=4,'core'=2,'tgt'=4] {'tgt','y'}, dimensions={0} | all-to-all | bytes 262144 | tf_op jit(solution)/shard_map/all_to_all | solution.py:531
  84.4 14.0 %col_second.1 = (f32[4,136,128]{2,1,0:T(8,128)S(1)}, f32[4,136,128]{2,1,0:T(8,128)S(1)}, f32[4,128]{1,0:T(4,128)}) custom-call(s32[2]{0:T(128)} %pad_add_fusion.at, f32[32,512]{1,0:T(8,128)S(1)} %copy-done.3, f32[32,512]{1,0:T(8,128)S(1)} %collective-permute-done.x1, f32[32,512]{1,0:T(8,128)S(1)} %collective-permute-done.1.x2, ...), custom_call_target="tpu_custom_call" | custom-call | tf_op jit(solution)/shard_map/col_second/pallas_call | solution.py:415
  98.4 1.9 %collective-permute-start.10 = (f32[4,136,128]{2,1,0:T(8,128)S(1)}, f32[4,136,128]{2,1,0:T(8,128)S(1)}, u32[]{:S(2)}, u32[]{:S(2)}) collective-permute-start(f32[4,136,128]{2,1,0:T(8,128)S(1)} %get-tuple-element.26), channel_id=1, source_target_pairs={{0,4},{4,0},{1,5},{5,1},{2,6},{6,2},{3,7},{7,3},{8,12},{12,8},{9,1... | collective-permute-start | bytes 835592 | tf_op jit(solution)/shard_map/ppermute | solution.py:536
  100.3 1.2 collective-permute-done.10.other
  101.5 0.7 merge.1
  102.2 1.7 %collective-permute-start.11 = (f32[136,128]{1,0:T(8,128)S(1)}, f32[136,128]{1,0:T(8,128)S(1)}, u32[]{:S(2)}, u32[]{:S(2)}) collective-permute-start(f32[136,128]{1,0:T(8,128)S(1)} %get-tuple-element.28), channel_id=1, source_target_pairs={{0,8},{8,16},{16,24},{24,0},{1,9},{9,17},{17,25},{25,1},{2,10},{10... | collective-permute-start | bytes 208904 | tf_op jit(solution)/shard_map/ppermute | solution.py:536
  103.9 1.2 collective-permute-start.12
  105.1 1.3 collective-permute-start.13
  106.4 0.2 collective-permute-done.11.p1
  106.6 2.0 %collective-permute-done.12.p2 = f32[136,128]{1,0:T(8,128)S(1)} collective-permute-done((f32[136,128]{1,0:T(8,128)S(1)}, f32[136,128]{1,0:T(8,128)S(1)}, u32[]{:S(2)}, u32[]{:S(2)}) %collective-permute-start.12) | collective-permute-done | bytes 69664 | tf_op jit(solution)/shard_map/ppermute | solution.py:536
  108.6 0.7 collective-permute-done.13.p3
  109.3 1.8 %collective-permute-start.16 = (f32[136,128]{1,0:T(8,128)S(1)}, f32[136,128]{1,0:T(8,128)S(1)}, u32[]{:S(2)}, u32[]{:S(2)}) collective-permute-start(f32[136,128]{1,0:T(8,128)S(1)} %finish.1), channel_id=1, source_target_pairs={{0,64},{4,20},{8,72},{12,28},{16,80},{20,4},{24,88},{28,12},{32,96... | collective-permute-start | bytes 208904 | tf_op jit(solution)/shard_map/ppermute | solution.py:519
  111.1 2.1 %collective-permute-start.15 = (f32[136,128]{1,0:T(8,128)S(1)}, f32[136,128]{1,0:T(8,128)S(1)}, u32[]{:S(2)}, u32[]{:S(2)}) collective-permute-start(f32[136,128]{1,0:T(8,128)S(1)} %finish.1), channel_id=1, source_target_pairs={{0,96},{4,28},{8,104},{12,4},{16,112},{20,12},{24,120},{28,20},{32... | collective-permute-start | bytes 208904 | tf_op jit(solution)/shard_map/ppermute | solution.py:519
  113.3 0.8 collective-permute-done.16
  114.0 1.3 collective-permute-done.15
  115.4 2.3 %collective-permute-done.14 = f32[136,128]{1,0:T(8,128)S(1)} collective-permute-done((f32[136,128]{1,0:T(8,128)S(1)}, f32[136,128]{1,0:T(8,128)S(1)}, u32[]{:S(2)}, u32[]{:S(2)}) %collective-permute-start.14) | collective-permute-done | bytes 69664 | tf_op jit(solution)/shard_map/ppermute | solution.py:519
  117.7 1.0 collective-permute-start.22
  118.7 0.5 collective-permute-start.20
  119.2 1.2 collective-permute-start.18
  120.5 3.2 %collective-permute-start.17 = (f32[4,136,128]{2,1,0:T(8,128)S(1)}, f32[4,136,128]{2,1,0:T(8,128)S(1)}, u32[]{:S(2)}, u32[]{:S(2)}) collective-permute-start(f32[4,136,128]{2,1,0:T(8,128)S(1)} %pad_maximum_fusion.refs_0_), channel_id=1, source_target_pairs={{0,4},{4,0},{1,5},{5,1},{2,6},{6,2},{3,7},{7,3},{8,12},{12,8},{9,1... | collective-permute-start | bytes 835592 | tf_op jit(solution)/shard_map/ppermute | solution.py:526
  123.6 2.5 %collective-permute-start.23 = (f32[4,136,128]{2,1,0:T(8,128)S(1)}, f32[4,136,128]{2,1,0:T(8,128)S(1)}, u32[]{:S(2)}, u32[]{:S(2)}) collective-permute-start(f32[4,136,128]{2,1,0:T(8,128)S(1)} %collective-permute-done.22.refs_6_), channel_id=1, source_target_pairs={{0,4},{4,0},{1,5},{5,1},{2,6},{6,2},{3,7},{7,3},{8,12},{12,8},{9,1... | collective-permute-start | bytes 835592 | tf_op jit(solution)/shard_map/ppermute | solution.py:526
  126.2 2.5 %collective-permute-done.20.refs_4_ = f32[4,136,128]{2,1,0:T(8,128)S(1)} collective-permute-done((f32[4,136,128]{2,1,0:T(8,128)S(1)}, f32[4,136,128]{2,1,0:T(8,128)S(1)}, u32[]{:S(2)}, u32[]{:S(2)}) %collective-permute-start.20) | collective-permute-done | bytes 278560 | tf_op jit(solution)/shard_map/ppermute | solution.py:519
  128.6 4.2 %collective-permute-start.21 = (f32[4,136,128]{2,1,0:T(8,128)S(1)}, f32[4,136,128]{2,1,0:T(8,128)S(1)}, u32[]{:S(2)}, u32[]{:S(2)}) collective-permute-start(f32[4,136,128]{2,1,0:T(8,128)S(1)} %collective-permute-done.20.refs_4_), channel_id=1, source_target_pairs={{0,4},{4,0},{1,5},{5,1},{2,6},{6,2},{3,7},{7,3},{8,12},{12,8},{9,1... | collective-permute-start | bytes 835592 | tf_op jit(solution)/shard_map/ppermute | solution.py:526
  132.8 0.0 collective-permute-start.19
  132.8 1.2 collective-permute-done.21.refs_5_
  134.0 0.4 collective-permute-done.19.refs_3_
  134.4 2.3 %place.1 = (f32[32,16384]{1,0:T(8,128)}, f32[32,4,128]{2,1,0:T(4,128)}) custom-call(s32[2]{0:T(128)} %pad_add_fusion.at, f32[4,136,128]{2,1,0:T(8,128)S(1)} %pad_maximum_fusion.refs_0_, f32[4,136,128]{2,1,0:T(8,128)S(1)} %collective-permute-done.17.refs_1_, f32[4,136,128]{2,1,0:T(8,128)S(1)} %collective-permute-done.18.refs_2_, ...), custom_call_target="tpu_custom_call" | custom-call | tf_op jit(solution)/shard_map/place/pallas_call | solution.py:497
  (20 shorter events, 0.1 us)
Async XLA Ops:
  0.6 1.6 %copy-start = (f32[32,16384]{1,0:T(8,128)S(1)}, f32[32,16384]{1,0:T(8,128)}, u32[]{:S(2)}) copy-start(f32[32,16384]{1,0:T(8,128)} %y_ref.7) | copy-start | bytes 6291460
  2.2 0.8 copy-start.2
  3.1 25.9 %copy-start.3 = (f32[32,512]{1,0:T(8,128)S(1)}, f32[32,512]{1,0:T(8,128)}, u32[]{:S(2)}) copy-start(f32[32,512]{1,0:T(8,128)} %x0.5) | copy-start | bytes 196612
  3.1 34.0 %copy-start.1 = (f32[32,16384]{1,0:T(8,128)S(1)}, f32[32,16384]{1,0:T(8,128)}, u32[]{:S(2)}) copy-start(f32[32,16384]{1,0:T(8,128)} %y_ref.7) | copy-start | bytes 6291460
  10.9 24.6 %all-to-all-start = ((f32[16,8,128]{2,1,0:T(8,128)}), f32[16,8,128]{2,1,0:T(8,128)S(1)}, u32[]{:S(2)}, u32[]{:S(2)}) async-start(f32[16,8,128]{2,1,0:T(8,128)} %row_first.1), calls=%async_computation | async-start | bytes 131072 | tf_op jit(solution)/shard_map/all_to_all | solution.py:531
  29.0 6.5 %collective-permute-start.2 = (f32[32,512]{1,0:T(8,128)S(1)}, f32[32,512]{1,0:T(8,128)S(1)}, u32[]{:S(2)}, u32[]{:S(2)}) collective-permute-start(f32[32,512]{1,0:T(8,128)S(1)} %copy-done.3), channel_id=1, source_target_pairs={{0,96},{32,0},{64,32},{96,64},{1,97},{33,1},{65,33},{97,65},{2,98}... | collective-permute-start | bytes 196616 | tf_op jit(solution)/shard_map/ppermute | solution.py:536
  31.7 4.7 %collective-permute-start.1 = (f32[32,512]{1,0:T(8,128)S(1)}, f32[32,512]{1,0:T(8,128)S(1)}, u32[]{:S(2)}, u32[]{:S(2)}) collective-permute-start(f32[32,512]{1,0:T(8,128)S(1)} %copy-done.3), channel_id=1, source_target_pairs={{0,64},{32,96},{64,0},{96,32},{1,65},{33,97},{65,1},{97,33},{2,66}... | collective-permute-start | bytes 196616 | tf_op jit(solution)/shard_map/ppermute | solution.py:536
  32.2 4.8 %collective-permute-start = (f32[32,512]{1,0:T(8,128)S(1)}, f32[32,512]{1,0:T(8,128)S(1)}, u32[]{:S(2)}, u32[]{:S(2)}) collective-permute-start(f32[32,512]{1,0:T(8,128)S(1)} %copy-done.3), channel_id=1, source_target_pairs={{0,32},{32,64},{64,96},{96,0},{1,33},{33,65},{65,97},{97,1},{2,34}... | collective-permute-start | bytes 196616 | tf_op jit(solution)/shard_map/ppermute | solution.py:536
  54.5 6.9 %collective-permute-start.5 = (f32[64,128]{1,0:T(8,128)S(1)}, f32[64,128]{1,0:T(8,128)S(1)}, u32[]{:S(2)}, u32[]{:S(2)}) collective-permute-start(f32[64,128]{1,0:T(8,128)S(1)} %get-tuple-element.20.p0), channel_id=1, source_target_pairs={{0,24},{8,0},{16,8},{24,16},{1,25},{9,1},{17,9},{25,17},{2,26},{10... | collective-permute-start | bytes 98312 | tf_op jit(solution)/shard_map/ppermute | solution.py:536
  54.6 6.8 %collective-permute-start.4 = (f32[64,128]{1,0:T(8,128)S(1)}, f32[64,128]{1,0:T(8,128)S(1)}, u32[]{:S(2)}, u32[]{:S(2)}) collective-permute-start(f32[64,128]{1,0:T(8,128)S(1)} %get-tuple-element.20.p0), channel_id=1, source_target_pairs={{0,8},{8,16},{16,24},{24,0},{1,9},{9,17},{17,25},{25,1},{2,10},{10... | collective-permute-start | bytes 98312 | tf_op jit(solution)/shard_map/ppermute | solution.py:536
  56.0 7.1 %collective-permute-start.3 = (f32[64,128]{1,0:T(8,128)S(1)}, f32[64,128]{1,0:T(8,128)S(1)}, u32[]{:S(2)}, u32[]{:S(2)}) collective-permute-start(f32[64,128]{1,0:T(8,128)S(1)} %get-tuple-element.20.p0), channel_id=1, source_target_pairs={{0,16},{8,24},{16,0},{24,8},{1,17},{9,25},{17,1},{25,9},{2,18},{10... | collective-permute-start | bytes 98312 | tf_op jit(solution)/shard_map/ppermute | solution.py:536
  56.0 8.8 %collective-permute-start.6 = (f32[64,128]{1,0:T(8,128)S(1)}, f32[64,128]{1,0:T(8,128)S(1)}, u32[]{:S(2)}, u32[]{:S(2)}) collective-permute-start(f32[64,128]{1,0:T(8,128)S(1)} %get-tuple-element.20.p0), channel_id=1, source_target_pairs={{0,4},{4,0},{1,5},{5,1},{2,6},{6,2},{3,7},{7,3},{8,12},{12,8},{9,1... | collective-permute-start | bytes 98312 | tf_op jit(solution)/shard_map/ppermute | solution.py:536
  61.3 3.4 %collective-permute-start.9 = (f32[64,128]{1,0:T(8,128)S(1)}, f32[64,128]{1,0:T(8,128)S(1)}, u32[]{:S(2)}, u32[]{:S(2)}) collective-permute-start(f32[64,128]{1,0:T(8,128)S(1)} %collective-permute-done.5.p3), channel_id=1, source_target_pairs={{0,4},{4,0},{1,5},{5,1},{2,6},{6,2},{3,7},{7,3},{8,12},{12,8},{9,1... | collective-permute-start | bytes 98312 | tf_op jit(solution)/shard_map/ppermute | solution.py:536
  61.4 3.4 %collective-permute-start.8 = (f32[64,128]{1,0:T(8,128)S(1)}, f32[64,128]{1,0:T(8,128)S(1)}, u32[]{:S(2)}, u32[]{:S(2)}) collective-permute-start(f32[64,128]{1,0:T(8,128)S(1)} %collective-permute-done.4.p2), channel_id=1, source_target_pairs={{0,4},{4,0},{1,5},{5,1},{2,6},{6,2},{3,7},{7,3},{8,12},{12,8},{9,1... | collective-permute-start | bytes 98312 | tf_op jit(solution)/shard_map/ppermute | solution.py:536
  63.1 2.5 %collective-permute-start.7 = (f32[64,128]{1,0:T(8,128)S(1)}, f32[64,128]{1,0:T(8,128)S(1)}, u32[]{:S(2)}, u32[]{:S(2)}) collective-permute-start(f32[64,128]{1,0:T(8,128)S(1)} %collective-permute-done.3.p1), channel_id=1, source_target_pairs={{0,4},{4,0},{1,5},{5,1},{2,6},{6,2},{3,7},{7,3},{8,12},{12,8},{9,1... | collective-permute-start | bytes 98312 | tf_op jit(solution)/shard_map/ppermute | solution.py:536
  98.4 3.0 %collective-permute-start.10 = (f32[4,136,128]{2,1,0:T(8,128)S(1)}, f32[4,136,128]{2,1,0:T(8,128)S(1)}, u32[]{:S(2)}, u32[]{:S(2)}) collective-permute-start(f32[4,136,128]{2,1,0:T(8,128)S(1)} %get-tuple-element.26), channel_id=1, source_target_pairs={{0,4},{4,0},{1,5},{5,1},{2,6},{6,2},{3,7},{7,3},{8,12},{12,8},{9,1... | collective-permute-start | bytes 835592 | tf_op jit(solution)/shard_map/ppermute | solution.py:536
  102.2 4.4 %collective-permute-start.11 = (f32[136,128]{1,0:T(8,128)S(1)}, f32[136,128]{1,0:T(8,128)S(1)}, u32[]{:S(2)}, u32[]{:S(2)}) collective-permute-start(f32[136,128]{1,0:T(8,128)S(1)} %get-tuple-element.28), channel_id=1, source_target_pairs={{0,8},{8,16},{16,24},{24,0},{1,9},{9,17},{17,25},{25,1},{2,10},{10... | collective-permute-start | bytes 208904 | tf_op jit(solution)/shard_map/ppermute | solution.py:536
  103.9 4.7 %collective-permute-start.12 = (f32[136,128]{1,0:T(8,128)S(1)}, f32[136,128]{1,0:T(8,128)S(1)}, u32[]{:S(2)}, u32[]{:S(2)}) collective-permute-start(f32[136,128]{1,0:T(8,128)S(1)} %get-tuple-element.29), channel_id=1, source_target_pairs={{0,16},{8,24},{16,0},{24,8},{1,17},{9,25},{17,1},{25,9},{2,18},{10... | collective-permute-start | bytes 208904 | tf_op jit(solution)/shard_map/ppermute | solution.py:536
  105.1 4.2 %collective-permute-start.13 = (f32[136,128]{1,0:T(8,128)S(1)}, f32[136,128]{1,0:T(8,128)S(1)}, u32[]{:S(2)}, u32[]{:S(2)}) collective-permute-start(f32[136,128]{1,0:T(8,128)S(1)} %get-tuple-element.30), channel_id=1, source_target_pairs={{0,24},{8,0},{16,8},{24,16},{1,25},{9,1},{17,9},{25,17},{2,26},{10... | collective-permute-start | bytes 208904 | tf_op jit(solution)/shard_map/ppermute | solution.py:536
  109.3 4.7 %collective-permute-start.16 = (f32[136,128]{1,0:T(8,128)S(1)}, f32[136,128]{1,0:T(8,128)S(1)}, u32[]{:S(2)}, u32[]{:S(2)}) collective-permute-start(f32[136,128]{1,0:T(8,128)S(1)} %finish.1), channel_id=1, source_target_pairs={{0,64},{4,20},{8,72},{12,28},{16,80},{20,4},{24,88},{28,12},{32,96... | collective-permute-start | bytes 208904 | tf_op jit(solution)/shard_map/ppermute | solution.py:519
  111.1 4.2 %collective-permute-start.15 = (f32[136,128]{1,0:T(8,128)S(1)}, f32[136,128]{1,0:T(8,128)S(1)}, u32[]{:S(2)}, u32[]{:S(2)}) collective-permute-start(f32[136,128]{1,0:T(8,128)S(1)} %finish.1), channel_id=1, source_target_pairs={{0,96},{4,28},{8,104},{12,4},{16,112},{20,12},{24,120},{28,20},{32... | collective-permute-start | bytes 208904 | tf_op jit(solution)/shard_map/ppermute | solution.py:519
  113.3 4.4 %collective-permute-start.14 = (f32[136,128]{1,0:T(8,128)S(1)}, f32[136,128]{1,0:T(8,128)S(1)}, u32[]{:S(2)}, u32[]{:S(2)}) collective-permute-start(f32[136,128]{1,0:T(8,128)S(1)} %finish.1), channel_id=1, source_target_pairs={{0,32},{4,12},{8,40},{12,20},{16,48},{20,28},{24,56},{28,4},{32,64... | collective-permute-start | bytes 208904 | tf_op jit(solution)/shard_map/ppermute | solution.py:519
  117.7 6.0 %collective-permute-start.22 = (f32[4,136,128]{2,1,0:T(8,128)S(1)}, f32[4,136,128]{2,1,0:T(8,128)S(1)}, u32[]{:S(2)}, u32[]{:S(2)}) collective-permute-start(f32[4,136,128]{2,1,0:T(8,128)S(1)} %pad_maximum_fusion.refs_0_), channel_id=1, source_target_pairs={{0,24},{4,100},{8,0},{12,108},{16,8},{20,116},{24,16},{28,124},{32... | collective-permute-start | bytes 835592 | tf_op jit(solution)/shard_map/ppermute | solution.py:519
  118.7 9.9 %collective-permute-start.20 = (f32[4,136,128]{2,1,0:T(8,128)S(1)}, f32[4,136,128]{2,1,0:T(8,128)S(1)}, u32[]{:S(2)}, u32[]{:S(2)}) collective-permute-start(f32[4,136,128]{2,1,0:T(8,128)S(1)} %pad_maximum_fusion.refs_0_), channel_id=1, source_target_pairs={{0,8},{4,36},{8,16},{12,44},{16,24},{20,52},{24,0},{28,60},{32,40}... | collective-permute-start | bytes 835592 | tf_op jit(solution)/shard_map/ppermute | solution.py:519
  119.2 13.6 %collective-permute-start.18 = (f32[4,136,128]{2,1,0:T(8,128)S(1)}, f32[4,136,128]{2,1,0:T(8,128)S(1)}, u32[]{:S(2)}, u32[]{:S(2)}) collective-permute-start(f32[4,136,128]{2,1,0:T(8,128)S(1)} %pad_maximum_fusion.refs_0_), channel_id=1, source_target_pairs={{0,16},{4,68},{8,24},{12,76},{16,0},{20,84},{24,8},{28,92},{32,48}... | collective-permute-start | bytes 835592 | tf_op jit(solution)/shard_map/ppermute | solution.py:519
  120.5 12.4 %collective-permute-start.17 = (f32[4,136,128]{2,1,0:T(8,128)S(1)}, f32[4,136,128]{2,1,0:T(8,128)S(1)}, u32[]{:S(2)}, u32[]{:S(2)}) collective-permute-start(f32[4,136,128]{2,1,0:T(8,128)S(1)} %pad_maximum_fusion.refs_0_), channel_id=1, source_target_pairs={{0,4},{4,0},{1,5},{5,1},{2,6},{6,2},{3,7},{7,3},{8,12},{12,8},{9,1... | collective-permute-start | bytes 835592 | tf_op jit(solution)/shard_map/ppermute | solution.py:526
  123.6 9.2 %collective-permute-start.23 = (f32[4,136,128]{2,1,0:T(8,128)S(1)}, f32[4,136,128]{2,1,0:T(8,128)S(1)}, u32[]{:S(2)}, u32[]{:S(2)}) collective-permute-start(f32[4,136,128]{2,1,0:T(8,128)S(1)} %collective-permute-done.22.refs_6_), channel_id=1, source_target_pairs={{0,4},{4,0},{1,5},{5,1},{2,6},{6,2},{3,7},{7,3},{8,12},{12,8},{9,1... | collective-permute-start | bytes 835592 | tf_op jit(solution)/shard_map/ppermute | solution.py:526
  128.6 5.4 %collective-permute-start.21 = (f32[4,136,128]{2,1,0:T(8,128)S(1)}, f32[4,136,128]{2,1,0:T(8,128)S(1)}, u32[]{:S(2)}, u32[]{:S(2)}) collective-permute-start(f32[4,136,128]{2,1,0:T(8,128)S(1)} %collective-permute-done.20.refs_4_), channel_id=1, source_target_pairs={{0,4},{4,0},{1,5},{5,1},{2,6},{6,2},{3,7},{7,3},{8,12},{12,8},{9,1... | collective-permute-start | bytes 835592 | tf_op jit(solution)/shard_map/ppermute | solution.py:526
  132.8 1.6 %collective-permute-start.19 = (f32[4,136,128]{2,1,0:T(8,128)S(1)}, f32[4,136,128]{2,1,0:T(8,128)S(1)}, u32[]{:S(2)}, u32[]{:S(2)}) collective-permute-start(f32[4,136,128]{2,1,0:T(8,128)S(1)} %collective-permute-done.18.refs_2_), channel_id=1, source_target_pairs={{0,4},{4,0},{1,5},{5,1},{2,6},{6,2},{3,7},{7,3},{8,12},{12,8},{9,1... | collective-permute-start | bytes 835592 | tf_op jit(solution)/shard_map/ppermute | solution.py:526

commit v4 on v3

--- a/solution.py
+++ b/solution.py
@@ -63,8 +63,8 @@
     out[192:208, :] = jnp.concatenate([ones, t1, t2, t3, ones, zeros], axis=0).astype(BF)
 
 
-def quarter(y_ref, at, t, tile):
-    start = at[0] * (y_ref.shape[1] // 4) + t * tile
+def quarter(y_ref, t, tile):
+    start = lax.axis_index("y") * (y_ref.shape[1] // 4) + t * tile
     return y_ref[:, pl.ds(pl.multiple_of(start, tile), tile)]
 
 
@@ -112,9 +112,17 @@
     return tuple(pltpu.VMEM(shape, F32) for shape in shapes)
 
 
-def row_first_kernel(tile, x_ref, y_ref, out, still, moving, scores, peak, total):
+def row_first_kernel(tile, x_far, y_far, out, y_ref, x_ref, still, moving, scores, peak, total, sem):
     count = x_ref.shape[1]
     steps = y_ref.shape[1] // tile
+    ahead = 2 * tile
+    get_x = pltpu.make_async_copy(x_far, x_ref, sem.at[0])
+    get_first = pltpu.make_async_copy(y_far.at[:, 0:ahead], y_ref.at[:, 0:ahead], sem.at[1])
+    get_rest = pltpu.make_async_copy(y_far.at[:, ahead:], y_ref.at[:, ahead:], sem.at[2])
+    get_x.start()
+    get_first.start()
+    get_rest.start()
+    get_x.wait()
     x = x_ref[...]
     norm = -UNIT * square_norm(x)
     build_still(x, norm, still)
@@ -129,6 +137,7 @@
     def multiply(slot):
         scores[slot] = jnp.dot(still[...], moving[slot], preferred_element_type=F32)
 
+    get_first.wait()
     make(0, 0)
     sample = jnp.dot(still[...], moving[0, :, 0:256], preferred_element_type=F32)
     base = jnp.max(jnp.maximum(sample[:, 0:128], sample[:, 128:256]).T, axis=0, keepdims=True)
@@ -141,6 +150,7 @@
             e = [jnp.exp2(scores[slot, r : r + 8, k : k + 128]) for k in range(0, tile, 128)]
             total[r : r + 8, :] += tree(jnp.add, e)
 
+    get_rest.wait()
     sweep(steps, make, multiply, process)
 
     @pl.when(jnp.max(total[...]) > 1e34)
@@ -166,45 +176,51 @@
     top = jnp.max(peaks, axis=0, keepdims=True)
     whole = jnp.sum(total[...].T * jnp.exp2(peaks - top), axis=0, keepdims=True)
     pair = jnp.concatenate([rows(top + base), rows(whole)], axis=0)
+    share = x_ref[pl.ds(pl.multiple_of(8 * lax.axis_index("tgt"), 8), 8), :]
     for s in range(out.shape[0]):
-        out[s] = pair
+        out[s, 0:8] = pair
+        for k in range(0, count, 128):
+            out[s, 8 + k // 16 : 16 + k // 16] = share[:, k : k + 128]
 
 
 def row_first(x, y, copies):
     tile, count = 1024, x.shape[1]
     return pl.pallas_call(
         functools.partial(row_first_kernel, tile),
-        in_specs=whole(2),
-        out_specs=whole(1)[0],
-        out_shape=kept((copies, 8, 128))[0],
+        in_specs=[pl.BlockSpec(memory_space=pl.ANY)] * 2,
+        out_specs=whole(2),
+        out_shape=kept((copies, 8 + count // 16, 128), y.shape),
         scratch_shapes=[
+            pltpu.VMEM(x.shape, F32),
             pltpu.VMEM((count, DEPTH), BF),
             pltpu.VMEM((2, DEPTH, tile), BF),
             pltpu.VMEM((2, count, tile), F32),
             pltpu.VMEM((count, 128), F32),
             pltpu.VMEM((count, 128), F32),
+            pltpu.SemaphoreType.DMA((3,)),
         ],
         compiler_params=params(),
         name="row_first",
-    )(*near([x, y]))
-
-
-def col_first_kernel(tile, log_b, at, x0, x1, x2, x3, parts, y_ref, out, dual_out, still, moving, scores, found):
-    count = x0.shape[1]
+    )(x, y)
+
+
+def col_first_kernel(tile, log_b, parts, y_ref, out, dual_out, x_out, still, moving, scores, found):
+    count = x_out.shape[2]
     half = found.shape[0] // 2
-    for k, x_ref in enumerate((x0, x1, x2, x3)):
-        row = (at[0] + 4 - k) % 4
+    for row in range(4):
         pieces = [parts[4 * s + row] for s in range(4)]
         top = tree(jnp.maximum, [p[0:4] for p in pieces])
-        whole = tree(jnp.add, [p[4:8] * jnp.exp2(p[0:4] - top) for p in pieces])
-        dual = -(top + log2(whole) + log_b)
-        dual_out[4 * k : 4 * k + 4, :] = dual
-        x = x_ref[...]
-        build_still(x, lanes(dual) - UNIT * square_norm(x), still.at[pl.ds(count * k, count)])
+        total = tree(jnp.add, [p[4:8] * jnp.exp2(p[0:4] - top) for p in pieces])
+        dual = -(top + log2(total) + log_b)
+        dual_out[4 * row : 4 * row + 4, :] = dual
+        shares = [jnp.concatenate([p[k : k + 8] for k in range(8, p.shape[0], 8)], axis=1) for p in pieces]
+        x = jnp.concatenate(shares, axis=0)
+        x_out[row] = x
+        build_still(x, lanes(dual) - UNIT * square_norm(x), still.at[pl.ds(count * row, count)])
     moving[:, 208:DEPTH, :] = jnp.zeros((2, DEPTH - 208, tile), BF)
 
     def make(t, slot):
-        y = quarter(y_ref, at, t, tile)
+        y = quarter(y_ref, t, tile)
         build_moving(y, -UNIT * square_norm(y), moving.at[slot])
 
     def multiply(slot):
@@ -246,57 +262,47 @@
     out[...] = found[...]
 
 
-def at_start(shape):
-    return pl.BlockSpec(shape, lambda i, at: (0,) * len(shape))
-
-
-def col_first(at, blocks, parts, y, log_b):
-    tile, count = 256, blocks[0].shape[1]
-    width = y.shape[1] // 4
+def col_first(parts, y, log_b, count):
+    tile, width = 256, y.shape[1] // 4
     lines = width // 64
     return pl.pallas_call(
         functools.partial(col_first_kernel, tile, log_b),
-        out_shape=kept((lines, 128), (16, 128)),
-        grid_spec=pltpu.PrefetchScalarGridSpec(
-            num_scalar_prefetch=1,
-            grid=(1,),
-            in_specs=whole(6),
-            out_specs=whole(2),
-            scratch_shapes=[
-                pltpu.VMEM((4 * count, DEPTH), BF),
-                pltpu.VMEM((2, DEPTH, tile), BF),
-                pltpu.VMEM((2, 4 * count, tile), F32),
-                pltpu.VMEM((lines, 128), F32),
-            ],
-        ),
+        in_specs=whole(2),
+        out_specs=whole(3),
+        out_shape=kept((lines, 128), (16, 128), (4, 32, count)),
+        scratch_shapes=[
+            pltpu.VMEM((4 * count, DEPTH), BF),
+            pltpu.VMEM((2, DEPTH, tile), BF),
+            pltpu.VMEM((2, 4 * count, tile), F32),
+            pltpu.VMEM((lines, 128), F32),
+        ],
         compiler_params=params(),
         name="col_first",
-    )(at, *near([*blocks, parts, y]))
-
-
-def row_second_kernel(
-    tile, log_a, log_b, at, x0, x1, x2, x3, f_ref, y_ref, p0, p1, p2, p3, p4, p5, p6, p7, *rest
-):
-    count = x0.shape[1]
-    out, own, every, still, moving, scores, total, dual = rest
-    parts = (p0, p1, p2, p3, p4, p5, p6, p7)
-    half = p0.shape[0] // 2
+    )(*near([parts, y]))
+
+
+def row_second_kernel(tile, log_a, log_b, x_ref, f_ref, y_ref, *rest):
+    out, own, every, still, moving, scores, total, dual = rest[8:]
+    count = x_ref.shape[2]
+    parts = rest[:8]
+    half = parts[0].shape[0] // 2
     top = tree(jnp.maximum, [p[0:half] for p in parts])
-    whole = tree(jnp.add, [p[half:] * jnp.exp2(p[0:half] - top) for p in parts])
-    g = -(top + log2(whole) + log_a)
+    sums = tree(jnp.add, [p[half:] * jnp.exp2(p[0:half] - top) for p in parts])
+    g = -(top + log2(sums) + log_a)
     every[...] = g
     for t in range(half // 2):
         dual[t] = g[2 * t : 2 * t + 2]
-    own[...] = jnp.concatenate([dual[2 * at[1]], dual[2 * at[1] + 1]], axis=0)
-    for k, x_ref in enumerate((x0, x1, x2, x3)):
-        x = x_ref[...]
-        f = lanes(f_ref[4 * k : 4 * k + 4])
-        build_still(x, f - UNIT * square_norm(x), still.at[pl.ds(count * k, count)])
+    place = 2 * lax.axis_index(("z", "core"))
+    own[...] = jnp.concatenate([dual[place], dual[place + 1]], axis=0)
+    for row in range(4):
+        x = x_ref[row]
+        f = lanes(f_ref[4 * row : 4 * row + 4])
+        build_still(x, f - UNIT * square_norm(x), still.at[pl.ds(count * row, count)])
     moving[:, 208:DEPTH, :] = jnp.zeros((2, DEPTH - 208, tile), BF)
     total[...] = jnp.zeros(total.shape, F32)
 
     def make(t, slot):
-        y = quarter(y_ref, at, t, tile)
+        y = quarter(y_ref, t, tile)
         build_moving(y, lanes(dual[t]) + log_b - UNIT * square_norm(y), moving.at[slot])
 
     def multiply(slot):
@@ -310,51 +316,45 @@
     sweep(y_ref.shape[1] // 4 // tile, make, multiply, process)
     for k in range(4):
         line = jnp.sum(total[count * k : count * k + count, :].T, axis=0, keepdims=True)
-        row = (at[0] + 4 - k) % 4
         for s in range(out.shape[0]):
-            out[s, row] = rows(line)
-
-
-def row_second(at, blocks, f, parts, y, log_a, log_b, copies):
-    tile, count = 256, blocks[0].shape[1]
-    width = y.shape[1] // 4
+            out[s, k] = rows(line)
+
+
+def row_second(x, f, y, parts, log_a, log_b, copies):
+    tile, count, width = 256, x.shape[2], y.shape[1] // 4
     return pl.pallas_call(
         functools.partial(row_second_kernel, tile, log_a, log_b),
+        in_specs=whole(3 + len(parts)),
+        out_specs=whole(3),
         out_shape=kept((copies, 4, 4, 128), (4, 128), (width // 128, 128)),
-        grid_spec=pltpu.PrefetchScalarGridSpec(
-            num_scalar_prefetch=1,
-            grid=(1,),
-            in_specs=whole(6 + len(parts)),
-            out_specs=whole(3),
-            scratch_shapes=[
-                pltpu.VMEM((4 * count, DEPTH), BF),
-                pltpu.VMEM((2, DEPTH, tile), BF),
-                pltpu.VMEM((2, 4 * count, tile), F32),
-                pltpu.VMEM((4 * count, 128), F32),
-                pltpu.VMEM((width // tile, 2, 128), F32),
-            ],
-        ),
+        scratch_shapes=[
+            pltpu.VMEM((4 * count, DEPTH), BF),
+            pltpu.VMEM((2, DEPTH, tile), BF),
+            pltpu.VMEM((2, 4 * count, tile), F32),
+            pltpu.VMEM((4 * count, 128), F32),
+            pltpu.VMEM((width // tile, 2, 128), F32),
+        ],
         compiler_params=params(),
         name="row_second",
-    )(at, *near([*blocks, f, y, *parts]))
-
-
-def col_second_kernel(
-    tile, log_a, at, x0, x1, x2, x3, f_ref, parts, y_ref, g_ref, mine, other, own, still, moving, scores, weights, values, dual, out
-):
-    count = x0.shape[1]
+    )(*near([x, f, y, *parts]))
+
+
+def col_second_kernel(tile, log_a, x_ref, f_ref, parts, y_ref, g_ref, mine, other, own, *rest):
+    still, moving, scores, weights, values, dual, out, fresh = rest
+    count = x_ref.shape[2]
     half = 4 * count
-    for k, x_ref in enumerate((x0, x1, x2, x3)):
-        row = (at[0] + 4 - k) % 4
-        whole = tree(jnp.add, [parts[s, row] for s in range(parts.shape[0])])
-        f = f_ref[4 * k : 4 * k + 4, :] - log2(whole)
-        if k == 0:
-            own[...] = f * (1.0 / UNIT)
-        x = x_ref[...]
-        build_still(x, lanes(f) - UNIT * square_norm(x), still.at[pl.ds(count * k, count)])
+    for row in range(4):
+        sums = tree(jnp.add, [parts[s, row] for s in range(parts.shape[0])])
+        f = f_ref[4 * row : 4 * row + 4, :] - log2(sums)
+        fresh[row] = f * (1.0 / UNIT)
+        x = x_ref[row]
+        here = slice(count * row, count * row + count)
+        there = slice(half + count * row, half + count * row + count)
+        build_still(x, lanes(f) - UNIT * square_norm(x), still.at[here])
         for part, piece in enumerate(split3(x)):
-            values[32 * part : 32 * part + 32, count * k : count * k + count] = piece
-            values[32 * part : 32 * part + 32, half + count * k : half + count * k + count] = piece
+            values[32 * part : 32 * part + 32, here] = piece
+            values[32 * part : 32 * part + 32, there] = piece
+    own[...] = fresh[lax.axis_index("y")]
     values[96:112, :] = jnp.ones((16, 2 * half), BF)
     moving[:, 208:DEPTH, :] = jnp.zeros((2, DEPTH - 208, tile), BF)
     weights[1] = jnp.zeros((2 * half, tile), BF)
@@ -363,7 +363,7 @@
         dual[t] = g_ref[2 * t : 2 * t + 2, :]
 
     def make(t, slot):
-        y = quarter(y_ref, at, t, tile)
+        y = quarter(y_ref, t, tile)
         build_moving(y, lanes(dual[t]) + log_a - UNIT * square_norm(y), moving.at[slot])
 
     def multiply(slot):
@@ -403,57 +403,49 @@
 
     lax.fori_loop(0, steps // 2, pair, 0)
     gather(steps // 2 - 1, 1)
-    core = at[1] % 2
+    core = lax.axis_index("core")
     for z in range(mine.shape[0]):
         mine[z] = out[2 * z + core]
         other[z] = out[2 * z + 1 - core]
 
 
-def col_second(at, blocks, f, parts, y, g, log_a):
-    tile, count = 256, blocks[0].shape[1]
-    width = y.shape[1] // 4
+def col_second(x, f, parts, y, g, log_a):
+    tile, count, width = 256, x.shape[2], y.shape[1] // 4
     return pl.pallas_call(
         functools.partial(col_second_kernel, tile, log_a),
+        in_specs=whole(5),
+        out_specs=whole(2) + [pl.BlockSpec((4, 128), lambda: (0, 0))],
         out_shape=kept(*((width // 1024, 136, 128),) * 2) + (jax.ShapeDtypeStruct((4, 128), F32),),
-        grid_spec=pltpu.PrefetchScalarGridSpec(
-            num_scalar_prefetch=1,
-            grid=(1,),
-            in_specs=whole(8),
-            out_specs=whole(2) + [at_start((4, 128))],
-            scratch_shapes=[
-                pltpu.VMEM((4 * count, DEPTH), BF),
-                pltpu.VMEM((2, DEPTH, tile), BF),
-                pltpu.VMEM((2, 4 * count, tile), F32),
-                pltpu.VMEM((2, 8 * count, tile), BF),
-                pltpu.VMEM((112, 8 * count), BF),
-                pltpu.VMEM((width // tile, 2, 128), F32),
-                pltpu.VMEM((width // 512, 136, 128), F32),
-            ],
-        ),
+        scratch_shapes=[
+            pltpu.VMEM((4 * count, DEPTH), BF),
+            pltpu.VMEM((2, DEPTH, tile), BF),
+            pltpu.VMEM((2, 4 * count, tile), F32),
+            pltpu.VMEM((2, 8 * count, tile), BF),
+            pltpu.VMEM((112, 8 * count), BF),
+            pltpu.VMEM((width // tile, 2, 128), F32),
+            pltpu.VMEM((width // 512, 136, 128), F32),
+            pltpu.VMEM((4, 4, 128), F32),
+        ],
         compiler_params=params(),
         name="col_second",
-    )(at, *near([*blocks, f, parts, y, g]))
-
-
-def merge_kernel(at, mine, other, *outs):
+    )(*near([x, f, parts, y, g]))
+
+
+def merge_kernel(mine, other, *outs):
     for k, out in enumerate(outs):
-        z = (at[1] // 2 + k) % 4
+        z = (lax.axis_index("z") + k) & 3
         out[...] = mine[z] + other[z]
 
 
-def merge(at, mine, other):
+def merge(mine, other):
     return pl.pallas_call(
         merge_kernel,
+        in_specs=whole(2),
+        out_specs=whole(4),
         out_shape=kept(*((136, 128),) * 4),
-        grid_spec=pltpu.PrefetchScalarGridSpec(
-            num_scalar_prefetch=1,
-            grid=(1,),
-            in_specs=whole(2),
-            out_specs=whole(4),
-        ),
         compiler_params=params(),
         name="merge",
-    )(at, *near([mine, other]))
+    )(*near([mine, other]))
 
 
 def finish_kernel(g_ref, p0, p1, p2, p3, out):
@@ -478,9 +470,9 @@
 TURNS = (0, 1, 3, 2)
 
 
-def place_kernel(turns, at, *refs):
+def place_kernel(turns, *refs):
     mapped, dual = refs[-2:]
-    y, z, core = at[0], at[1] // 2, at[1] % 2
+    y, z, core = lax.axis_index("y"), lax.axis_index("z"), lax.axis_index("core")
     for n, ref in enumerate(refs[:-2]):
         turn, owner = turns[n // 2], core if n % 2 == 0 else 1 - core
         for b in range(4):
@@ -493,19 +485,14 @@
             dual[spot] = ref[b, 128:132, :]
 
 
-def place(at, pieces, turns):
+def place(pieces, turns):
     return pl.pallas_call(
         functools.partial(place_kernel, turns),
+        in_specs=whole(len(pieces)),
         out_shape=(jax.ShapeDtypeStruct((32, 16384), F32), jax.ShapeDtypeStruct((32, 4, 128), F32)),
-        grid_spec=pltpu.PrefetchScalarGridSpec(
-            num_scalar_prefetch=1,
-            grid=(1,),
-            in_specs=whole(len(pieces)),
-            out_specs=(at_start((32, 16384)), at_start((32, 4, 128))),
-        ),
         compiler_params=params(),
         name="place",
-    )(at, *near(pieces))
+    )(*near(pieces))
 
 
 def turned(block, turn, first):
@@ -519,12 +506,12 @@
     return lax.ppermute(block, ("y", "z", "core"), pairs)
 
 
-def publish(at, block):
+def publish(block):
     line = jnp.stack([block] + [turned(block, turn, True) for turn in TURNS[1:]])
     turns = (0, 2, 1, 3)
     pieces = [line] + [turned(line, turn, False) for turn in turns[1:]]
     others = [lax.ppermute(piece, "core", [(0, 1), (1, 0)]) for piece in pieces]
-    return place(at, [p for pair in zip(pieces, others) for p in pair], turns)
+    return place([p for pair in zip(pieces, others) for p in pair], turns)
 
 
 def spread(copies, axes):
@@ -539,20 +526,15 @@
 def body(x, y):
     log_a = -math.log2(x.shape[1] * 32)
     log_b = -math.log2(y.shape[1] * 4)
-    place = lax.axis_index("y"), lax.axis_index(("z", "core"))
-    at = jnp.stack(place).astype(jnp.int32)
-    first = row_first(x, y, 16)
-    early, _ = lax.optimization_barrier((x, first))
-    blocks = [x] + [along(early, "y", turn) for turn in (1, 2, 3)]
-
-    partial, f1 = col_first(at, blocks, spread(first, ("tgt", "y")), y, log_b)
+    first, near_y = row_first(x, y, 16)
+    partial, f1, near_x = col_first(spread(first, ("tgt", "y")), near_y, log_b, x.shape[1])
     partial = [partial] + [along(partial, "z", turn) for turn in (2, 1, 3)]
     partial = partial + [along(p, "core", 1) for p in partial]
-    second, own_g, g1 = row_second(at, blocks, f1, partial, y, log_a, log_b, 16)
-    mine, other, source_dual = col_second(at, blocks, f1, spread(second, ("tgt", "y")), y, g1, log_a)
-    sums = merge(at, mine, along(other, "core", 1))
+    second, own_g, g1 = row_second(near_x, f1, near_y, partial, log_a, log_b, 16)
+    mine, other, source_dual = col_second(near_x, f1, spread(second, ("tgt", "y")), near_y, g1, log_a)
+    sums = merge(mine, along(other, "core", 1))
     sums = [sums[0]] + [along(sums[turn], "z", turn) for turn in (1, 2, 3)]
-    mapped, target_dual = publish(at, finish(own_g, sums))
+    mapped, target_dual = publish(finish(own_g, sums))
     return source_dual.reshape(-1), target_dual.reshape(-1), mapped
 
 

time: 138 us -> 127 us (0.920)
  starting transfers between devices: 54.9 us -> 38.9 us
  blocking collectives: 11.3 us -> 25.1 us
  waiting for transfers between devices: 16.9 us -> 12.6 us
  Pallas kernels: 49.8 us -> 47 us
  local copies, waits for them, and re-layouts: 2.43 us -> 0 us
    all_to_all x1 -> x0, starting transfers between devices: 18.1 us -> none  [spread(): return lax.all_to_all(copies, axes, 0, 0)]
    all_to_all x1 -> x2, blocking collectives: 11.3 us -> 25.1 us  [spread(): return lax.all_to_all(copies, axes, 0, 0)]
    ppermute x4, starting transfers between devices: 9.91 us -> 12.6 us  [publish(): others = [lax.ppermute(piece, 'core', [(0, 1), (1, 0)]) for piece in pieces]]
    unnamed x8 -> x0, local copies, waits for them, and re-layouts: 2.43 us -> none
    pallas_call x5, Pallas kernels: 42.3 us -> 40.2 us  [the longest x1 16.7 us: col_first(): pl.pallas_call(functools.partial(col_first_kernel, tile, log_b), in_specs...]
    all_to_all x1 -> x0, waiting for transfers between devices: 2.09 us -> none  [spread(): return lax.all_to_all(copies, axes, 0, 0)]
    ppermute x6, waiting for transfers between devices: 6.83 us -> 5.35 us  [turned(): return lax.ppermute(block, ('y', 'z', 'core'), pairs)]
    ppermute x14 -> x11, waiting for transfers between devices: 6.41 us -> 5.72 us  [along(): return lax.ppermute(block, axis, [(i, (i + turn) % n) for i in range(n)])]
  transfers between devices with their start and end apart: 25 -> 21, of which waited for: 14 -> 12; matrix products, arithmetic and copies ran while one was open for 0% -> 0% of each run, Pallas kernels for 0% -> 0%
where the time goes in v4:
time: 127 us; the launch traced here: 124 us
  Pallas kernels  47 us (37%)
  starting transfers between devices  38.9 us (31%)
  blocking collectives  25.1 us (20%)
  waiting for transfers between devices  12.6 us (10%)
    all_to_all x2, blocking collectives, spread(): return lax.all_to_all(copies, axes, 0, 0)  25.1 us
    ppermute x11, starting transfers between devices, along(): return lax.ppermute(block, axis, [(i, (i + turn) % n) for i in range(n)])  20.3 us
    pallas_call x1, Pallas kernels, col_first(): pl.pallas_call(functools.partial(col_first_kernel, tile, log_b), in_specs...  16.7 us
    pallas_call x1, Pallas kernels, col_second(): pl.pallas_call(functools.partial(col_second_kernel, tile, log_a), in_spec...  13.3 us
    ppermute x4, starting transfers between devices, publish(): others = [lax.ppermute(piece, 'core', [(0, 1), (1, 0)]) for piece in pieces]  12.6 us
    pallas_call x1, Pallas kernels, row_first(): pl.pallas_call(functools.partial(row_first_kernel, tile), in_specs=[pl.Bl...  8.5 us
    pallas_call x1, Pallas kernels, row_second(): pl.pallas_call(functools.partial(row_second_kernel, tile, log_a, log_b),...  6.77 us
    ppermute x6, starting transfers between devices, turned(): return lax.ppermute(block, ('y', 'z', 'core'), pairs)  6.03 us
  transfers between devices with their start and end apart: 21, of which 12 were waited for; matrix products, arithmetic and copies ran while one was open for 0% of the time, Pallas kernels for 0%

profile of v4, /device:TPU:1, one launch (start us, length us, event | category | flops | bytes accessed | tf_op | source)
XLA Modules:
  0.0 124.4 jit_solution(1152156256386826710)
XLA Ops:
  0.6 8.5 %row_first.1 = (f32[16,40,128]{2,1,0:T(8,128)S(1)}, f32[32,16384]{1,0:T(8,128)S(1)}) custom-call(f32[32,512]{1,0:T(8,128)} %x_far.1, f32[32,16384]{1,0:T(8,128)} %y_far.1), custom_call_target="tpu_custom_call" | custom-call | tf_op jit(solution)/shard_map/row_first/pallas_call | solution.py:188
  9.1 15.2 %all_to_all.10.parts = f32[16,40,128]{2,1,0:T(8,128)S(1)} all-to-all(f32[16,40,128]{2,1,0:T(8,128)S(1)} %get-tuple-element.20), channel_id=1, replica_groups=mesh['y'=4,'z'=4,'core'=2,'tgt'=4] {'tgt','y'}, dimensions={0} | all-to-all | bytes 655360 | tf_op jit(solution)/shard_map/all_to_all | solution.py:518
  24.3 16.7 %col_first.1 = (f32[64,128]{1,0:T(8,128)S(1)}, f32[16,128]{1,0:T(8,128)S(1)}, f32[4,32,512]{2,1,0:T(8,128)S(1)}) custom-call(f32[16,40,128]{2,1,0:T(8,128)S(1)} %all_to_all.10.parts, f32[32,16384]{1,0:T(8,128)S(1)} %get-tuple-element.21.y_ref), custom_call_target="tpu_custom_call" | custom-call | tf_op jit(solution)/shard_map/col_first/pallas_call | solution.py:268
  41.1 3.8 %collective-permute-start.2 = (f32[64,128]{1,0:T(8,128)S(1)}, f32[64,128]{1,0:T(8,128)S(1)}, u32[]{:S(2)}, u32[]{:S(2)}) collective-permute-start(f32[64,128]{1,0:T(8,128)S(1)} %get-tuple-element.24.rest_0_), channel_id=1, source_target_pairs={{0,24},{8,0},{16,8},{24,16},{1,25},{9,1},{17,9},{25,17},{2,26},{10... | collective-permute-start | bytes 98312 | tf_op jit(solution)/shard_map/ppermute | solution.py:523
  44.9 0.0 collective-permute-start.1
  44.9 9.5 %collective-permute-start = (f32[64,128]{1,0:T(8,128)S(1)}, f32[64,128]{1,0:T(8,128)S(1)}, u32[]{:S(2)}, u32[]{:S(2)}) collective-permute-start(f32[64,128]{1,0:T(8,128)S(1)} %get-tuple-element.24.rest_0_), channel_id=1, source_target_pairs={{0,16},{8,24},{16,0},{24,8},{1,17},{9,25},{17,1},{25,9},{2,18},{10... | collective-permute-start | bytes 98312 | tf_op jit(solution)/shard_map/ppermute | solution.py:523
  54.3 0.0 collective-permute-start.3
  54.3 0.0 collective-permute-done.2.rest_3_
  54.3 0.5 collective-permute-start.6
  54.9 0.0 collective-permute-done.1.rest_2_
  54.9 0.1 collective-permute-start.5
  54.9 1.0 collective-permute-done.rest_1_
  56.0 0.0 collective-permute-start.4
  56.0 0.0 collective-permute-done.3.rest_4_
  56.0 0.0 collective-permute-done.6.rest_7_
  56.0 0.1 collective-permute-done.5.rest_6_
  56.1 1.1 collective-permute-done.4.rest_5_
  57.2 6.8 %row_second.1 = (f32[16,4,4,128]{3,2,1,0:T(4,128)S(1)}, f32[4,128]{1,0:T(4,128)S(1)}, f32[32,128]{1,0:T(8,128)S(1)}) custom-call(f32[4,32,512]{2,1,0:T(8,128)S(1)} %get-tuple-element.22.x_ref, f32[16,128]{1,0:T(8,128)S(1)} %get-tuple-element.23.f_ref, f32[32,16384]{1,0:T(8,128)S(1)} %get-tuple-element.21.y_ref, f32[64,128]{1,0:T(8,128)S(1)} %get-tuple-element.24.rest_0_, ...), custom_call_target="tpu_custom_call" | custom-call | tf_op jit(solution)/shard_map/row_second/pallas_call | solution.py:325
  64.0 9.9 %all_to_all.11.parts = f32[16,4,4,128]{3,2,1,0:T(4,128)S(1)} all-to-all(f32[16,4,4,128]{3,2,1,0:T(4,128)S(1)} %get-tuple-element.25), channel_id=1, replica_groups=mesh['y'=4,'z'=4,'core'=2,'tgt'=4] {'tgt','y'}, dimensions={0} | all-to-all | bytes 262144 | tf_op jit(solution)/shard_map/all_to_all | solution.py:518
  73.9 13.3 %col_second.1 = (f32[4,136,128]{2,1,0:T(8,128)S(1)}, f32[4,136,128]{2,1,0:T(8,128)S(1)}, f32[4,128]{1,0:T(4,128)}) custom-call(f32[4,32,512]{2,1,0:T(8,128)S(1)} %get-tuple-element.22.x_ref, f32[16,128]{1,0:T(8,128)S(1)} %get-tuple-element.23.f_ref, f32[16,4,4,128]{3,2,1,0:T(4,128)S(1)} %all_to_all.11.parts, f32[32,16384]{1,0:T(8,128)S(1)} %get-tuple-element.21.y_ref, ...), custom_call_target="tpu_custom_call" | custom-call | tf_op jit(solution)/shard_map/col_second/pallas_call | solution.py:414
  87.2 1.6 %collective-permute-start.7 = (f32[4,136,128]{2,1,0:T(8,128)S(1)}, f32[4,136,128]{2,1,0:T(8,128)S(1)}, u32[]{:S(2)}, u32[]{:S(2)}) collective-permute-start(f32[4,136,128]{2,1,0:T(8,128)S(1)} %get-tuple-element.30), channel_id=1, source_target_pairs={{0,4},{4,0},{1,5},{5,1},{2,6},{6,2},{3,7},{7,3},{8,12},{12,8},{9,1... | collective-permute-start | bytes 835592 | tf_op jit(solution)/shard_map/ppermute | solution.py:523
  88.8 1.2 collective-permute-done.7.other
  90.1 1.0 collective-permute-start.8
  91.0 2.0 %collective-permute-start.9 = (f32[136,128]{1,0:T(8,128)S(1)}, f32[136,128]{1,0:T(8,128)S(1)}, u32[]{:S(2)}, u32[]{:S(2)}) collective-permute-start(f32[136,128]{1,0:T(8,128)S(1)} %get-tuple-element.33), channel_id=1, source_target_pairs={{0,16},{8,24},{16,0},{24,8},{1,17},{9,25},{17,1},{25,9},{2,18},{10... | collective-permute-start | bytes 208904 | tf_op jit(solution)/shard_map/ppermute | solution.py:523
  93.0 1.8 %collective-permute-start.10 = (f32[136,128]{1,0:T(8,128)S(1)}, f32[136,128]{1,0:T(8,128)S(1)}, u32[]{:S(2)}, u32[]{:S(2)}) collective-permute-start(f32[136,128]{1,0:T(8,128)S(1)} %get-tuple-element.34), channel_id=1, source_target_pairs={{0,24},{8,0},{16,8},{24,16},{1,25},{9,1},{17,9},{25,17},{2,26},{10... | collective-permute-start | bytes 208904 | tf_op jit(solution)/shard_map/ppermute | solution.py:523
  94.8 0.0 collective-permute-done.8.p1
  94.8 1.2 collective-permute-done.9.p2
  96.1 1.1 collective-permute-done.10.p3
  97.1 1.8 %collective-permute-start.13 = (f32[136,128]{1,0:T(8,128)S(1)}, f32[136,128]{1,0:T(8,128)S(1)}, u32[]{:S(2)}, u32[]{:S(2)}) collective-permute-start(f32[136,128]{1,0:T(8,128)S(1)} %finish.1), channel_id=1, source_target_pairs={{0,64},{4,20},{8,72},{12,28},{16,80},{20,4},{24,88},{28,12},{32,96... | collective-permute-start | bytes 208904 | tf_op jit(solution)/shard_map/ppermute | solution.py:506
  98.9 1.2 collective-permute-start.12
  100.1 0.3 collective-permute-start.11
  100.4 1.5 %collective-permute-done.13 = f32[136,128]{1,0:T(8,128)S(1)} collective-permute-done((f32[136,128]{1,0:T(8,128)S(1)}, f32[136,128]{1,0:T(8,128)S(1)}, u32[]{:S(2)}, u32[]{:S(2)}) %collective-permute-start.13) | collective-permute-done | bytes 69664 | tf_op jit(solution)/shard_map/ppermute | solution.py:506
  101.9 1.2 collective-permute-done.12
  103.1 1.4 %collective-permute-done.11 = f32[136,128]{1,0:T(8,128)S(1)} collective-permute-done((f32[136,128]{1,0:T(8,128)S(1)}, f32[136,128]{1,0:T(8,128)S(1)}, u32[]{:S(2)}, u32[]{:S(2)}) %collective-permute-start.11) | collective-permute-done | bytes 69664 | tf_op jit(solution)/shard_map/ppermute | solution.py:506
  104.5 1.4 %collective-permute-start.19 = (f32[4,136,128]{2,1,0:T(8,128)S(1)}, f32[4,136,128]{2,1,0:T(8,128)S(1)}, u32[]{:S(2)}, u32[]{:S(2)}) collective-permute-start(f32[4,136,128]{2,1,0:T(8,128)S(1)} %pad_maximum_fusion.refs_0_), channel_id=1, source_target_pairs={{0,24},{4,100},{8,0},{12,108},{16,8},{20,116},{24,16},{28,124},{32... | collective-permute-start | bytes 835592 | tf_op jit(solution)/shard_map/ppermute | solution.py:506
  105.9 0.2 collective-permute-start.17
  106.0 1.2 collective-permute-start.15
  107.3 4.7 %collective-permute-start.14 = (f32[4,136,128]{2,1,0:T(8,128)S(1)}, f32[4,136,128]{2,1,0:T(8,128)S(1)}, u32[]{:S(2)}, u32[]{:S(2)}) collective-permute-start(f32[4,136,128]{2,1,0:T(8,128)S(1)} %pad_maximum_fusion.refs_0_), channel_id=1, source_target_pairs={{0,4},{4,0},{1,5},{5,1},{2,6},{6,2},{3,7},{7,3},{8,12},{12,8},{9,1... | collective-permute-start | bytes 835592 | tf_op jit(solution)/shard_map/ppermute | solution.py:513
  112.0 0.0 collective-permute-done.19.refs_6_
  112.0 2.5 %collective-permute-start.20 = (f32[4,136,128]{2,1,0:T(8,128)S(1)}, f32[4,136,128]{2,1,0:T(8,128)S(1)}, u32[]{:S(2)}, u32[]{:S(2)}) collective-permute-start(f32[4,136,128]{2,1,0:T(8,128)S(1)} %collective-permute-done.19.refs_6_), channel_id=1, source_target_pairs={{0,4},{4,0},{1,5},{5,1},{2,6},{6,2},{3,7},{7,3},{8,12},{12,8},{9,1... | collective-permute-start | bytes 835592 | tf_op jit(solution)/shard_map/ppermute | solution.py:513
  114.5 1.3 %collective-permute-done.17.refs_4_ = f32[4,136,128]{2,1,0:T(8,128)S(1)} collective-permute-done((f32[4,136,128]{2,1,0:T(8,128)S(1)}, f32[4,136,128]{2,1,0:T(8,128)S(1)}, u32[]{:S(2)}, u32[]{:S(2)}) %collective-permute-start.17) | collective-permute-done | bytes 278560 | tf_op jit(solution)/shard_map/ppermute | solution.py:506
  115.8 5.4 %collective-permute-start.18 = (f32[4,136,128]{2,1,0:T(8,128)S(1)}, f32[4,136,128]{2,1,0:T(8,128)S(1)}, u32[]{:S(2)}, u32[]{:S(2)}) collective-permute-start(f32[4,136,128]{2,1,0:T(8,128)S(1)} %collective-permute-done.17.refs_4_), channel_id=1, source_target_pairs={{0,4},{4,0},{1,5},{5,1},{2,6},{6,2},{3,7},{7,3},{8,12},{12,8},{9,1... | collective-permute-start | bytes 835592 | tf_op jit(solution)/shard_map/ppermute | solution.py:513
  121.2 0.0 collective-permute-done.15.refs_2_
  121.2 0.0 collective-permute-start.16
  121.2 0.0 collective-permute-done.14.refs_1_
  121.2 1.2 collective-permute-done.18.refs_5_
  122.4 0.4 collective-permute-done.16.refs_3_
  122.8 1.6 %place.1 = (f32[32,16384]{1,0:T(8,128)}, f32[32,4,128]{2,1,0:T(4,128)}) custom-call(f32[4,136,128]{2,1,0:T(8,128)S(1)} %pad_maximum_fusion.refs_0_, f32[4,136,128]{2,1,0:T(8,128)S(1)} %collective-permute-done.14.refs_1_, f32[4,136,128]{2,1,0:T(8,128)S(1)} %collective-permute-done.15.refs_2_, f32[4,136,128]{2,1,0:T(8,128)S(1)} %collective-permute-done.16.refs_3_, ...), custom_call_target="tpu_custom_call" | custom-call | tf_op jit(solution)/shard_map/place/pallas_call | solution.py:489
  (4 shorter events, 0.1 us)
Async XLA Ops:
  41.1 13.3 %collective-permute-start.2 = (f32[64,128]{1,0:T(8,128)S(1)}, f32[64,128]{1,0:T(8,128)S(1)}, u32[]{:S(2)}, u32[]{:S(2)}) collective-permute-start(f32[64,128]{1,0:T(8,128)S(1)} %get-tuple-element.24.rest_0_), channel_id=1, source_target_pairs={{0,24},{8,0},{16,8},{24,16},{1,25},{9,1},{17,9},{25,17},{2,26},{10... | collective-permute-start | bytes 98312 | tf_op jit(solution)/shard_map/ppermute | solution.py:523
  44.9 10.0 %collective-permute-start.1 = (f32[64,128]{1,0:T(8,128)S(1)}, f32[64,128]{1,0:T(8,128)S(1)}, u32[]{:S(2)}, u32[]{:S(2)}) collective-permute-start(f32[64,128]{1,0:T(8,128)S(1)} %get-tuple-element.24.rest_0_), channel_id=1, source_target_pairs={{0,8},{8,16},{16,24},{24,0},{1,9},{9,17},{17,25},{25,1},{2,10},{10... | collective-permute-start | bytes 98312 | tf_op jit(solution)/shard_map/ppermute | solution.py:523
  44.9 11.1 %collective-permute-start = (f32[64,128]{1,0:T(8,128)S(1)}, f32[64,128]{1,0:T(8,128)S(1)}, u32[]{:S(2)}, u32[]{:S(2)}) collective-permute-start(f32[64,128]{1,0:T(8,128)S(1)} %get-tuple-element.24.rest_0_), channel_id=1, source_target_pairs={{0,16},{8,24},{16,0},{24,8},{1,17},{9,25},{17,1},{25,9},{2,18},{10... | collective-permute-start | bytes 98312 | tf_op jit(solution)/shard_map/ppermute | solution.py:523
  54.3 1.7 %collective-permute-start.3 = (f32[64,128]{1,0:T(8,128)S(1)}, f32[64,128]{1,0:T(8,128)S(1)}, u32[]{:S(2)}, u32[]{:S(2)}) collective-permute-start(f32[64,128]{1,0:T(8,128)S(1)} %get-tuple-element.24.rest_0_), channel_id=1, source_target_pairs={{0,4},{4,0},{1,5},{5,1},{2,6},{6,2},{3,7},{7,3},{8,12},{12,8},{9,1... | collective-permute-start | bytes 98312 | tf_op jit(solution)/shard_map/ppermute | solution.py:523
  54.3 1.7 %collective-permute-start.6 = (f32[64,128]{1,0:T(8,128)S(1)}, f32[64,128]{1,0:T(8,128)S(1)}, u32[]{:S(2)}, u32[]{:S(2)}) collective-permute-start(f32[64,128]{1,0:T(8,128)S(1)} %collective-permute-done.2.rest_3_), channel_id=1, source_target_pairs={{0,4},{4,0},{1,5},{5,1},{2,6},{6,2},{3,7},{7,3},{8,12},{12,8},{9,1... | collective-permute-start | bytes 98312 | tf_op jit(solution)/shard_map/ppermute | solution.py:523
  54.9 1.2 collective-permute-start.5
  56.0 1.2 collective-permute-start.4
  87.2 2.8 %collective-permute-start.7 = (f32[4,136,128]{2,1,0:T(8,128)S(1)}, f32[4,136,128]{2,1,0:T(8,128)S(1)}, u32[]{:S(2)}, u32[]{:S(2)}) collective-permute-start(f32[4,136,128]{2,1,0:T(8,128)S(1)} %get-tuple-element.30), channel_id=1, source_target_pairs={{0,4},{4,0},{1,5},{5,1},{2,6},{6,2},{3,7},{7,3},{8,12},{12,8},{9,1... | collective-permute-start | bytes 835592 | tf_op jit(solution)/shard_map/ppermute | solution.py:523
  90.1 4.8 %collective-permute-start.8 = (f32[136,128]{1,0:T(8,128)S(1)}, f32[136,128]{1,0:T(8,128)S(1)}, u32[]{:S(2)}, u32[]{:S(2)}) collective-permute-start(f32[136,128]{1,0:T(8,128)S(1)} %get-tuple-element.32), channel_id=1, source_target_pairs={{0,8},{8,16},{16,24},{24,0},{1,9},{9,17},{17,25},{25,1},{2,10},{10... | collective-permute-start | bytes 208904 | tf_op jit(solution)/shard_map/ppermute | solution.py:523
  91.0 5.0 %collective-permute-start.9 = (f32[136,128]{1,0:T(8,128)S(1)}, f32[136,128]{1,0:T(8,128)S(1)}, u32[]{:S(2)}, u32[]{:S(2)}) collective-permute-start(f32[136,128]{1,0:T(8,128)S(1)} %get-tuple-element.33), channel_id=1, source_target_pairs={{0,16},{8,24},{16,0},{24,8},{1,17},{9,25},{17,1},{25,9},{2,18},{10... | collective-permute-start | bytes 208904 | tf_op jit(solution)/shard_map/ppermute | solution.py:523
  93.0 4.1 %collective-permute-start.10 = (f32[136,128]{1,0:T(8,128)S(1)}, f32[136,128]{1,0:T(8,128)S(1)}, u32[]{:S(2)}, u32[]{:S(2)}) collective-permute-start(f32[136,128]{1,0:T(8,128)S(1)} %get-tuple-element.34), channel_id=1, source_target_pairs={{0,24},{8,0},{16,8},{24,16},{1,25},{9,1},{17,9},{25,17},{2,26},{10... | collective-permute-start | bytes 208904 | tf_op jit(solution)/shard_map/ppermute | solution.py:523
  97.1 4.7 %collective-permute-start.13 = (f32[136,128]{1,0:T(8,128)S(1)}, f32[136,128]{1,0:T(8,128)S(1)}, u32[]{:S(2)}, u32[]{:S(2)}) collective-permute-start(f32[136,128]{1,0:T(8,128)S(1)} %finish.1), channel_id=1, source_target_pairs={{0,64},{4,20},{8,72},{12,28},{16,80},{20,4},{24,88},{28,12},{32,96... | collective-permute-start | bytes 208904 | tf_op jit(solution)/shard_map/ppermute | solution.py:506
  98.9 4.1 %collective-permute-start.12 = (f32[136,128]{1,0:T(8,128)S(1)}, f32[136,128]{1,0:T(8,128)S(1)}, u32[]{:S(2)}, u32[]{:S(2)}) collective-permute-start(f32[136,128]{1,0:T(8,128)S(1)} %finish.1), channel_id=1, source_target_pairs={{0,96},{4,28},{8,104},{12,4},{16,112},{20,12},{24,120},{28,20},{32... | collective-permute-start | bytes 208904 | tf_op jit(solution)/shard_map/ppermute | solution.py:506
  100.1 4.4 %collective-permute-start.11 = (f32[136,128]{1,0:T(8,128)S(1)}, f32[136,128]{1,0:T(8,128)S(1)}, u32[]{:S(2)}, u32[]{:S(2)}) collective-permute-start(f32[136,128]{1,0:T(8,128)S(1)} %finish.1), channel_id=1, source_target_pairs={{0,32},{4,12},{8,40},{12,20},{16,48},{20,28},{24,56},{28,4},{32,64... | collective-permute-start | bytes 208904 | tf_op jit(solution)/shard_map/ppermute | solution.py:506
  104.5 7.5 %collective-permute-start.19 = (f32[4,136,128]{2,1,0:T(8,128)S(1)}, f32[4,136,128]{2,1,0:T(8,128)S(1)}, u32[]{:S(2)}, u32[]{:S(2)}) collective-permute-start(f32[4,136,128]{2,1,0:T(8,128)S(1)} %pad_maximum_fusion.refs_0_), channel_id=1, source_target_pairs={{0,24},{4,100},{8,0},{12,108},{16,8},{20,116},{24,16},{28,124},{32... | collective-permute-start | bytes 835592 | tf_op jit(solution)/shard_map/ppermute | solution.py:506
  105.9 9.9 %collective-permute-start.17 = (f32[4,136,128]{2,1,0:T(8,128)S(1)}, f32[4,136,128]{2,1,0:T(8,128)S(1)}, u32[]{:S(2)}, u32[]{:S(2)}) collective-permute-start(f32[4,136,128]{2,1,0:T(8,128)S(1)} %pad_maximum_fusion.refs_0_), channel_id=1, source_target_pairs={{0,8},{4,36},{8,16},{12,44},{16,24},{20,52},{24,0},{28,60},{32,40}... | collective-permute-start | bytes 835592 | tf_op jit(solution)/shard_map/ppermute | solution.py:506
  106.0 15.1 %collective-permute-start.15 = (f32[4,136,128]{2,1,0:T(8,128)S(1)}, f32[4,136,128]{2,1,0:T(8,128)S(1)}, u32[]{:S(2)}, u32[]{:S(2)}) collective-permute-start(f32[4,136,128]{2,1,0:T(8,128)S(1)} %pad_maximum_fusion.refs_0_), channel_id=1, source_target_pairs={{0,16},{4,68},{8,24},{12,76},{16,0},{20,84},{24,8},{28,92},{32,48}... | collective-permute-start | bytes 835592 | tf_op jit(solution)/shard_map/ppermute | solution.py:506
  107.3 13.9 %collective-permute-start.14 = (f32[4,136,128]{2,1,0:T(8,128)S(1)}, f32[4,136,128]{2,1,0:T(8,128)S(1)}, u32[]{:S(2)}, u32[]{:S(2)}) collective-permute-start(f32[4,136,128]{2,1,0:T(8,128)S(1)} %pad_maximum_fusion.refs_0_), channel_id=1, source_target_pairs={{0,4},{4,0},{1,5},{5,1},{2,6},{6,2},{3,7},{7,3},{8,12},{12,8},{9,1... | collective-permute-start | bytes 835592 | tf_op jit(solution)/shard_map/ppermute | solution.py:513
  112.0 9.2 %collective-permute-start.20 = (f32[4,136,128]{2,1,0:T(8,128)S(1)}, f32[4,136,128]{2,1,0:T(8,128)S(1)}, u32[]{:S(2)}, u32[]{:S(2)}) collective-permute-start(f32[4,136,128]{2,1,0:T(8,128)S(1)} %collective-permute-done.19.refs_6_), channel_id=1, source_target_pairs={{0,4},{4,0},{1,5},{5,1},{2,6},{6,2},{3,7},{7,3},{8,12},{12,8},{9,1... | collective-permute-start | bytes 835592 | tf_op jit(solution)/shard_map/ppermute | solution.py:513
  115.8 6.6 %collective-permute-start.18 = (f32[4,136,128]{2,1,0:T(8,128)S(1)}, f32[4,136,128]{2,1,0:T(8,128)S(1)}, u32[]{:S(2)}, u32[]{:S(2)}) collective-permute-start(f32[4,136,128]{2,1,0:T(8,128)S(1)} %collective-permute-done.17.refs_4_), channel_id=1, source_target_pairs={{0,4},{4,0},{1,5},{5,1},{2,6},{6,2},{3,7},{7,3},{8,12},{12,8},{9,1... | collective-permute-start | bytes 835592 | tf_op jit(solution)/shard_map/ppermute | solution.py:513
  121.2 1.6 %collective-permute-start.16 = (f32[4,136,128]{2,1,0:T(8,128)S(1)}, f32[4,136,128]{2,1,0:T(8,128)S(1)}, u32[]{:S(2)}, u32[]{:S(2)}) collective-permute-start(f32[4,136,128]{2,1,0:T(8,128)S(1)} %collective-permute-done.15.refs_2_), channel_id=1, source_target_pairs={{0,4},{4,0},{1,5},{5,1},{2,6},{6,2},{3,7},{7,3},{8,12},{12,8},{9,1... | collective-permute-start | bytes 835592 | tf_op jit(solution)/shard_map/ppermute | solution.py:513

commit v5 on v4

--- a/solution.py
+++ b/solution.py
@@ -115,7 +115,7 @@
 def row_first_kernel(tile, x_far, y_far, out, y_ref, x_ref, still, moving, scores, peak, total, sem):
     count = x_ref.shape[1]
     steps = y_ref.shape[1] // tile
-    ahead = 2 * tile
+    ahead = tile
     get_x = pltpu.make_async_copy(x_far, x_ref, sem.at[0])
     get_first = pltpu.make_async_copy(y_far.at[:, 0:ahead], y_ref.at[:, 0:ahead], sem.at[1])
     get_rest = pltpu.make_async_copy(y_far.at[:, ahead:], y_ref.at[:, ahead:], sem.at[2])
@@ -184,7 +184,7 @@
 
 
 def row_first(x, y, copies):
-    tile, count = 1024, x.shape[1]
+    tile, count = 2048, x.shape[1]
     return pl.pallas_call(
         functools.partial(row_first_kernel, tile),
         in_specs=[pl.BlockSpec(memory_space=pl.ANY)] * 2,
@@ -206,7 +206,7 @@
 
 def col_first_kernel(tile, log_b, parts, y_ref, out, dual_out, x_out, still, moving, scores, found):
     count = x_out.shape[2]
-    half = found.shape[0] // 2
+    half, group = found.shape[0] // 2, tile // 128
     for row in range(4):
         pieces = [parts[4 * s + row] for s in range(4)]
         top = tree(jnp.maximum, [p[0:4] for p in pieces])
@@ -232,7 +232,7 @@
             total = [jnp.exp2(scores[slot, 8 * q : 8 * q + 8, column]) for q in range(8)]
             for r in range(64, 4 * count, 64):
                 total = [a + jnp.exp2(scores[slot, r + 8 * q : r + 8 * q + 8, column]) for q, a in enumerate(total)]
-            found[pl.ds(half + 2 * t + k // 128, 1), :] = jnp.sum(tree(jnp.add, total), axis=0, keepdims=True)
+            found[pl.ds(half + group * t + k // 128, 1), :] = jnp.sum(tree(jnp.add, total), axis=0, keepdims=True)
 
     found[0:half, :] = jnp.zeros((half, 128), F32)
     steps = y_ref.shape[1] // 4 // tile
@@ -252,24 +252,26 @@
                     total = total * jnp.exp2(peak - new) + tree(jnp.add, [jnp.exp2(a - new) for a in s])
                     peak = new
                 best = jnp.max(peak, axis=0, keepdims=True)
-                found[pl.ds(2 * t + k // 128, 1), :] = best
+                found[pl.ds(group * t + k // 128, 1), :] = best
                 whole = jnp.sum(total * jnp.exp2(peak - best), axis=0, keepdims=True)
-                found[pl.ds(half + 2 * t + k // 128, 1), :] = whole
+                found[pl.ds(half + group * t + k // 128, 1), :] = whole
             return carry
 
         lax.fori_loop(0, steps, step, 0)
 
-    out[...] = found[...]
-
-
-def col_first(parts, y, log_b, count):
-    tile, width = 256, y.shape[1] // 4
+    line = found[0:half] + log2(found[half:])
+    for s in range(out.shape[0]):
+        out[s] = line
+
+
+def col_first(parts, y, log_b, count, copies):
+    tile, width = 512, y.shape[1] // 4
     lines = width // 64
     return pl.pallas_call(
         functools.partial(col_first_kernel, tile, log_b),
         in_specs=whole(2),
         out_specs=whole(3),
-        out_shape=kept((lines, 128), (16, 128), (4, 32, count)),
+        out_shape=kept((copies, lines // 2, 128), (16, 128), (4, 32, count)),
         scratch_shapes=[
             pltpu.VMEM((4 * count, DEPTH), BF),
             pltpu.VMEM((2, DEPTH, tile), BF),
@@ -281,19 +283,17 @@
     )(*near([parts, y]))
 
 
-def row_second_kernel(tile, log_a, log_b, x_ref, f_ref, y_ref, *rest):
-    out, own, every, still, moving, scores, total, dual = rest[8:]
+def row_second_kernel(tile, log_a, log_b, x_ref, f_ref, y_ref, parts, *rest):
+    out, own, every, still, moving, scores, total, dual = rest
     count = x_ref.shape[2]
-    parts = rest[:8]
-    half = parts[0].shape[0] // 2
-    top = tree(jnp.maximum, [p[0:half] for p in parts])
-    sums = tree(jnp.add, [p[half:] * jnp.exp2(p[0:half] - top) for p in parts])
-    g = -(top + log2(sums) + log_a)
+    half = parts.shape[1]
+    logs = [parts[s] for s in range(parts.shape[0])]
+    top = tree(jnp.maximum, logs)
+    g = -(top + log2(tree(jnp.add, [jnp.exp2(p - top) for p in logs])) + log_a)
     every[...] = g
-    for t in range(half // 2):
-        dual[t] = g[2 * t : 2 * t + 2]
-    place = 2 * lax.axis_index(("z", "core"))
-    own[...] = jnp.concatenate([dual[place], dual[place + 1]], axis=0)
+    for t in range(half // 4):
+        dual[t] = g[4 * t : 4 * t + 4]
+    own[...] = dual[lax.axis_index(("z", "core"))]
     for row in range(4):
         x = x_ref[row]
         f = lanes(f_ref[4 * row : 4 * row + 4])
@@ -321,10 +321,10 @@
 
 
 def row_second(x, f, y, parts, log_a, log_b, copies):
-    tile, count, width = 256, x.shape[2], y.shape[1] // 4
+    tile, count, width = 512, x.shape[2], y.shape[1] // 4
     return pl.pallas_call(
         functools.partial(row_second_kernel, tile, log_a, log_b),
-        in_specs=whole(3 + len(parts)),
+        in_specs=whole(4),
         out_specs=whole(3),
         out_shape=kept((copies, 4, 4, 128), (4, 128), (width // 128, 128)),
         scratch_shapes=[
@@ -332,11 +332,11 @@
             pltpu.VMEM((2, DEPTH, tile), BF),
             pltpu.VMEM((2, 4 * count, tile), F32),
             pltpu.VMEM((4 * count, 128), F32),
-            pltpu.VMEM((width // tile, 2, 128), F32),
+            pltpu.VMEM((width // tile, tile // 128, 128), F32),
         ],
         compiler_params=params(),
         name="row_second",
-    )(*near([x, f, y, *parts]))
+    )(*near([x, f, y, parts]))
 
 
 def col_second_kernel(tile, log_a, x_ref, f_ref, parts, y_ref, g_ref, mine, other, own, *rest):
@@ -527,9 +527,8 @@
     log_a = -math.log2(x.shape[1] * 32)
     log_b = -math.log2(y.shape[1] * 4)
     first, near_y = row_first(x, y, 16)
-    partial, f1, near_x = col_first(spread(first, ("tgt", "y")), near_y, log_b, x.shape[1])
-    partial = [partial] + [along(partial, "z", turn) for turn in (2, 1, 3)]
-    partial = partial + [along(p, "core", 1) for p in partial]
+    partial, f1, near_x = col_first(spread(first, ("tgt", "y")), near_y, log_b, x.shape[1], 8)
+    partial = spread(partial, ("z", "core"))
     second, own_g, g1 = row_second(near_x, f1, near_y, partial, log_a, log_b, 16)
     mine, other, source_dual = col_second(near_x, f1, spread(second, ("tgt", "y")), near_y, g1, log_a)
     sums = merge(mine, along(other, "core", 1))

time: 127 us -> 126 us (level); the launches traced: 124 us -> 127 us
  blocking collectives: 25.1 us -> 47.3 us
  starting transfers between devices: 38.9 us -> 23.1 us
  Pallas kernels: 47 us -> 43.5 us
    all_to_all x2 -> x3, blocking collectives: 25.1 us -> 47.3 us  [spread(): return lax.all_to_all(copies, axes, 0, 0)]
    ppermute x11 -> x4, starting transfers between devices: 20.3 us -> 5.23 us  [along(): return lax.ppermute(block, axis, [(i, (i + turn) % n) for i in range(n)])]
    pallas_call x1, Pallas kernels: 16.7 us -> 13.9 us  [col_first(): pl.pallas_call(functools.partial(col_first_kernel, tile, log_b), in_specs...]
    ppermute x11 -> x4, waiting for transfers between devices: 5.72 us -> 4.76 us  [along(): return lax.ppermute(block, axis, [(i, (i + turn) % n) for i in range(n)])]
  transfers between devices with their start and end apart: 21 -> 14, of which waited for: 12 -> 10; matrix products, arithmetic and copies ran while one was open for 0% -> 0% of each run, Pallas kernels for 0% -> 0%
where the time goes in v5:
time: 126 us; the launch traced here: 127 us
  blocking collectives  47.3 us (38%)
  Pallas kernels  43.5 us (35%)
  starting transfers between devices  23.1 us (18%)
  waiting for transfers between devices  12 us (10%)
    all_to_all x3, blocking collectives, spread(): return lax.all_to_all(copies, axes, 0, 0)  47.3 us
    pallas_call x1, Pallas kernels, col_first(): pl.pallas_call(functools.partial(col_first_kernel, tile, log_b), in_specs...  13.9 us
    pallas_call x1, Pallas kernels, col_second(): pl.pallas_call(functools.partial(col_second_kernel, tile, log_a), in_spec...  13.3 us
    ppermute x4, starting transfers between devices, publish(): others = [lax.ppermute(piece, 'core', [(0, 1), (1, 0)]) for piece in pieces]  11.9 us
    pallas_call x1, Pallas kernels, row_first(): pl.pallas_call(functools.partial(row_first_kernel, tile), in_specs=[pl.Bl...  8.35 us
    pallas_call x1, Pallas kernels, row_second(): pl.pallas_call(functools.partial(row_second_kernel, tile, log_a, log_b),...  6.38 us
    ppermute x6, starting transfers between devices, turned(): return lax.ppermute(block, ('y', 'z', 'core'), pairs)  6 us
    ppermute x6, waiting for transfers between devices, turned(): return lax.ppermute(block, ('y', 'z', 'core'), pairs)  5.71 us
  transfers between devices with their start and end apart: 14, of which 10 were waited for; matrix products, arithmetic and copies ran while one was open for 0% of the time, Pallas kernels for 0%

profile of v5, /device:TPU:1, one launch (start us, length us, event | category | flops | bytes accessed | tf_op | source)
XLA Modules:
  0.0 126.7 jit_solution(9897292892918483286)
XLA Ops:
  0.6 8.3 %row_first.1 = (f32[16,40,128]{2,1,0:T(8,128)S(1)}, f32[32,16384]{1,0:T(8,128)S(1)}) custom-call(f32[32,512]{1,0:T(8,128)} %x_far.1, f32[32,16384]{1,0:T(8,128)} %y_far.1), custom_call_target="tpu_custom_call" | custom-call | tf_op jit(solution)/shard_map/row_first/pallas_call | solution.py:188
  9.0 24.9 %all_to_all.15.parts = f32[16,40,128]{2,1,0:T(8,128)S(1)} all-to-all(f32[16,40,128]{2,1,0:T(8,128)S(1)} %get-tuple-element.20), channel_id=1, replica_groups=mesh['y'=4,'z'=4,'core'=2,'tgt'=4] {'tgt','y'}, dimensions={0} | all-to-all | bytes 655360 | tf_op jit(solution)/shard_map/all_to_all | solution.py:518
  33.9 13.9 %col_first.1 = (f32[8,32,128]{2,1,0:T(8,128)S(1)}, f32[16,128]{1,0:T(8,128)S(1)}, f32[4,32,512]{2,1,0:T(8,128)S(1)}) custom-call(f32[16,40,128]{2,1,0:T(8,128)S(1)} %all_to_all.15.parts, f32[32,16384]{1,0:T(8,128)S(1)} %get-tuple-element.21.y_ref), custom_call_target="tpu_custom_call" | custom-call | tf_op jit(solution)/shard_map/col_first/pallas_call | solution.py:270
  47.7 12.5 %all_to_all.16.parts = f32[8,32,128]{2,1,0:T(8,128)S(1)} all-to-all(f32[8,32,128]{2,1,0:T(8,128)S(1)} %get-tuple-element.24), channel_id=1, replica_groups=mesh['y'=4,'z'=4,'core'=2,'tgt'=4] {'z','core'}, dimensions={0} | all-to-all | bytes 262144 | tf_op jit(solution)/shard_map/all_to_all | solution.py:518
  60.3 6.4 %row_second.1 = (f32[16,4,4,128]{3,2,1,0:T(4,128)S(1)}, f32[4,128]{1,0:T(4,128)S(1)}, f32[32,128]{1,0:T(8,128)S(1)}) custom-call(f32[4,32,512]{2,1,0:T(8,128)S(1)} %get-tuple-element.22.x_ref, f32[16,128]{1,0:T(8,128)S(1)} %get-tuple-element.23.f_ref, f32[32,16384]{1,0:T(8,128)S(1)} %get-tuple-element.21.y_ref, f32[8,32,128]{2,1,0:T(8,128)S(1)} %all_to_all.16.parts), custom_call_target="tpu_custom_call" | custom-call | tf_op jit(solution)/shard_map/row_second/pallas_call | solution.py:325
  66.7 9.9 %all_to_all.17.parts = f32[16,4,4,128]{3,2,1,0:T(4,128)S(1)} all-to-all(f32[16,4,4,128]{3,2,1,0:T(4,128)S(1)} %get-tuple-element.25), channel_id=1, replica_groups=mesh['y'=4,'z'=4,'core'=2,'tgt'=4] {'tgt','y'}, dimensions={0} | all-to-all | bytes 262144 | tf_op jit(solution)/shard_map/all_to_all | solution.py:518
  76.6 13.3 %col_second.1 = (f32[4,136,128]{2,1,0:T(8,128)S(1)}, f32[4,136,128]{2,1,0:T(8,128)S(1)}, f32[4,128]{1,0:T(4,128)}) custom-call(f32[4,32,512]{2,1,0:T(8,128)S(1)} %get-tuple-element.22.x_ref, f32[16,128]{1,0:T(8,128)S(1)} %get-tuple-element.23.f_ref, f32[16,4,4,128]{3,2,1,0:T(4,128)S(1)} %all_to_all.17.parts, f32[32,16384]{1,0:T(8,128)S(1)} %get-tuple-element.21.y_ref, ...), custom_call_target="tpu_custom_call" | custom-call | tf_op jit(solution)/shard_map/col_second/pallas_call | solution.py:414
  89.8 2.4 %collective-permute-start = (f32[4,136,128]{2,1,0:T(8,128)S(1)}, f32[4,136,128]{2,1,0:T(8,128)S(1)}, u32[]{:S(2)}, u32[]{:S(2)}) collective-permute-start(f32[4,136,128]{2,1,0:T(8,128)S(1)} %get-tuple-element.30), channel_id=1, source_target_pairs={{0,4},{4,0},{1,5},{5,1},{2,6},{6,2},{3,7},{7,3},{8,12},{12,8},{9,1... | collective-permute-start | bytes 835592 | tf_op jit(solution)/shard_map/ppermute | solution.py:523
  92.2 1.2 collective-permute-done.other
  93.5 0.4 collective-permute-start.1
  93.8 1.8 %collective-permute-start.2 = (f32[136,128]{1,0:T(8,128)S(1)}, f32[136,128]{1,0:T(8,128)S(1)}, u32[]{:S(2)}, u32[]{:S(2)}) collective-permute-start(f32[136,128]{1,0:T(8,128)S(1)} %get-tuple-element.33), channel_id=1, source_target_pairs={{0,16},{8,24},{16,0},{24,8},{1,17},{9,25},{17,1},{25,9},{2,18},{10... | collective-permute-start | bytes 208904 | tf_op jit(solution)/shard_map/ppermute | solution.py:523
  95.6 0.7 collective-permute-start.3
  96.3 2.3 %collective-permute-done.1.p1 = f32[136,128]{1,0:T(8,128)S(1)} collective-permute-done((f32[136,128]{1,0:T(8,128)S(1)}, f32[136,128]{1,0:T(8,128)S(1)}, u32[]{:S(2)}, u32[]{:S(2)}) %collective-permute-start.1) | collective-permute-done | bytes 69664 | tf_op jit(solution)/shard_map/ppermute | solution.py:523
  98.6 0.6 collective-permute-done.2.p2
  99.2 0.7 collective-permute-done.3.p3
  99.9 0.7 collective-permute-start.6
  100.6 2.4 %collective-permute-start.5 = (f32[136,128]{1,0:T(8,128)S(1)}, f32[136,128]{1,0:T(8,128)S(1)}, u32[]{:S(2)}, u32[]{:S(2)}) collective-permute-start(f32[136,128]{1,0:T(8,128)S(1)} %finish.1), channel_id=1, source_target_pairs={{0,96},{4,28},{8,104},{12,4},{16,112},{20,12},{24,120},{28,20},{32... | collective-permute-start | bytes 208904 | tf_op jit(solution)/shard_map/ppermute | solution.py:506
  103.0 0.1 collective-permute-start.4
  103.1 1.5 %collective-permute-done.6 = f32[136,128]{1,0:T(8,128)S(1)} collective-permute-done((f32[136,128]{1,0:T(8,128)S(1)}, f32[136,128]{1,0:T(8,128)S(1)}, u32[]{:S(2)}, u32[]{:S(2)}) %collective-permute-start.6) | collective-permute-done | bytes 69664 | tf_op jit(solution)/shard_map/ppermute | solution.py:506
  104.6 0.9 collective-permute-done.5
  105.6 1.8 %collective-permute-done.4 = f32[136,128]{1,0:T(8,128)S(1)} collective-permute-done((f32[136,128]{1,0:T(8,128)S(1)}, f32[136,128]{1,0:T(8,128)S(1)}, u32[]{:S(2)}, u32[]{:S(2)}) %collective-permute-start.4) | collective-permute-done | bytes 69664 | tf_op jit(solution)/shard_map/ppermute | solution.py:506
  107.4 1.0 collective-permute-start.12
  108.4 0.5 collective-permute-start.10
  108.9 1.2 collective-permute-start.8
  110.2 4.1 %collective-permute-start.7 = (f32[4,136,128]{2,1,0:T(8,128)S(1)}, f32[4,136,128]{2,1,0:T(8,128)S(1)}, u32[]{:S(2)}, u32[]{:S(2)}) collective-permute-start(f32[4,136,128]{2,1,0:T(8,128)S(1)} %pad_maximum_fusion.refs_0_), channel_id=1, source_target_pairs={{0,4},{4,0},{1,5},{5,1},{2,6},{6,2},{3,7},{7,3},{8,12},{12,8},{9,1... | collective-permute-start | bytes 835592 | tf_op jit(solution)/shard_map/ppermute | solution.py:513
  114.3 0.0 collective-permute-done.12.refs_6_
  114.3 2.5 %collective-permute-start.13 = (f32[4,136,128]{2,1,0:T(8,128)S(1)}, f32[4,136,128]{2,1,0:T(8,128)S(1)}, u32[]{:S(2)}, u32[]{:S(2)}) collective-permute-start(f32[4,136,128]{2,1,0:T(8,128)S(1)} %collective-permute-done.12.refs_6_), channel_id=1, source_target_pairs={{0,4},{4,0},{1,5},{5,1},{2,6},{6,2},{3,7},{7,3},{8,12},{12,8},{9,1... | collective-permute-start | bytes 835592 | tf_op jit(solution)/shard_map/ppermute | solution.py:513
  116.8 1.5 %collective-permute-done.10.refs_4_ = f32[4,136,128]{2,1,0:T(8,128)S(1)} collective-permute-done((f32[4,136,128]{2,1,0:T(8,128)S(1)}, f32[4,136,128]{2,1,0:T(8,128)S(1)}, u32[]{:S(2)}, u32[]{:S(2)}) %collective-permute-start.10) | collective-permute-done | bytes 278560 | tf_op jit(solution)/shard_map/ppermute | solution.py:506
  118.3 5.2 %collective-permute-start.11 = (f32[4,136,128]{2,1,0:T(8,128)S(1)}, f32[4,136,128]{2,1,0:T(8,128)S(1)}, u32[]{:S(2)}, u32[]{:S(2)}) collective-permute-start(f32[4,136,128]{2,1,0:T(8,128)S(1)} %collective-permute-done.10.refs_4_), channel_id=1, source_target_pairs={{0,4},{4,0},{1,5},{5,1},{2,6},{6,2},{3,7},{7,3},{8,12},{12,8},{9,1... | collective-permute-start | bytes 835592 | tf_op jit(solution)/shard_map/ppermute | solution.py:513
  123.5 0.0 collective-permute-done.8.refs_2_
  123.5 0.0 collective-permute-start.9
  123.5 0.0 collective-permute-done.7.refs_1_
  123.5 0.0 collective-permute-done.13.refs_7_
  123.5 1.2 collective-permute-done.11.refs_5_
  124.7 0.4 collective-permute-done.9.refs_3_
  125.1 1.6 %place.1 = (f32[32,16384]{1,0:T(8,128)}, f32[32,4,128]{2,1,0:T(4,128)}) custom-call(f32[4,136,128]{2,1,0:T(8,128)S(1)} %pad_maximum_fusion.refs_0_, f32[4,136,128]{2,1,0:T(8,128)S(1)} %collective-permute-done.7.refs_1_, f32[4,136,128]{2,1,0:T(8,128)S(1)} %collective-permute-done.8.refs_2_, f32[4,136,128]{2,1,0:T(8,128)S(1)} %collective-permute-done.9.refs_3_, ...), custom_call_target="tpu_custom_call" | custom-call | tf_op jit(solution)/shard_map/place/pallas_call | solution.py:489
  (3 shorter events, 0.1 us)
Async XLA Ops:
  89.8 3.6 %collective-permute-start = (f32[4,136,128]{2,1,0:T(8,128)S(1)}, f32[4,136,128]{2,1,0:T(8,128)S(1)}, u32[]{:S(2)}, u32[]{:S(2)}) collective-permute-start(f32[4,136,128]{2,1,0:T(8,128)S(1)} %get-tuple-element.30), channel_id=1, source_target_pairs={{0,4},{4,0},{1,5},{5,1},{2,6},{6,2},{3,7},{7,3},{8,12},{12,8},{9,1... | collective-permute-start | bytes 835592 | tf_op jit(solution)/shard_map/ppermute | solution.py:523
  93.5 5.2 %collective-permute-start.1 = (f32[136,128]{1,0:T(8,128)S(1)}, f32[136,128]{1,0:T(8,128)S(1)}, u32[]{:S(2)}, u32[]{:S(2)}) collective-permute-start(f32[136,128]{1,0:T(8,128)S(1)} %get-tuple-element.32), channel_id=1, source_target_pairs={{0,8},{8,16},{16,24},{24,0},{1,9},{9,17},{17,25},{25,1},{2,10},{10... | collective-permute-start | bytes 208904 | tf_op jit(solution)/shard_map/ppermute | solution.py:523
  93.8 5.4 %collective-permute-start.2 = (f32[136,128]{1,0:T(8,128)S(1)}, f32[136,128]{1,0:T(8,128)S(1)}, u32[]{:S(2)}, u32[]{:S(2)}) collective-permute-start(f32[136,128]{1,0:T(8,128)S(1)} %get-tuple-element.33), channel_id=1, source_target_pairs={{0,16},{8,24},{16,0},{24,8},{1,17},{9,25},{17,1},{25,9},{2,18},{10... | collective-permute-start | bytes 208904 | tf_op jit(solution)/shard_map/ppermute | solution.py:523
  95.6 4.3 %collective-permute-start.3 = (f32[136,128]{1,0:T(8,128)S(1)}, f32[136,128]{1,0:T(8,128)S(1)}, u32[]{:S(2)}, u32[]{:S(2)}) collective-permute-start(f32[136,128]{1,0:T(8,128)S(1)} %get-tuple-element.34), channel_id=1, source_target_pairs={{0,24},{8,0},{16,8},{24,16},{1,25},{9,1},{17,9},{25,17},{2,26},{10... | collective-permute-start | bytes 208904 | tf_op jit(solution)/shard_map/ppermute | solution.py:523
  99.9 4.7 %collective-permute-start.6 = (f32[136,128]{1,0:T(8,128)S(1)}, f32[136,128]{1,0:T(8,128)S(1)}, u32[]{:S(2)}, u32[]{:S(2)}) collective-permute-start(f32[136,128]{1,0:T(8,128)S(1)} %finish.1), channel_id=1, source_target_pairs={{0,64},{4,20},{8,72},{12,28},{16,80},{20,4},{24,88},{28,12},{32,96... | collective-permute-start | bytes 208904 | tf_op jit(solution)/shard_map/ppermute | solution.py:506
  100.6 5.0 %collective-permute-start.5 = (f32[136,128]{1,0:T(8,128)S(1)}, f32[136,128]{1,0:T(8,128)S(1)}, u32[]{:S(2)}, u32[]{:S(2)}) collective-permute-start(f32[136,128]{1,0:T(8,128)S(1)} %finish.1), channel_id=1, source_target_pairs={{0,96},{4,28},{8,104},{12,4},{16,112},{20,12},{24,120},{28,20},{32... | collective-permute-start | bytes 208904 | tf_op jit(solution)/shard_map/ppermute | solution.py:506
  103.0 4.4 %collective-permute-start.4 = (f32[136,128]{1,0:T(8,128)S(1)}, f32[136,128]{1,0:T(8,128)S(1)}, u32[]{:S(2)}, u32[]{:S(2)}) collective-permute-start(f32[136,128]{1,0:T(8,128)S(1)} %finish.1), channel_id=1, source_target_pairs={{0,32},{4,12},{8,40},{12,20},{16,48},{20,28},{24,56},{28,4},{32,64... | collective-permute-start | bytes 208904 | tf_op jit(solution)/shard_map/ppermute | solution.py:506
  107.4 6.9 %collective-permute-start.12 = (f32[4,136,128]{2,1,0:T(8,128)S(1)}, f32[4,136,128]{2,1,0:T(8,128)S(1)}, u32[]{:S(2)}, u32[]{:S(2)}) collective-permute-start(f32[4,136,128]{2,1,0:T(8,128)S(1)} %pad_maximum_fusion.refs_0_), channel_id=1, source_target_pairs={{0,24},{4,100},{8,0},{12,108},{16,8},{20,116},{24,16},{28,124},{32... | collective-permute-start | bytes 835592 | tf_op jit(solution)/shard_map/ppermute | solution.py:506
  108.4 9.9 %collective-permute-start.10 = (f32[4,136,128]{2,1,0:T(8,128)S(1)}, f32[4,136,128]{2,1,0:T(8,128)S(1)}, u32[]{:S(2)}, u32[]{:S(2)}) collective-permute-start(f32[4,136,128]{2,1,0:T(8,128)S(1)} %pad_maximum_fusion.refs_0_), channel_id=1, source_target_pairs={{0,8},{4,36},{8,16},{12,44},{16,24},{20,52},{24,0},{28,60},{32,40}... | collective-permute-start | bytes 835592 | tf_op jit(solution)/shard_map/ppermute | solution.py:506
  108.9 14.6 %collective-permute-start.8 = (f32[4,136,128]{2,1,0:T(8,128)S(1)}, f32[4,136,128]{2,1,0:T(8,128)S(1)}, u32[]{:S(2)}, u32[]{:S(2)}) collective-permute-start(f32[4,136,128]{2,1,0:T(8,128)S(1)} %pad_maximum_fusion.refs_0_), channel_id=1, source_target_pairs={{0,16},{4,68},{8,24},{12,76},{16,0},{20,84},{24,8},{28,92},{32,48}... | collective-permute-start | bytes 835592 | tf_op jit(solution)/shard_map/ppermute | solution.py:506
  110.2 13.4 %collective-permute-start.7 = (f32[4,136,128]{2,1,0:T(8,128)S(1)}, f32[4,136,128]{2,1,0:T(8,128)S(1)}, u32[]{:S(2)}, u32[]{:S(2)}) collective-permute-start(f32[4,136,128]{2,1,0:T(8,128)S(1)} %pad_maximum_fusion.refs_0_), channel_id=1, source_target_pairs={{0,4},{4,0},{1,5},{5,1},{2,6},{6,2},{3,7},{7,3},{8,12},{12,8},{9,1... | collective-permute-start | bytes 835592 | tf_op jit(solution)/shard_map/ppermute | solution.py:513
  114.3 9.2 %collective-permute-start.13 = (f32[4,136,128]{2,1,0:T(8,128)S(1)}, f32[4,136,128]{2,1,0:T(8,128)S(1)}, u32[]{:S(2)}, u32[]{:S(2)}) collective-permute-start(f32[4,136,128]{2,1,0:T(8,128)S(1)} %collective-permute-done.12.refs_6_), channel_id=1, source_target_pairs={{0,4},{4,0},{1,5},{5,1},{2,6},{6,2},{3,7},{7,3},{8,12},{12,8},{9,1... | collective-permute-start | bytes 835592 | tf_op jit(solution)/shard_map/ppermute | solution.py:513
  118.3 6.4 %collective-permute-start.11 = (f32[4,136,128]{2,1,0:T(8,128)S(1)}, f32[4,136,128]{2,1,0:T(8,128)S(1)}, u32[]{:S(2)}, u32[]{:S(2)}) collective-permute-start(f32[4,136,128]{2,1,0:T(8,128)S(1)} %collective-permute-done.10.refs_4_), channel_id=1, source_target_pairs={{0,4},{4,0},{1,5},{5,1},{2,6},{6,2},{3,7},{7,3},{8,12},{12,8},{9,1... | collective-permute-start | bytes 835592 | tf_op jit(solution)/shard_map/ppermute | solution.py:513
  123.5 1.6 %collective-permute-start.9 = (f32[4,136,128]{2,1,0:T(8,128)S(1)}, f32[4,136,128]{2,1,0:T(8,128)S(1)}, u32[]{:S(2)}, u32[]{:S(2)}) collective-permute-start(f32[4,136,128]{2,1,0:T(8,128)S(1)} %collective-permute-done.8.refs_2_), channel_id=1, source_target_pairs={{0,4},{4,0},{1,5},{5,1},{2,6},{6,2},{3,7},{7,3},{8,12},{12,8},{9,1... | collective-permute-start | bytes 835592 | tf_op jit(solution)/shard_map/ppermute | solution.py:513

commit v6 on v5

--- a/solution.py
+++ b/solution.py
@@ -532,7 +532,7 @@
     second, own_g, g1 = row_second(near_x, f1, near_y, partial, log_a, log_b, 16)
     mine, other, source_dual = col_second(near_x, f1, spread(second, ("tgt", "y")), near_y, g1, log_a)
     sums = merge(mine, along(other, "core", 1))
-    sums = [sums[0]] + [along(sums[turn], "z", turn) for turn in (1, 2, 3)]
+    sums = [sums[0]] + [along(sums[turn], "z", turn) for turn in (2, 1, 3)]
     mapped, target_dual = publish(finish(own_g, sums))
     return source_dual.reshape(-1), target_dual.reshape(-1), mapped
 

time: 126 us -> 124 us (0.984); the launches traced: 127 us -> 123 us
  blocking collectives: 47.3 us -> 43.7 us
    all_to_all x3, blocking collectives: 47.3 us -> 43.7 us  [spread(): return lax.all_to_all(copies, axes, 0, 0)]
  transfers between devices with their start and end apart: 14 -> 14, of which waited for: 10 -> 8; matrix products, arithmetic and copies ran while one was open for 0% -> 0% of each run, Pallas kernels for 0% -> 0%
where the time goes in v6:
time: 124 us; the launch traced here: 123 us
  blocking collectives  43.7 us (35%)
  Pallas kernels  43.6 us (35%)
  starting transfers between devices  22.6 us (18%)
  waiting for transfers between devices  12.1 us (10%)
    all_to_all x3, blocking collectives, spread(): return lax.all_to_all(copies, axes, 0, 0)  43.7 us
    pallas_call x1, Pallas kernels, col_first(): pl.pallas_call(functools.partial(col_first_kernel, tile, log_b), in_specs...  13.9 us
    pallas_call x1, Pallas kernels, col_second(): pl.pallas_call(functools.partial(col_second_kernel, tile, log_a), in_spec...  13.3 us
    ppermute x4, starting transfers between devices, publish(): others = [lax.ppermute(piece, 'core', [(0, 1), (1, 0)]) for piece in pieces]  11.7 us
    pallas_call x1, Pallas kernels, row_first(): pl.pallas_call(functools.partial(row_first_kernel, tile), in_specs=[pl.Bl...  8.35 us
    pallas_call x1, Pallas kernels, row_second(): pl.pallas_call(functools.partial(row_second_kernel, tile, log_a, log_b),...  6.38 us
    ppermute x6, waiting for transfers between devices, turned(): return lax.ppermute(block, ('y', 'z', 'core'), pairs)  5.7 us
    ppermute x4, starting transfers between devices, along(): return lax.ppermute(block, axis, [(i, (i + turn) % n) for i in range(n)])  5.67 us
  transfers between devices with their start and end apart: 14, of which 8 were waited for; matrix products, arithmetic and copies ran while one was open for 0% of the time, Pallas kernels for 0%

profile of v6, /device:TPU:1, one launch (start us, length us, event | category | flops | bytes accessed | tf_op | source)
XLA Modules:
  0.0 122.7 jit_solution(3021245572670567327)
XLA Ops:
  0.6 8.3 %row_first.1 = (f32[16,40,128]{2,1,0:T(8,128)S(1)}, f32[32,16384]{1,0:T(8,128)S(1)}) custom-call(f32[32,512]{1,0:T(8,128)} %x_far.1, f32[32,16384]{1,0:T(8,128)} %y_far.1), custom_call_target="tpu_custom_call" | custom-call | tf_op jit(solution)/shard_map/row_first/pallas_call | solution.py:188
  9.0 15.2 %all_to_all.15.parts = f32[16,40,128]{2,1,0:T(8,128)S(1)} all-to-all(f32[16,40,128]{2,1,0:T(8,128)S(1)} %get-tuple-element.20), channel_id=1, replica_groups=mesh['y'=4,'z'=4,'core'=2,'tgt'=4] {'tgt','y'}, dimensions={0} | all-to-all | bytes 655360 | tf_op jit(solution)/shard_map/all_to_all | solution.py:518
  24.2 13.9 %col_first.1 = (f32[8,32,128]{2,1,0:T(8,128)S(1)}, f32[16,128]{1,0:T(8,128)S(1)}, f32[4,32,512]{2,1,0:T(8,128)S(1)}) custom-call(f32[16,40,128]{2,1,0:T(8,128)S(1)} %all_to_all.15.parts, f32[32,16384]{1,0:T(8,128)S(1)} %get-tuple-element.21.y_ref), custom_call_target="tpu_custom_call" | custom-call | tf_op jit(solution)/shard_map/col_first/pallas_call | solution.py:270
  38.1 18.6 %all_to_all.16.parts = f32[8,32,128]{2,1,0:T(8,128)S(1)} all-to-all(f32[8,32,128]{2,1,0:T(8,128)S(1)} %get-tuple-element.24), channel_id=1, replica_groups=mesh['y'=4,'z'=4,'core'=2,'tgt'=4] {'z','core'}, dimensions={0} | all-to-all | bytes 262144 | tf_op jit(solution)/shard_map/all_to_all | solution.py:518
  56.7 6.4 %row_second.1 = (f32[16,4,4,128]{3,2,1,0:T(4,128)S(1)}, f32[4,128]{1,0:T(4,128)S(1)}, f32[32,128]{1,0:T(8,128)S(1)}) custom-call(f32[4,32,512]{2,1,0:T(8,128)S(1)} %get-tuple-element.22.x_ref, f32[16,128]{1,0:T(8,128)S(1)} %get-tuple-element.23.f_ref, f32[32,16384]{1,0:T(8,128)S(1)} %get-tuple-element.21.y_ref, f32[8,32,128]{2,1,0:T(8,128)S(1)} %all_to_all.16.parts), custom_call_target="tpu_custom_call" | custom-call | tf_op jit(solution)/shard_map/row_second/pallas_call | solution.py:325
  63.1 9.9 %all_to_all.17.parts = f32[16,4,4,128]{3,2,1,0:T(4,128)S(1)} all-to-all(f32[16,4,4,128]{3,2,1,0:T(4,128)S(1)} %get-tuple-element.25), channel_id=1, replica_groups=mesh['y'=4,'z'=4,'core'=2,'tgt'=4] {'tgt','y'}, dimensions={0} | all-to-all | bytes 262144 | tf_op jit(solution)/shard_map/all_to_all | solution.py:518
  73.0 13.3 %col_second.1 = (f32[4,136,128]{2,1,0:T(8,128)S(1)}, f32[4,136,128]{2,1,0:T(8,128)S(1)}, f32[4,128]{1,0:T(4,128)}) custom-call(f32[4,32,512]{2,1,0:T(8,128)S(1)} %get-tuple-element.22.x_ref, f32[16,128]{1,0:T(8,128)S(1)} %get-tuple-element.23.f_ref, f32[16,4,4,128]{3,2,1,0:T(4,128)S(1)} %all_to_all.17.parts, f32[32,16384]{1,0:T(8,128)S(1)} %get-tuple-element.21.y_ref, ...), custom_call_target="tpu_custom_call" | custom-call | tf_op jit(solution)/shard_map/col_second/pallas_call | solution.py:414
  86.3 2.4 %collective-permute-start = (f32[4,136,128]{2,1,0:T(8,128)S(1)}, f32[4,136,128]{2,1,0:T(8,128)S(1)}, u32[]{:S(2)}, u32[]{:S(2)}) collective-permute-start(f32[4,136,128]{2,1,0:T(8,128)S(1)} %get-tuple-element.30), channel_id=1, source_target_pairs={{0,4},{4,0},{1,5},{5,1},{2,6},{6,2},{3,7},{7,3},{8,12},{12,8},{9,1... | collective-permute-start | bytes 835592 | tf_op jit(solution)/shard_map/ppermute | solution.py:523
  88.6 1.2 collective-permute-done.other
  89.9 0.6 collective-permute-start.1
  90.5 0.9 collective-permute-start.2
  91.4 1.7 %collective-permute-start.3 = (f32[136,128]{1,0:T(8,128)S(1)}, f32[136,128]{1,0:T(8,128)S(1)}, u32[]{:S(2)}, u32[]{:S(2)}) collective-permute-start(f32[136,128]{1,0:T(8,128)S(1)} %get-tuple-element.34), channel_id=1, source_target_pairs={{0,24},{8,0},{16,8},{24,16},{1,25},{9,1},{17,9},{25,17},{2,26},{10... | collective-permute-start | bytes 208904 | tf_op jit(solution)/shard_map/ppermute | solution.py:523
  93.2 1.5 %collective-permute-done.1.p1 = f32[136,128]{1,0:T(8,128)S(1)} collective-permute-done((f32[136,128]{1,0:T(8,128)S(1)}, f32[136,128]{1,0:T(8,128)S(1)}, u32[]{:S(2)}, u32[]{:S(2)}) %collective-permute-start.1) | collective-permute-done | bytes 69664 | tf_op jit(solution)/shard_map/ppermute | solution.py:523
  94.7 2.2 %collective-permute-done.2.p2 = f32[136,128]{1,0:T(8,128)S(1)} collective-permute-done((f32[136,128]{1,0:T(8,128)S(1)}, f32[136,128]{1,0:T(8,128)S(1)}, u32[]{:S(2)}, u32[]{:S(2)}) %collective-permute-start.2) | collective-permute-done | bytes 69664 | tf_op jit(solution)/shard_map/ppermute | solution.py:523
  96.8 0.0 collective-permute-done.3.p3
  96.8 0.6 collective-permute-start.6
  97.5 1.8 %collective-permute-start.5 = (f32[136,128]{1,0:T(8,128)S(1)}, f32[136,128]{1,0:T(8,128)S(1)}, u32[]{:S(2)}, u32[]{:S(2)}) collective-permute-start(f32[136,128]{1,0:T(8,128)S(1)} %finish.1), channel_id=1, source_target_pairs={{0,96},{4,28},{8,104},{12,4},{16,112},{20,12},{24,120},{28,20},{32... | collective-permute-start | bytes 208904 | tf_op jit(solution)/shard_map/ppermute | solution.py:506
  99.3 0.0 collective-permute-start.4
  99.3 2.3 %collective-permute-done.6 = f32[136,128]{1,0:T(8,128)S(1)} collective-permute-done((f32[136,128]{1,0:T(8,128)S(1)}, f32[136,128]{1,0:T(8,128)S(1)}, u32[]{:S(2)}, u32[]{:S(2)}) %collective-permute-start.6) | collective-permute-done | bytes 69664 | tf_op jit(solution)/shard_map/ppermute | solution.py:506
  101.6 0.0 collective-permute-done.5
  101.6 2.0 %collective-permute-done.4 = f32[136,128]{1,0:T(8,128)S(1)} collective-permute-done((f32[136,128]{1,0:T(8,128)S(1)}, f32[136,128]{1,0:T(8,128)S(1)}, u32[]{:S(2)}, u32[]{:S(2)}) %collective-permute-start.4) | collective-permute-done | bytes 69664 | tf_op jit(solution)/shard_map/ppermute | solution.py:506
  103.7 0.7 collective-permute-start.12
  104.4 0.8 collective-permute-start.10
  105.2 1.2 %collective-permute-start.8 = (f32[4,136,128]{2,1,0:T(8,128)S(1)}, f32[4,136,128]{2,1,0:T(8,128)S(1)}, u32[]{:S(2)}, u32[]{:S(2)}) collective-permute-start(f32[4,136,128]{2,1,0:T(8,128)S(1)} %pad_maximum_fusion.refs_0_), channel_id=1, source_target_pairs={{0,16},{4,68},{8,24},{12,76},{16,0},{20,84},{24,8},{28,92},{32,48}... | collective-permute-start | bytes 835592 | tf_op jit(solution)/shard_map/ppermute | solution.py:506
  106.4 3.9 %collective-permute-start.7 = (f32[4,136,128]{2,1,0:T(8,128)S(1)}, f32[4,136,128]{2,1,0:T(8,128)S(1)}, u32[]{:S(2)}, u32[]{:S(2)}) collective-permute-start(f32[4,136,128]{2,1,0:T(8,128)S(1)} %pad_maximum_fusion.refs_0_), channel_id=1, source_target_pairs={{0,4},{4,0},{1,5},{5,1},{2,6},{6,2},{3,7},{7,3},{8,12},{12,8},{9,1... | collective-permute-start | bytes 835592 | tf_op jit(solution)/shard_map/ppermute | solution.py:513
  110.3 0.0 collective-permute-done.12.refs_6_
  110.3 2.7 %collective-permute-start.13 = (f32[4,136,128]{2,1,0:T(8,128)S(1)}, f32[4,136,128]{2,1,0:T(8,128)S(1)}, u32[]{:S(2)}, u32[]{:S(2)}) collective-permute-start(f32[4,136,128]{2,1,0:T(8,128)S(1)} %collective-permute-done.12.refs_6_), channel_id=1, source_target_pairs={{0,4},{4,0},{1,5},{5,1},{2,6},{6,2},{3,7},{7,3},{8,12},{12,8},{9,1... | collective-permute-start | bytes 835592 | tf_op jit(solution)/shard_map/ppermute | solution.py:513
  113.0 1.3 %collective-permute-done.10.refs_4_ = f32[4,136,128]{2,1,0:T(8,128)S(1)} collective-permute-done((f32[4,136,128]{2,1,0:T(8,128)S(1)}, f32[4,136,128]{2,1,0:T(8,128)S(1)}, u32[]{:S(2)}, u32[]{:S(2)}) %collective-permute-start.10) | collective-permute-done | bytes 278560 | tf_op jit(solution)/shard_map/ppermute | solution.py:506
  114.3 5.2 %collective-permute-start.11 = (f32[4,136,128]{2,1,0:T(8,128)S(1)}, f32[4,136,128]{2,1,0:T(8,128)S(1)}, u32[]{:S(2)}, u32[]{:S(2)}) collective-permute-start(f32[4,136,128]{2,1,0:T(8,128)S(1)} %collective-permute-done.10.refs_4_), channel_id=1, source_target_pairs={{0,4},{4,0},{1,5},{5,1},{2,6},{6,2},{3,7},{7,3},{8,12},{12,8},{9,1... | collective-permute-start | bytes 835592 | tf_op jit(solution)/shard_map/ppermute | solution.py:513
  119.5 0.0 collective-permute-done.8.refs_2_
  119.5 0.0 collective-permute-start.9
  119.5 0.0 collective-permute-done.7.refs_1_
  119.5 0.0 collective-permute-done.13.refs_7_
  119.5 1.2 collective-permute-done.11.refs_5_
  120.7 0.4 collective-permute-done.9.refs_3_
  121.1 1.6 %place.1 = (f32[32,16384]{1,0:T(8,128)}, f32[32,4,128]{2,1,0:T(4,128)}) custom-call(f32[4,136,128]{2,1,0:T(8,128)S(1)} %pad_maximum_fusion.refs_0_, f32[4,136,128]{2,1,0:T(8,128)S(1)} %collective-permute-done.7.refs_1_, f32[4,136,128]{2,1,0:T(8,128)S(1)} %collective-permute-done.8.refs_2_, f32[4,136,128]{2,1,0:T(8,128)S(1)} %collective-permute-done.9.refs_3_, ...), custom_call_target="tpu_custom_call" | custom-call | tf_op jit(solution)/shard_map/place/pallas_call | solution.py:489
  (3 shorter events, 0.1 us)
Async XLA Ops:
  86.3 3.6 %collective-permute-start = (f32[4,136,128]{2,1,0:T(8,128)S(1)}, f32[4,136,128]{2,1,0:T(8,128)S(1)}, u32[]{:S(2)}, u32[]{:S(2)}) collective-permute-start(f32[4,136,128]{2,1,0:T(8,128)S(1)} %get-tuple-element.30), channel_id=1, source_target_pairs={{0,4},{4,0},{1,5},{5,1},{2,6},{6,2},{3,7},{7,3},{8,12},{12,8},{9,1... | collective-permute-start | bytes 835592 | tf_op jit(solution)/shard_map/ppermute | solution.py:523
  89.9 4.8 %collective-permute-start.1 = (f32[136,128]{1,0:T(8,128)S(1)}, f32[136,128]{1,0:T(8,128)S(1)}, u32[]{:S(2)}, u32[]{:S(2)}) collective-permute-start(f32[136,128]{1,0:T(8,128)S(1)} %get-tuple-element.32), channel_id=1, source_target_pairs={{0,16},{8,24},{16,0},{24,8},{1,17},{9,25},{17,1},{25,9},{2,18},{10... | collective-permute-start | bytes 208904 | tf_op jit(solution)/shard_map/ppermute | solution.py:523
  90.5 6.3 %collective-permute-start.2 = (f32[136,128]{1,0:T(8,128)S(1)}, f32[136,128]{1,0:T(8,128)S(1)}, u32[]{:S(2)}, u32[]{:S(2)}) collective-permute-start(f32[136,128]{1,0:T(8,128)S(1)} %get-tuple-element.33), channel_id=1, source_target_pairs={{0,8},{8,16},{16,24},{24,0},{1,9},{9,17},{17,25},{25,1},{2,10},{10... | collective-permute-start | bytes 208904 | tf_op jit(solution)/shard_map/ppermute | solution.py:523
  91.4 5.4 %collective-permute-start.3 = (f32[136,128]{1,0:T(8,128)S(1)}, f32[136,128]{1,0:T(8,128)S(1)}, u32[]{:S(2)}, u32[]{:S(2)}) collective-permute-start(f32[136,128]{1,0:T(8,128)S(1)} %get-tuple-element.34), channel_id=1, source_target_pairs={{0,24},{8,0},{16,8},{24,16},{1,25},{9,1},{17,9},{25,17},{2,26},{10... | collective-permute-start | bytes 208904 | tf_op jit(solution)/shard_map/ppermute | solution.py:523
  96.8 4.7 %collective-permute-start.6 = (f32[136,128]{1,0:T(8,128)S(1)}, f32[136,128]{1,0:T(8,128)S(1)}, u32[]{:S(2)}, u32[]{:S(2)}) collective-permute-start(f32[136,128]{1,0:T(8,128)S(1)} %finish.1), channel_id=1, source_target_pairs={{0,64},{4,20},{8,72},{12,28},{16,80},{20,4},{24,88},{28,12},{32,96... | collective-permute-start | bytes 208904 | tf_op jit(solution)/shard_map/ppermute | solution.py:506
  97.5 4.1 %collective-permute-start.5 = (f32[136,128]{1,0:T(8,128)S(1)}, f32[136,128]{1,0:T(8,128)S(1)}, u32[]{:S(2)}, u32[]{:S(2)}) collective-permute-start(f32[136,128]{1,0:T(8,128)S(1)} %finish.1), channel_id=1, source_target_pairs={{0,96},{4,28},{8,104},{12,4},{16,112},{20,12},{24,120},{28,20},{32... | collective-permute-start | bytes 208904 | tf_op jit(solution)/shard_map/ppermute | solution.py:506
  99.3 4.4 %collective-permute-start.4 = (f32[136,128]{1,0:T(8,128)S(1)}, f32[136,128]{1,0:T(8,128)S(1)}, u32[]{:S(2)}, u32[]{:S(2)}) collective-permute-start(f32[136,128]{1,0:T(8,128)S(1)} %finish.1), channel_id=1, source_target_pairs={{0,32},{4,12},{8,40},{12,20},{16,48},{20,28},{24,56},{28,4},{32,64... | collective-permute-start | bytes 208904 | tf_op jit(solution)/shard_map/ppermute | solution.py:506
  103.7 6.6 %collective-permute-start.12 = (f32[4,136,128]{2,1,0:T(8,128)S(1)}, f32[4,136,128]{2,1,0:T(8,128)S(1)}, u32[]{:S(2)}, u32[]{:S(2)}) collective-permute-start(f32[4,136,128]{2,1,0:T(8,128)S(1)} %pad_maximum_fusion.refs_0_), channel_id=1, source_target_pairs={{0,24},{4,100},{8,0},{12,108},{16,8},{20,116},{24,16},{28,124},{32... | collective-permute-start | bytes 835592 | tf_op jit(solution)/shard_map/ppermute | solution.py:506
  104.4 9.9 %collective-permute-start.10 = (f32[4,136,128]{2,1,0:T(8,128)S(1)}, f32[4,136,128]{2,1,0:T(8,128)S(1)}, u32[]{:S(2)}, u32[]{:S(2)}) collective-permute-start(f32[4,136,128]{2,1,0:T(8,128)S(1)} %pad_maximum_fusion.refs_0_), channel_id=1, source_target_pairs={{0,8},{4,36},{8,16},{12,44},{16,24},{20,52},{24,0},{28,60},{32,40}... | collective-permute-start | bytes 835592 | tf_op jit(solution)/shard_map/ppermute | solution.py:506
  105.2 14.3 %collective-permute-start.8 = (f32[4,136,128]{2,1,0:T(8,128)S(1)}, f32[4,136,128]{2,1,0:T(8,128)S(1)}, u32[]{:S(2)}, u32[]{:S(2)}) collective-permute-start(f32[4,136,128]{2,1,0:T(8,128)S(1)} %pad_maximum_fusion.refs_0_), channel_id=1, source_target_pairs={{0,16},{4,68},{8,24},{12,76},{16,0},{20,84},{24,8},{28,92},{32,48}... | collective-permute-start | bytes 835592 | tf_op jit(solution)/shard_map/ppermute | solution.py:506
  106.4 13.1 %collective-permute-start.7 = (f32[4,136,128]{2,1,0:T(8,128)S(1)}, f32[4,136,128]{2,1,0:T(8,128)S(1)}, u32[]{:S(2)}, u32[]{:S(2)}) collective-permute-start(f32[4,136,128]{2,1,0:T(8,128)S(1)} %pad_maximum_fusion.refs_0_), channel_id=1, source_target_pairs={{0,4},{4,0},{1,5},{5,1},{2,6},{6,2},{3,7},{7,3},{8,12},{12,8},{9,1... | collective-permute-start | bytes 835592 | tf_op jit(solution)/shard_map/ppermute | solution.py:513
  110.3 9.2 %collective-permute-start.13 = (f32[4,136,128]{2,1,0:T(8,128)S(1)}, f32[4,136,128]{2,1,0:T(8,128)S(1)}, u32[]{:S(2)}, u32[]{:S(2)}) collective-permute-start(f32[4,136,128]{2,1,0:T(8,128)S(1)} %collective-permute-done.12.refs_6_), channel_id=1, source_target_pairs={{0,4},{4,0},{1,5},{5,1},{2,6},{6,2},{3,7},{7,3},{8,12},{12,8},{9,1... | collective-permute-start | bytes 835592 | tf_op jit(solution)/shard_map/ppermute | solution.py:513
  114.3 6.4 %collective-permute-start.11 = (f32[4,136,128]{2,1,0:T(8,128)S(1)}, f32[4,136,128]{2,1,0:T(8,128)S(1)}, u32[]{:S(2)}, u32[]{:S(2)}) collective-permute-start(f32[4,136,128]{2,1,0:T(8,128)S(1)} %collective-permute-done.10.refs_4_), channel_id=1, source_target_pairs={{0,4},{4,0},{1,5},{5,1},{2,6},{6,2},{3,7},{7,3},{8,12},{12,8},{9,1... | collective-permute-start | bytes 835592 | tf_op jit(solution)/shard_map/ppermute | solution.py:513
  119.5 1.6 %collective-permute-start.9 = (f32[4,136,128]{2,1,0:T(8,128)S(1)}, f32[4,136,128]{2,1,0:T(8,128)S(1)}, u32[]{:S(2)}, u32[]{:S(2)}) collective-permute-start(f32[4,136,128]{2,1,0:T(8,128)S(1)} %collective-permute-done.8.refs_2_), channel_id=1, source_target_pairs={{0,4},{4,0},{1,5},{5,1},{2,6},{6,2},{3,7},{7,3},{8,12},{12,8},{9,1... | collective-permute-start | bytes 835592 | tf_op jit(solution)/shard_map/ppermute | solution.py:513
